TPU v7x, 128 devices: a whole 4x4x4 slice. The times are simulated.
128 devices in a mesh: seq: 16 (over y, x), mp: 8 (over z, core).
Axes of the slice: x: 4, y: 4, z: 4, core: 2. Of those that a mesh axis runs over, the one named last changes fastest.
Arguments:
- residual_activations: bfloat16 [16384, 4096], P('seq', 'mp'), may hold values from -6 to 6
- prelayer_gain_vector: bfloat16 [4096], replicated, may hold values from 0.099609375 to 1.8984375
- gating_projection: bfloat16 [4096], replicated, may hold values from -0.25 to 0.25
- asker_projection: bfloat16 [4096, 8192], P(None, 'mp'), may hold values from -0.09375 to 0.09375
- lookup_projection: bfloat16 [4096, 1024], P(None, 'mp'), may hold values from -0.09375 to 0.09375
- content_projection: bfloat16 [4096, 1024], P(None, 'mp'), may hold values from -0.09375 to 0.09375
- final_projection: bfloat16 [8192, 4096], P(None, 'mp'), may hold values from -0.0625 to 0.0625
- logit_sharpness: float32 [64], P('mp'), may hold values from 1 to 64
- selection_table: int32 [16, 256], P('seq'), may hold values from 0 to 1023, as said below
- dispatched_tally_table: int32 [16, 16], replicated, may hold values from 0 to 16, as said below
Outputs:
- blended: bfloat16 [16384, 4096], P('seq', 'mp')
Inputs may be any that keep to these rules, and one draw needn't show every extreme that they name: `dispatched_tally_table`: entry [s, d] counts the routed tokens of source shard s whose compacted place falls to owner d: the compacted sequence lists all routed tokens in sequence order and is dealt in blocks of 8 places, block b to owner b mod 16. Every entry is a multiple of 8, and every column sums to 128. `selection_table`: row s lists in increasing order the distinct local indices of the routed tokens of source shard s, as many as row s of dispatched_tally_table sums to, and zeros after them.
All inputs are finite; a program needn't handle non-finite values.
Results may differ from a plain program's by a relative error of at most 0.0059.
Values may be sent and summed in bfloat16 or wider, within the bound.
No kernel may reach another device: no remote copies, remote signals or barrier semaphores. Data moves between devices by JAX's collectives and lax.ppermute only.
A program may use at most 64 MiB of HBM per device.

v0:
```python
import math

import jax
import jax.numpy as jnp
from jax import lax
from jax.sharding import PartitionSpec as P

HEADS = 64
SHARED_KV_COUNT = 8
PER_HEAD_DIM = 128
SEL = 128


def compact(incoming, prefix, spans, shard, nseq, owned):
    span_ids = jnp.arange(nseq, dtype=jnp.int32) * nseq + shard
    source_of = jnp.sum(
        (prefix[None, :] + spans[None, :] <= span_ids[:, None]).astype(jnp.int32), axis=1
    )
    matches = source_of[:, None] == jnp.arange(nseq, dtype=jnp.int32)[None, :]
    start_of = jnp.sum(jnp.where(matches, prefix[None, :], 0), axis=1)
    half_of = (span_ids - start_of) // nseq
    blocks = incoming.reshape(2 * nseq, incoming.shape[2], incoming.shape[3])
    return blocks[half_of * nseq + source_of].reshape(owned, incoming.shape[3])


def build_return(delta, prefix, spans, shard, nseq, block_rows):
    first = (shard - prefix) % nseq
    counter = jnp.arange(2, dtype=jnp.int32)[:, None] * nseq + first[None, :]
    usable = counter < spans[None, :]
    target = jnp.minimum((prefix[None, :] + counter) // nseq, nseq - 1)
    blocks = delta.reshape(nseq, block_rows, delta.shape[1])[target]
    return jnp.where(usable[:, :, None, None], blocks, jnp.zeros_like(blocks))


def on_device(
    residual_activations,
    prelayer_gain_vector,
    gating_projection,
    asker_projection,
    lookup_projection,
    content_projection,
    final_projection,
    logit_sharpness,
    selection_table,
    dispatched_tally_table,
):
    nseq = lax.axis_size("seq")
    shard = lax.axis_index("seq")
    owned = SEL
    block_rows = owned // nseq
    slots = selection_table.shape[1]
    sent = jnp.sum(dispatched_tally_table, axis=1)
    spans = sent // block_rows
    prefix = jnp.cumsum(spans) - spans
    mine = jnp.arange(nseq, dtype=jnp.int32) == shard
    my_prefix = jnp.sum(jnp.where(mine, prefix, 0))
    my_sent = jnp.sum(jnp.where(mine, sent, 0))
    rotation = my_prefix % nseq
    index_list = selection_table[0]
    live = jnp.arange(slots) < my_sent
    gathered_rows = residual_activations[index_list]
    gathered_rows = jnp.where(live[:, None], gathered_rows, jnp.zeros_like(gathered_rows))
    whole_rows = lax.all_gather(gathered_rows, "mp", axis=1, tiled=True)
    outgoing = jnp.roll(
        whole_rows.reshape(2, nseq, block_rows, whole_rows.shape[1]), rotation, axis=1
    )
    incoming = lax.all_to_all(outgoing, "seq", split_axis=1, concat_axis=1, tiled=True)
    full = compact(incoming, prefix, spans, shard, nseq, owned)
    gate = jax.nn.sigmoid(jnp.dot(full, gating_projection, preferred_element_type=jnp.float32))
    widened = full.astype(jnp.float32)
    inverse = lax.rsqrt(jnp.mean(widened * widened, axis=1, keepdims=True) + 1e-05)
    normed = (widened * inverse * prelayer_gain_vector.astype(jnp.float32)).astype(jnp.bfloat16)
    query = jnp.dot(normed, asker_projection, preferred_element_type=jnp.float32).astype(
        jnp.bfloat16
    )
    keys = jnp.dot(normed, lookup_projection, preferred_element_type=jnp.float32).astype(
        jnp.bfloat16
    )
    values = jnp.dot(normed, content_projection, preferred_element_type=jnp.float32).astype(
        jnp.bfloat16
    )
    paired = jnp.stack([keys, values])
    memory_pair_portion = lookup_projection.shape[1] // PER_HEAD_DIM
    asker_cluster = HEADS // SHARED_KV_COUNT
    query_heads = query.reshape(owned, memory_pair_portion, asker_cluster, PER_HEAD_DIM)
    gating_multipliers = logit_sharpness.reshape(memory_pair_portion, asker_cluster) / math.sqrt(
        PER_HEAD_DIM
    )
    own_slots = jnp.arange(owned, dtype=jnp.int32)
    query_places = (
        own_slots // block_rows * nseq * block_rows + shard * block_rows + own_slots % block_rows
    )
    start_best = jnp.full((memory_pair_portion, asker_cluster, owned), -1e30, jnp.float32)
    piece = lax.all_gather(paired, "seq", axis=1, tiled=True)
    best = start_best
    count = piece.shape[1]
    key_piece = piece[0].reshape(count, memory_pair_portion, PER_HEAD_DIM)
    value_piece = piece[1].reshape(count, memory_pair_portion, PER_HEAD_DIM)
    index_all = jnp.arange(count, dtype=jnp.int32)
    owner = index_all // owned
    position = index_all % owned
    key_places = (
        position // block_rows * nseq * block_rows + owner * block_rows + position % block_rows
    )
    allowed = key_places[None, :] <= query_places[:, None]
    score = jnp.einsum("qngd,knd->ngqk", query_heads, key_piece, preferred_element_type=jnp.float32)
    score = jnp.where(allowed[None, None], score * gating_multipliers[:, :, None, None], -1e30)
    new_best = jnp.maximum(best, jnp.max(score, axis=3))
    weights = jnp.where(allowed[None, None], jnp.exp(score - new_best[..., None]), 0.0)
    totals = jnp.sum(weights, axis=3)
    mixed = jnp.einsum(
        "ngqk,knd->ngqd",
        weights.astype(jnp.bfloat16),
        value_piece,
        preferred_element_type=jnp.float32,
    )
    sums = mixed
    best, totals, sums = (new_best, totals, sums)
    attended = (sums / totals[..., None]).astype(jnp.bfloat16)
    attended = attended.transpose(2, 0, 1, 3).reshape(
        owned, memory_pair_portion * asker_cluster * PER_HEAD_DIM
    )
    projected = jnp.dot(
        lax.all_gather(attended, "mp", axis=1, tiled=True),
        final_projection,
        preferred_element_type=jnp.float32,
    )
    delta = (gate[:, None] * projected).astype(jnp.bfloat16)
    outgoing_back = build_return(delta, prefix, spans, shard, nseq, block_rows)
    coming_back = lax.all_to_all(outgoing_back, "seq", split_axis=1, concat_axis=1, tiled=True)
    restored = jnp.roll(coming_back, -rotation, axis=1).reshape(slots, delta.shape[1])
    restored = jnp.where(live[:, None], restored, jnp.zeros_like(restored))
    updated = (
        residual_activations.astype(jnp.float32).at[index_list].add(restored.astype(jnp.float32))
    )
    return updated.astype(jnp.bfloat16)


def solution(mesh):
    placed = (
        P("seq", "mp"),
        P(),
        P(),
        P(None, "mp"),
        P(None, "mp"),
        P(None, "mp"),
        P(None, "mp"),
        P("mp"),
        P("seq", None),
        P(),
    )
    return jax.shard_map(
        on_device, mesh=mesh, in_specs=placed, out_specs=P("seq", "mp"), check_vma=False
    )
```

profile of v0, /device:TPU:1, one launch (start us, length us, event | category | flops | bytes accessed | tf_op | source)
XLA Modules:
  0.0 201.7 jit_solution(617594323271170253)
XLA Ops:
  6.5 0.9 reduce_sum.69
  7.5 0.1 copy.35
  7.6 0.1 reduce.3
  7.7 0.6 and_select_fusion.4
  8.3 0.6 iota_compare_fusion.1
  9.0 0.7 compare_select_fusion
  9.7 2.6 %gather_fusion = bf16[256,512]{1,0:T(8,128)(2,1)S(1)} fusion(bf16[1024,512]{1,0:T(8,128)(2,1)} %param.10, s32[1024]{0:T(1024)S(1)} %pad_clamp_fusion.2), kind=kCustom, calls=%fused_computation | custom fusion | bytes 525312 | tf_op jit(solution)/shard_map/gather | solution.py:61
  12.3 0.8 broadcast_select_fusion
  13.1 0.0 all-gather.4.cloned.1.call-update
  13.1 0.6 fusion.52
  15.6 26.6 %all-gather.4.cloned.1.call-done = bf16[256,4096]{1,0:T(8,128)(2,1)} async-done(((bf16[256,512]{1,0:T(8,128)(2,1)}), bf16[256,4096]{1,0:T(8,128)(2,1)}) %all-gather.4.cloned.1.call-update) | async-done | bytes 2097168 | tf_op jit(solution)/shard_map/all_gather | solution.py:63
  42.3 2.4 %fusion.7 = bf16[2,16,8,4096]{3,2,1,0:T(8,128)(2,1)S(1)} fusion(s32[]{:T(128)S(6)} %select_n.208, bf16[2,16,8,4096]{3,2,1,0:T(8,128)(2,1)} %bitcast.124), kind=kLoop, calls=%fused_computation.15 | loop fusion | flops 1048576 | bytes 4194308 | tf_op jit(solution)/shard_map/jit(_roll_dynamic)/concatenate | solution.py:64
  44.6 1.5 copy.48
  46.1 6.6 %all-to-all-start = ((bf16[2,16,8,4096]{3,2,0,1:T(8,128)(2,1)}), bf16[2,16,8,4096]{3,2,0,1:T(8,128)(2,1)S(1)}, u32[]{:S(2)}, u32[]{:S(2)}) async-start(bf16[2,16,8,4096]{3,2,0,1:T(8,128)(2,1)} %copy.48), calls=%async_computation | async-start | bytes 4194304 | tf_op jit(solution)/shard_map/all_to_all | solution.py:67
  52.7 0.0 all-gather.6.cloned.1.call-start
  52.8 0.2 convert_reduce_fusion
  53.0 0.2 select_reduce_fusion
  53.2 32.2 %all-to-all-done = bf16[2,16,8,4096]{3,2,0,1:T(8,128)(2,1)S(1)} async-done(((bf16[2,16,8,4096]{3,2,0,1:T(8,128)(2,1)}), bf16[2,16,8,4096]{3,2,0,1:T(8,128)(2,1)S(1)}, u32[]{:S(2)}, u32[]{:S(2)}) %all-to-all-start) | async-done | bytes 2097184 | tf_op jit(solution)/shard_map/all_to_all | solution.py:67
  85.4 1.5 copy.38
  86.8 2.2 %gather_fusion.1 = bf16[16,8,4096]{2,1,0:T(8,128)(2,1)S(1)} fusion(bf16[32,8,4096]{2,1,0:T(8,128)(2,1)} %bitcast.123, s32[1024]{0:T(1024)S(1)} %pad_clamp_fusion.1), kind=kCustom, calls=%fused_computation.1 | custom fusion | bytes 2097216 | tf_op jit(solution)/shard_map/gather | solution.py:23
  89.0 0.3 multiply_reduce_fusion
  89.4 0.1 rsqrt.12
  89.5 0.5 fusion.11
  90.0 1.7 fusion.12
  91.7 0.6 pad_maximum_fusion
  92.4 0.0 all-gather.8.cloned.1.call-start
  92.5 0.3 broadcast_compare_fusion
  92.8 4.7 %fusion.8 = bf16[16,8,8,128]{3,2,1,0:T(8,128)(2,1)S(1)} fusion(bf16[4096,1024]{1,0:T(8,128)(2,1)} %param.13, bf16[16,8,4096]{2,1,0:T(8,128)(2,1)S(1)} %gather_fusion.1, f32[4096]{0:T(1024)S(1)} %convert_element_type.49, f32[128]{0:T(128)S(1)} %rsqrt.12), kind=kOutput, calls=%fused_computation.20 | convolution fusion | flops 1075970048 | bytes 9716224 | tf_op jit(solution)/shard_map/dot_general | solution.py:73
  97.5 34.0 %all-gather.6.cloned.1.call-done = bf16[2,2048,128]{2,1,0:T(8,128)(2,1)} async-done(((bf16[2,128,128]{2,1,0:T(8,128)(2,1)}), bf16[2,2048,128]{2,1,0:T(8,128)(2,1)}) %all-gather.6.cloned.1.call-update) | async-done | bytes 1048592 | tf_op jit(solution)/shard_map/all_gather | solution.py:94
  131.5 2.3 %fusion = (f32[8,128]{1,0:T(8,128)S(1)}, f32[2048,128,8]{1,0,2:T(8,128)S(1)}) fusion(f32[8]{0:T(128)S(1)} %broadcast_multiply_fusion, pred[128,2048]{0,1:T(8,128)(4,1)S(1)} %broadcast_compare_fusion, bf16[16,8,8,128]{3,2,1,0:T(8,128)(2,1)S(1)} %fusion.8, bf16[2,2048,128]{2,1,0:T(8,128)(2,1)} %all-gather.6.cloned.1.call-done), kind=kOutput, calls=%fused_computation.7 | convolution fusion | flops 543161344 | bytes 9441312 | tf_op jit(solution)/shard_map/qngd,knd->ngqk/dot_general | solution.py:106
  133.8 2.1 %fusion.1 = f32[8,128]{1,0:T(8,128)S(1)} fusion(f32[2048,128,8]{1,0,2:T(8,128)S(1)} %get-tuple-element.10, f32[8,128]{1,0:T(8,128)S(1)} %broadcast_maximum_fusion, f32[8]{0:T(128)S(1)} %broadcast_multiply_fusion, pred[128,2048]{0,1:T(8,128)(4,1)S(1)} %broadcast_compare_fusion), kind=kLoop, calls=%fused_computation.8 | loop fusion | flops 10484736 | bytes 8658976 | tf_op jit(solution)/shard_map/reduce_sum | solution.py:110
  136.0 2.8 %fusion.21 = bf16[8,128,128]{1,2,0:T(8,128)(2,1)} fusion(f32[2048,128,8]{1,0,2:T(8,128)S(1)} %get-tuple-element.10, f32[8,128]{1,0:T(8,128)S(1)} %broadcast_maximum_fusion, f32[8]{0:T(128)S(1)} %broadcast_multiply_fusion, pred[128,2048]{0,1:T(8,128)(4,1)S(1)} %broadcast_compare_fusion, bf16[2,2048,128]{2,1,0:T(8,128)(2,1)S(1)} %copy-done.2, ...), kind=kOutput, calls=%fused_computation.34 | convolution fusion | flops 547618816 | bytes 9445888 | tf_op jit(solution)/shard_map/ngqk,knd->ngqd/dot_general | solution.py:111
  138.9 0.1 compare_select_fusion.1
  138.9 0.1 reshape.597
  139.0 0.1 add_compare_fusion
  139.1 0.4 fusion.16
  139.5 26.0 %all-gather.8.cloned.1.call-done = bf16[128,8192]{0,1:T(8,128)(2,1)} async-done(((bf16[128,1024]{0,1:T(8,128)(2,1)}), bf16[128,8192]{0,1:T(8,128)(2,1)}) %all-gather.8.cloned.1.call-update) | async-done | bytes 2097168 | tf_op jit(solution)/shard_map/all_gather | solution.py:124
  165.5 5.3 %fusion.10 = bf16[16,8,512]{2,1,0:T(8,128)(2,1)S(1)} fusion(bf16[128,8192]{0,1:T(8,128)(2,1)} %all-gather.8.cloned.1.call-done, bf16[8192,512]{1,0:T(8,128)(2,1)} %param.16, f32[128]{0:T(128)S(1)} %fusion.16), kind=kOutput, calls=%fused_computation.22 | convolution fusion | flops 1073872896 | bytes 10617344 | tf_op jit(solution)/shard_map/dot_general | solution.py:123
  170.8 0.6 gather_fusion.2
  171.4 0.1 broadcast_select_fusion.1
  171.5 0.7 copy.42
  172.2 6.5 %all-to-all-start.1 = ((bf16[2,16,8,512]{3,2,0,1:T(8,128)(2,1)}), bf16[2,16,8,512]{3,2,0,1:T(8,128)(2,1)S(1)}, u32[]{:S(2)}, u32[]{:S(2)}) async-start(bf16[2,16,8,512]{3,2,0,1:T(8,128)(2,1)} %copy.42), calls=%async_computation.1 | async-start | bytes 524288 | tf_op jit(solution)/shard_map/all_to_all | solution.py:130
  178.8 1.6 convert_element_type.45
  180.4 6.6 %all-to-all-done.1 = bf16[2,16,8,512]{3,2,0,1:T(8,128)(2,1)S(1)} async-done(((bf16[2,16,8,512]{3,2,0,1:T(8,128)(2,1)}), bf16[2,16,8,512]{3,2,0,1:T(8,128)(2,1)S(1)}, u32[]{:S(2)}, u32[]{:S(2)}) %all-to-all-start.1) | async-done | bytes 262176 | tf_op jit(solution)/shard_map/all_to_all | solution.py:130
  187.0 0.1 fusion.27
  187.2 0.1 bitcast_select_fusion.1
  187.3 5.2 %scatter_custom_fusion = f32[1024,512]{1,0:T(8,128)} fusion(f32[1024,512]{1,0:T(8,128)} %convert_element_type.45, s32[256]{0:T(256)S(1)} %bitcast.128, bf16[256,512]{1,0:T(8,128)(2,1)S(1)} %bitcast_select_fusion.1), kind=kCustom, calls=%fused_computation.40 | custom fusion | flops 262144 | bytes 2359296 | tf_op jit(solution)/shard_map/scatter-add | solution.py:134
  192.5 2.7 %convert_element_type.59 = bf16[1024,512]{1,0:T(8,128)(2,1)} convert(f32[1024,512]{1,0:T(8,128)} %scatter_custom_fusion) | non-fusion elementwise | flops 524288 | bytes 3145728 | tf_op jit(solution)/shard_map/convert_element_type | solution.py:136
  (30 shorter events, 0.2 us)
Async XLA Ops:
  6.5 82.9 %copy-start = (bf16[4096,128]{1,0:T(8,128)(2,1)S(1)}, bf16[4096,128]{1,0:T(8,128)(2,1)}, u32[]{:S(2)}) copy-start(bf16[4096,128]{1,0:T(8,128)(2,1)} %param.14) | copy-start | bytes 3145732
  6.5 35.7 %all-gather.4.cloned.1.call-start = ((), (), s32[]{:S(2)}) async-start(), calls=%async_computation.2 | async-start | bytes 2359296 | tf_op jit(solution)/shard_map/all_gather | solution.py:63
  46.1 6.7 %copy-start.3 = (bf16[4096]{0:T(1024)(128)(2,1)S(1)}, bf16[4096]{0:T(1024)(128)(2,1)}, u32[]{:S(2)}) copy-start(bf16[4096]{0:T(1024)(128)(2,1)} %param.11) | copy-start | bytes 24580
  46.1 39.2 %all-to-all-start = ((bf16[2,16,8,4096]{3,2,0,1:T(8,128)(2,1)}), bf16[2,16,8,4096]{3,2,0,1:T(8,128)(2,1)S(1)}, u32[]{:S(2)}, u32[]{:S(2)}) async-start(bf16[2,16,8,4096]{3,2,0,1:T(8,128)(2,1)} %copy.48), calls=%async_computation | async-start | bytes 4194304 | tf_op jit(solution)/shard_map/all_to_all | solution.py:67
  52.7 78.8 %all-gather.6.cloned.1.call-start = ((), (), s32[]{:S(2)}) async-start(), calls=%async_computation.3 | async-start | bytes 1114112 | tf_op jit(solution)/shard_map/all_gather | solution.py:94
  90.0 2.5 %copy-start.5 = (f32[8]{0:T(128)S(1)}, f32[8]{0:T(128)}, u32[]{:S(2)}) copy-start(f32[8]{0:T(128)} %param.17) | copy-start | bytes 100
  92.4 73.1 %all-gather.8.cloned.1.call-start = ((), (), s32[]{:S(2)}) async-start(), calls=%async_computation.4 | async-start | bytes 2359296 | tf_op jit(solution)/shard_map/all_gather | solution.py:124
  133.8 2.1 %copy-start.2 = (bf16[2,2048,128]{2,1,0:T(8,128)(2,1)S(1)}, bf16[2,2048,128]{2,1,0:T(8,128)(2,1)}, u32[]{:S(2)}) copy-start(bf16[2,2048,128]{2,1,0:T(8,128)(2,1)} %all-gather.6.cloned.1.call-done) | copy-start | bytes 3145732
  136.0 2.8 %copy-start.4 = (bf16[4096]{0:T(1024)(128)(2,1)S(1)}, bf16[4096]{0:T(1024)(128)(2,1)}, u32[]{:S(2)}) copy-start(bf16[4096]{0:T(1024)(128)(2,1)} %param.12) | copy-start | bytes 24580
  170.8 8.0 %copy-start.1 = (bf16[1024,512]{1,0:T(8,128)(2,1)S(1)}, bf16[1024,512]{1,0:T(8,128)(2,1)}, u32[]{:S(2)}) copy-start(bf16[1024,512]{1,0:T(8,128)(2,1)} %param.10) | copy-start | bytes 3145732
  172.2 14.8 %all-to-all-start.1 = ((bf16[2,16,8,512]{3,2,0,1:T(8,128)(2,1)}), bf16[2,16,8,512]{3,2,0,1:T(8,128)(2,1)S(1)}, u32[]{:S(2)}, u32[]{:S(2)}) async-start(bf16[2,16,8,512]{3,2,0,1:T(8,128)(2,1)} %copy.42), calls=%async_computation.1 | async-start | bytes 524288 | tf_op jit(solution)/shard_map/all_to_all | solution.py:130
Sparse Core Ops, SparseCore 0:
  13.2 29.0 all-gather.3
  92.5 38.9 all-gather.5
  138.9 26.4 all-gather.7
where the time goes:
time: 202 us
  waiting for transfers between devices  125 us (62%)
  other arithmetic  20.7 us (10%)
  matrix products  17.7 us (9%)
  between operations  15.3 us (8%)
  starting transfers between devices  13.2 us (7%)
  local copies, waits for them, and re-layouts  9.37 us (5%)
    all_gather x1, waiting for transfers between devices, on_device(): piece = lax.all_gather(paired, 'seq', axis=1, tiled=True)  34 us
    all_to_all x1, waiting for transfers between devices, on_device(): lax.all_to_all(outgoing, 'seq', split_axis=1, concat_axis=1, tiled=True)  32.2 us
    all_gather x1, waiting for transfers between devices, on_device(): whole_rows = lax.all_gather(gathered_rows, 'mp', axis=1, tiled=True)  26.6 us
    all_gather x1, waiting for transfers between devices, on_device(): lax.all_gather(attended, 'mp', axis=1, tiled=True)  26 us
    all_to_all x1, starting transfers between devices, on_device(): lax.all_to_all(outgoing, 'seq', split_axis=1, concat_axis=1, tiled=True)  6.6 us
    all_to_all x1, waiting for transfers between devices, on_device(): lax.all_to_all(outgoing_back, 'seq', split_axis=1, concat_axis=1, tiled=T...  6.57 us
    all_to_all x1, starting transfers between devices, on_device(): lax.all_to_all(outgoing_back, 'seq', split_axis=1, concat_axis=1, tiled=T...  6.53 us
    dot_general x1, matrix products, on_device(): jnp.dot(lax.all_gather(attended, 'mp', axis=1, tiled=True), final_project...  5.31 us
  transfers between devices with their start and end apart: 5, of which 5 were waited for; matrix products, arithmetic and copies ran while one was open for 4% of the time, Pallas kernels for 0%

commit v1 on v0

v1 whole, which is shorter than its diff:
```python
import functools
import math

import jax
import jax.numpy as jnp
from jax import lax
from jax.experimental import pallas as pl
from jax.experimental.pallas import tpu as pltpu
from jax.sharding import PartitionSpec as P

NSEQ = 16
NMP = 8
BLOCK = 8
OWNED = 128
SLOTS = 256
SRC = 1024
FEAT = 512
WIDTH = 4096
HEAD = 128
GROUP = 8
MIB = 1 << 20

VMEM = pl.BlockSpec(memory_space=pltpu.VMEM)
SMEM = pl.BlockSpec(memory_space=pltpu.SMEM)
F32 = jnp.float32
BF16 = jnp.bfloat16


def params(mib):
    return pltpu.CompilerParams(vmem_limit_bytes=mib * MIB)


def cost(flops, bytes_accessed, transcendentals=0):
    return pl.CostEstimate(flops=flops, bytes_accessed=bytes_accessed, transcendentals=transcendentals)


def own_span(tally, shard):
    row = lax.broadcasted_iota(jnp.int32, (NSEQ, NSEQ), 0)
    before = jnp.sum(jnp.where(row < shard, tally, 0))
    mine = jnp.sum(jnp.where(row == shard, tally, 0))
    return before // BLOCK, mine


def pick_kernel(tally_ref, select_ref, rows_ref, out_ref):
    first, count = own_span(tally_ref[...], lax.axis_index("seq"))
    listed = select_ref[...]
    slot = lax.broadcasted_iota(jnp.int32, (1, SLOTS), 1)
    listed = jnp.where(slot < count, listed, -1).astype(F32)
    column = jnp.broadcast_to(listed, (128, SLOTS)).T
    lane = lax.broadcasted_iota(jnp.int32, (SLOTS, 128), 1).astype(F32)
    hot = jnp.concatenate(
        [(column == lane + float(128 * k)).astype(F32) for k in range(SRC // 128)], axis=1
    ).astype(BF16)
    picked = jnp.dot(hot, rows_ref[...], preferred_element_type=F32)
    for j in range(SLOTS // BLOCK):
        owner = lax.rem(first + j, NSEQ)
        out_ref[owner, j // NSEQ] = picked[BLOCK * j : BLOCK * (j + 1)].astype(BF16)


def table_kernel(tally_ref, table_ref):
    shard = lax.axis_index("seq")
    starts = []
    start = jnp.int32(0)
    for s in range(NSEQ):
        starts.append(start)
        table_ref[0, s] = start
        total = jnp.int32(0)
        for d in range(NSEQ):
            total = total + tally_ref[s, d]
        start = start + total // BLOCK
    starts.append(start)
    for i in range(NSEQ):
        block = i * NSEQ + shard
        source = jnp.int32(0)
        begin = jnp.int32(0)
        for s in range(1, NSEQ):
            past = starts[s] <= block
            source = jnp.where(past, s, source)
            begin = jnp.where(past, starts[s], begin)
        table_ref[1, i] = source
        table_ref[2, i] = (block - begin) // NSEQ


def compact_kernel(table_ref, in_ref, out_ref):
    for i in range(0, NSEQ, 2):
        pair = [
            in_ref[table_ref[1, k], table_ref[2, k]].astype(F32) for k in (i, i + 1)
        ]
        out_ref[BLOCK * i : BLOCK * (i + 2)] = jnp.concatenate(pair, axis=0).astype(BF16)


def block_of(k):
    me = lax.axis_index("mp")
    chip = lax.rem(me // 2 + (4 - k // 2), 4)
    core = lax.rem(lax.rem(me, 2) + k % 2, 2)
    return chip * 2 + core


def pair_kernel(gain_ref, keys_ref, values_ref, *refs):
    blocks, (normed_ref, pair_ref) = refs[:NMP], refs[NMP:]
    squares = jnp.zeros((OWNED, 128), F32)
    for k in range(NMP):
        wide = blocks[k][...].astype(F32)
        square = wide * wide
        for c in range(FEAT // 128):
            squares = squares + square[:, 128 * c : 128 * (c + 1)]
    inverse = lax.rsqrt(jnp.sum(squares, axis=1, keepdims=True) / WIDTH + 1e-05)
    keys = jnp.zeros((OWNED, HEAD), F32)
    values = jnp.zeros((OWNED, HEAD), F32)
    for k in range(NMP):
        m = block_of(k)
        rows = pl.ds(pl.multiple_of(m * FEAT, FEAT), FEAT)
        normed = (blocks[k][...].astype(F32) * inverse * gain_ref[m]).astype(BF16)
        normed_ref[k] = normed
        keys = keys + jnp.dot(normed, keys_ref[rows, :], preferred_element_type=F32)
        values = values + jnp.dot(normed, values_ref[rows, :], preferred_element_type=F32)
    keys = keys.astype(BF16)
    values = values.astype(BF16)
    for d in range(NSEQ):
        pair_ref[d, :, :HEAD] = keys
        pair_ref[d, :, HEAD:] = values


def query_kernel(normed_ref, weight_ref, gate_weight_ref, *refs):
    blocks, (query_ref, gate_ref) = refs[:NMP], refs[NMP:]
    total = jnp.zeros((OWNED, GROUP * HEAD), F32)
    routed = jnp.zeros((OWNED, FEAT), F32)
    for k in range(NMP):
        m = block_of(k)
        rows = pl.ds(pl.multiple_of(m * FEAT, FEAT), FEAT)
        total = total + jnp.dot(normed_ref[k], weight_ref[rows, :], preferred_element_type=F32)
        routed = routed + blocks[k][...].astype(F32) * gate_weight_ref[m]
    query_ref[...] = total.astype(BF16)
    gate_ref[...] = jnp.broadcast_to(
        jax.nn.sigmoid(jnp.sum(routed, axis=1, keepdims=True)), (OWNED, 128)
    )


def attention_kernel(sharp_ref, query_ref, pair_ref, out_ref):
    shard = lax.axis_index("seq")
    step = 4 * BLOCK
    rows = GROUP * step
    many = NSEQ * step
    scale = jnp.concatenate(
        [jnp.full((step, 1), sharp_ref[h] * (math.log2(math.e) / math.sqrt(HEAD)), F32) for h in range(GROUP)],
        axis=0,
    )
    q_row = lax.rem(lax.broadcasted_iota(jnp.int32, (rows, 1), 0), step)
    q_place = (q_row // BLOCK * NSEQ + shard) * BLOCK + q_row % BLOCK
    k_row = lax.broadcasted_iota(jnp.int32, (1, many), 1)
    k_place = ((k_row % step) // BLOCK * NSEQ + k_row // step) * BLOCK + k_row % BLOCK
    allowed = k_place <= q_place
    for j in range(4):
        here = slice(step * j, step * (j + 1))
        query = jnp.concatenate(
            [query_ref[here, HEAD * h : HEAD * (h + 1)] for h in range(GROUP)], axis=0
        )
        scores = []
        best = None
        for c in range(j + 1):
            keys = pair_ref[:, step * c : step * (c + 1), :HEAD].reshape(many, HEAD)
            score = lax.dot_general(
                query, keys, (((1,), (1,)), ((), ())), preferred_element_type=F32
            )
            if c == j:
                score = jnp.where(allowed, score, -1e30)
            scores.append(score)
            top = jnp.max(score, axis=1, keepdims=True)
            best = top if best is None else jnp.maximum(best, top)
        offset = best * scale
        total = jnp.zeros((rows, 1), F32)
        mixed = jnp.zeros((rows, HEAD), F32)
        for c in range(j + 1):
            weight = jnp.exp2(scores[c] * scale - offset)
            total = total + jnp.sum(weight, axis=1, keepdims=True)
            values = pair_ref[:, step * c : step * (c + 1), HEAD:].reshape(many, HEAD)
            mixed = mixed + jnp.dot(weight.astype(BF16), values, preferred_element_type=F32)
        mixed = (mixed / total).astype(BF16)
        for h in range(GROUP):
            out_ref[here, HEAD * h : HEAD * (h + 1)] = mixed[step * h : step * (h + 1)]


def project_kernel(table_ref, gate_ref, weight_ref, *refs):
    blocks, (out_ref, delta_ref) = refs[:NMP], refs[NMP:]
    shard = lax.axis_index("seq")
    wide = GROUP * HEAD
    total = jnp.zeros((OWNED, FEAT), F32)
    for k in range(NMP):
        m = block_of(k)
        rows = pl.ds(pl.multiple_of(m * wide, wide), wide)
        total = total + jnp.dot(blocks[k][...], weight_ref[rows, :], preferred_element_type=F32)
    delta = total * gate_ref[:, :1]
    for i in range(NSEQ):
        delta_ref[i] = delta[BLOCK * i : BLOCK * (i + 1)]
    for s in range(NSEQ):
        first = table_ref[0, s]
        counter = lax.rem(shard + NSEQ * NSEQ - first, NSEQ)
        for half in range(2):
            place = jnp.minimum((first + counter) // NSEQ + half, NSEQ - 1)
            out_ref[s, half] = delta_ref[place].astype(BF16)


def blend_kernel(tally_ref, select_ref, rows_ref, back_ref, out_ref, update_ref):
    first, count = own_span(tally_ref[...], lax.axis_index("seq"))
    for j in range(0, SLOTS // BLOCK, 2):
        pair = [
            back_ref[lax.rem(first + k, NSEQ), k // NSEQ].astype(F32) for k in (j, j + 1)
        ]
        update_ref[BLOCK * j : BLOCK * (j + 2)] = jnp.concatenate(pair, axis=0).astype(BF16)
    slot = lax.broadcasted_iota(jnp.int32, (1, SLOTS), 1)
    listed = jnp.where(slot < count, select_ref[...], -1)
    token = lax.broadcasted_iota(jnp.int32, (SRC, 1), 0)
    hot = (listed == token).astype(F32).astype(BF16)
    added = jnp.dot(hot, update_ref[...], preferred_element_type=F32)
    out_ref[...] = (rows_ref[...].astype(F32) + added).astype(BF16)


def z_step(array, steps):
    pairs = [(z * 2 + c, (z + steps) % 4 * 2 + c) for z in range(4) for c in range(2)]
    return lax.ppermute(array, "mp", pairs)


def other_core(array):
    return lax.ppermute(array, "mp", [(m, m ^ 1) for m in range(NMP)])


def gather_mp(array):
    chips = {0: array, 1: z_step(array, 1), 3: z_step(array, 3), 2: z_step(array, 2)}
    out = []
    for k in range(4):
        out += [chips[k], other_core(chips[k])]
    return out


def shape(dims, dtype=BF16):
    return jax.ShapeDtypeStruct(dims, dtype)


def on_device(
    residual_activations,
    prelayer_gain_vector,
    gating_projection,
    asker_projection,
    lookup_projection,
    content_projection,
    final_projection,
    logit_sharpness,
    selection_table,
    dispatched_tally_table,
):
    gain = prelayer_gain_vector.astype(F32).reshape(NMP, 1, FEAT)
    gate_weight = gating_projection.astype(F32).reshape(NMP, 1, FEAT)
    outgoing = pl.pallas_call(
        pick_kernel,
        out_shape=shape((NSEQ, 2, BLOCK, FEAT)),
        in_specs=[VMEM] * 3,
        out_specs=VMEM,
        compiler_params=params(16),
        name="pick",
    )(dispatched_tally_table, selection_table, residual_activations)
    table = pl.pallas_call(
        table_kernel,
        out_shape=shape((3, NSEQ), jnp.int32),
        in_specs=[SMEM],
        out_specs=SMEM,
        compiler_params=params(4),
        name="table",
    )(dispatched_tally_table)
    incoming = lax.all_to_all(outgoing, "seq", split_axis=0, concat_axis=0, tiled=True)
    tokens = pl.pallas_call(
        compact_kernel,
        out_shape=shape((OWNED, FEAT)),
        in_specs=[SMEM, VMEM],
        out_specs=VMEM,
        compiler_params=params(4),
        name="compact",
    )(table, incoming)
    blocks = gather_mp(tokens)
    normed, pair = pl.pallas_call(
        pair_kernel,
        out_shape=(shape((NMP, OWNED, FEAT)), shape((NSEQ, OWNED, 2 * HEAD))),
        in_specs=[VMEM] * (3 + NMP),
        out_specs=(VMEM, VMEM),
        compiler_params=params(16),
        cost_estimate=cost(2 * OWNED * WIDTH * 2 * HEAD, 4 * MIB),
        name="pair",
    )(gain, lookup_projection, content_projection, *blocks)
    pairs = lax.all_to_all(pair, "seq", split_axis=0, concat_axis=0, tiled=True)
    query, gate = pl.pallas_call(
        query_kernel,
        out_shape=(shape((OWNED, GROUP * HEAD)), shape((OWNED, 128), F32)),
        in_specs=[VMEM] * (3 + NMP),
        out_specs=(VMEM, VMEM),
        compiler_params=params(24),
        cost_estimate=cost(2 * OWNED * WIDTH * GROUP * HEAD, 10 * MIB),
        name="query",
    )(normed, asker_projection, gate_weight, *blocks)
    attended = pl.pallas_call(
        attention_kernel,
        out_shape=shape((OWNED, GROUP * HEAD)),
        in_specs=[SMEM, VMEM, VMEM],
        out_specs=VMEM,
        compiler_params=params(24),
        name="attend",
    )(logit_sharpness, query, pairs)
    heads = gather_mp(attended)
    outgoing_back = pl.pallas_call(
        project_kernel,
        out_shape=shape((NSEQ, 2, BLOCK, FEAT)),
        in_specs=[SMEM] + [VMEM] * (2 + NMP),
        out_specs=VMEM,
        scratch_shapes=[pltpu.VMEM((NSEQ, BLOCK, FEAT), F32)],
        compiler_params=params(24),
        name="project",
    )(table, gate, final_projection, *heads)
    back = lax.all_to_all(outgoing_back, "seq", split_axis=0, concat_axis=0, tiled=True)
    return pl.pallas_call(
        blend_kernel,
        out_shape=shape((SRC, FEAT)),
        in_specs=[VMEM] * 4,
        out_specs=VMEM,
        scratch_shapes=[pltpu.VMEM((SLOTS, FEAT), BF16)],
        compiler_params=params(24),
        name="blend",
    )(dispatched_tally_table, selection_table, residual_activations, back)


def solution(mesh):
    placed = (
        P("seq", "mp"),
        P(),
        P(),
        P(None, "mp"),
        P(None, "mp"),
        P(None, "mp"),
        P(None, "mp"),
        P("mp"),
        P("seq", None),
        P(),
    )
    return jax.shard_map(
        on_device, mesh=mesh, in_specs=placed, out_specs=P("seq", "mp"), check_vma=False
    )
```

time: 202 us -> 101 us (0.50)
  waiting for transfers between devices: 125 us -> 22.9 us
  starting transfers between devices: 13.2 us -> 36.9 us
  other arithmetic: 20.7 us -> 1.4 us
  matrix products: 17.7 us -> 0 us
  between operations: 15.3 us -> 0.11 us
  Pallas kernels: 0 us -> 14.2 us
  blocking collectives: 0 us -> 11.9 us
  local copies, waits for them, and re-layouts: 9.37 us -> 12.5 us
    all_gather x3 -> x0, waiting for transfers between devices: 86.6 us -> none  [the longest x1 34 us: on_device(): piece = lax.all_gather(paired, 'seq', axis=1, tiled=True)]
    ppermute x0 -> x14, starting transfers between devices: none -> 25.6 us  [the longest x8 19.5 us: other_core(): return lax.ppermute(array, 'mp', [(m, m ^ 1) for m in range(NMP)])]
    all_to_all x2, waiting for transfers between devices: 38.7 us -> 16.6 us  [the longest x1 11.6 us: on_device(): pairs = lax.all_to_all(pair, 'seq', split_axis=0, concat_axis=0, tiled=True)]
    dot_general x7 -> x0, matrix products: 17.7 us -> none  [the longest x1 5.31 us: on_device(): jnp.dot(lax.all_gather(attended, 'mp', axis=1, tiled=True), final_project...]
    pallas_call x0 -> x8, Pallas kernels: none -> 14.2 us  [the longest x1 3.46 us: on_device(): pl.pallas_call(attention_kernel, out_shape=shape((OWNED, GROUP * HEAD)),...]
    all_to_all x0 -> x1, blocking collectives: none -> 11.9 us  [on_device(): lax.all_to_all(outgoing_back, 'seq', split_axis=0, concat_axis=0, tiled=T...]
    unnamed x14 -> x24, local copies, waits for them, and re-layouts: 1.53 us -> 12.5 us
    ppermute x0 -> x14, waiting for transfers between devices: none -> 6.24 us  [the longest x6 4.8 us: z_step(): return lax.ppermute(array, 'mp', pairs)]
  transfers between devices with their start and end apart: 5 -> 16, of which waited for: 5 -> 6; matrix products, arithmetic and copies ran while one was open for 4% -> 1% of each run, Pallas kernels for 0% -> 3%
where the time goes in v1:
time: 101 us; the launch traced here: 99.9 us
  starting transfers between devices  36.9 us (37%)
  waiting for transfers between devices  22.9 us (23%)
  Pallas kernels  14.2 us (14%)
  local copies, waits for them, and re-layouts  12.5 us (12%)
  blocking collectives  11.9 us (12%)
  other arithmetic  1.4 us (1%)
    ppermute x8, starting transfers between devices, other_core(): return lax.ppermute(array, 'mp', [(m, m ^ 1) for m in range(NMP)])  19.5 us
    unnamed x24, local copies, waits for them, and re-layouts  12.5 us
    all_to_all x1, blocking collectives, on_device(): lax.all_to_all(outgoing_back, 'seq', split_axis=0, concat_axis=0, tiled=T...  11.9 us
    all_to_all x1, waiting for transfers between devices, on_device(): pairs = lax.all_to_all(pair, 'seq', split_axis=0, concat_axis=0, tiled=True)  11.6 us
    all_to_all x1, starting transfers between devices, on_device(): lax.all_to_all(outgoing, 'seq', split_axis=0, concat_axis=0, tiled=True)  7.71 us
    ppermute x6, starting transfers between devices, z_step(): return lax.ppermute(array, 'mp', pairs)  6.1 us
    all_to_all x1, waiting for transfers between devices, on_device(): lax.all_to_all(outgoing, 'seq', split_axis=0, concat_axis=0, tiled=True)  5.01 us
    ppermute x6, waiting for transfers between devices, z_step(): return lax.ppermute(array, 'mp', pairs)  4.8 us
  transfers between devices with their start and end apart: 16, of which 6 were waited for; matrix products, arithmetic and copies ran while one was open for 1% of the time, Pallas kernels for 3%

profile of v1, /device:TPU:1, one launch (start us, length us, event | category | flops | bytes accessed | tf_op | source)
XLA Modules:
  0.0 99.9 jit_solution(8944968005409892292)
XLA Ops:
  0.0 1.2 %copy-done.2 = bf16[1024,512]{1,0:T(8,128)(2,1)S(1)} copy-done((bf16[1024,512]{1,0:T(8,128)(2,1)S(1)}, bf16[1024,512]{1,0:T(8,128)(2,1)}, u32[]{:S(2)}) %copy-start.2) | copy-done | bytes 1048600
  1.2 0.7 copy-done.6
  1.9 0.7 copy-done.9
  2.6 1.4 %pick.1 = bf16[16,2,8,512]{3,2,1,0:T(8,128)(2,1)} custom-call(s32[16,16]{1,0:T(8,128)S(1)} %copy-done.6, s32[1,256]{1,0:T(1,128)S(1)} %copy-done.9, bf16[1024,512]{1,0:T(8,128)(2,1)S(1)} %copy-done.2), custom_call_target="tpu_custom_call" | custom-call | tf_op jit(solution)/shard_map/pick/pallas_call | solution.py:253
  4.0 7.7 %all-to-all-start = ((bf16[16,2,8,512]{3,2,1,0:T(8,128)(2,1)}), bf16[16,2,8,512]{3,2,1,0:T(8,128)(2,1)S(1)}, u32[]{:S(2)}, u32[]{:S(2)}) async-start(bf16[16,2,8,512]{3,2,1,0:T(8,128)(2,1)} %pick.1), calls=%async_computation | async-start | bytes 524288 | tf_op jit(solution)/shard_map/all_to_all | solution.py:269
  11.7 0.0 copy-start.7
  11.7 0.7 copy-done.7
  12.4 1.8 %table.1.table_ref = s32[3,16]{1,0:T(4,128)S(1)} custom-call(s32[16,16]{1,0:T(8,128)S(1)} %copy-done.7), custom_call_target="tpu_custom_call" | custom-call | tf_op jit(solution)/shard_map/table/pallas_call | solution.py:261
  14.2 5.0 %all-to-all-done.in_ref = bf16[16,2,8,512]{3,2,1,0:T(8,128)(2,1)S(1)} async-done(((bf16[16,2,8,512]{3,2,1,0:T(8,128)(2,1)}), bf16[16,2,8,512]{3,2,1,0:T(8,128)(2,1)S(1)}, u32[]{:S(2)}, u32[]{:S(2)}) %all-to-all-start) | async-done | bytes 262176 | tf_op jit(solution)/shard_map/all_to_all | solution.py:269
  19.2 0.6 compact.1.refs_0_
  19.8 3.8 %collective-permute-start.5 = (bf16[128,512]{1,0:T(8,128)(2,1)S(1)}, bf16[128,512]{1,0:T(8,128)(2,1)S(1)}, u32[]{:S(2)}, u32[]{:S(2)}) collective-permute-start(bf16[128,512]{1,0:T(8,128)(2,1)S(1)} %compact.1.refs_0_), channel_id=1, source_target_pairs={{0,6},{1,7},{2,0},{3,1},{4,2},{5,3},{6,4},{7,5},{8,14},{9,15},{10,... | collective-permute-start | bytes 393224 | tf_op jit(solution)/shard_map/ppermute | solution.py:220
  23.7 0.0 collective-permute-start.3
  23.7 0.7 collective-permute-start.1
  24.4 2.9 %collective-permute-start = (bf16[128,512]{1,0:T(8,128)(2,1)S(1)}, bf16[128,512]{1,0:T(8,128)(2,1)S(1)}, u32[]{:S(2)}, u32[]{:S(2)}) collective-permute-start(bf16[128,512]{1,0:T(8,128)(2,1)S(1)} %compact.1.refs_0_), channel_id=1, source_target_pairs={{0,1},{1,0},{2,3},{3,2},{4,5},{5,4},{6,7},{7,6},{8,9},{9,8},{10,11... | collective-permute-start | bytes 393224 | tf_op jit(solution)/shard_map/ppermute | solution.py:224
  27.3 2.9 %collective-permute-start.6 = (bf16[128,512]{1,0:T(8,128)(2,1)S(1)}, bf16[128,512]{1,0:T(8,128)(2,1)S(1)}, u32[]{:S(2)}, u32[]{:S(2)}) collective-permute-start(bf16[128,512]{1,0:T(8,128)(2,1)S(1)} %collective-permute-done.5.refs_6_), channel_id=1, source_target_pairs={{0,1},{1,0},{2,3},{3,2},{4,5},{5,4},{6,7},{7,6},{8,9},{9,8},{10,11... | collective-permute-start | bytes 393224 | tf_op jit(solution)/shard_map/ppermute | solution.py:224
  30.2 2.4 %collective-permute-start.4 = (bf16[128,512]{1,0:T(8,128)(2,1)S(1)}, bf16[128,512]{1,0:T(8,128)(2,1)S(1)}, u32[]{:S(2)}, u32[]{:S(2)}) collective-permute-start(bf16[128,512]{1,0:T(8,128)(2,1)S(1)} %collective-permute-done.3.refs_4_), channel_id=1, source_target_pairs={{0,1},{1,0},{2,3},{3,2},{4,5},{5,4},{6,7},{7,6},{8,9},{9,8},{10,11... | collective-permute-start | bytes 393224 | tf_op jit(solution)/shard_map/ppermute | solution.py:224
  32.6 0.0 collective-permute-done.1.refs_2_
  32.6 1.0 collective-permute-start.2
  33.6 0.7 reshape.14
  34.3 0.0 collective-permute-done.4.refs_5_
  34.3 0.3 collective-permute-done.2.refs_3_
  34.6 1.2 %copy-done.4 = bf16[4096,128]{1,0:T(8,128)(2,1)S(1)} copy-done((bf16[4096,128]{1,0:T(8,128)(2,1)S(1)}, bf16[4096,128]{1,0:T(8,128)(2,1)}, u32[]{:S(2)}) %copy-start.4) | copy-done | bytes 1048600
  35.8 1.2 %copy-done.5 = bf16[4096,128]{1,0:T(8,128)(2,1)S(1)} copy-done((bf16[4096,128]{1,0:T(8,128)(2,1)S(1)}, bf16[4096,128]{1,0:T(8,128)(2,1)}, u32[]{:S(2)}) %copy-start.5) | copy-done | bytes 1048600
  37.1 2.1 %pair.1 = (bf16[8,128,512]{2,1,0:T(8,128)(2,1)S(1)}, bf16[16,128,256]{2,1,0:T(8,128)(2,1)}) custom-call(f32[8,1,512]{2,1,0:T(1,128)S(1)} %bitcast.2, bf16[4096,128]{1,0:T(8,128)(2,1)S(1)} %copy-done.4, bf16[4096,128]{1,0:T(8,128)(2,1)S(1)} %copy-done.5, bf16[128,512]{1,0:T(8,128)(2,1)S(1)} %compact.1.refs_0_, ...), custom_call_target="tpu_custom_call" | custom-call | flops 268435456 | bytes 4194304 | tf_op jit(solution)/shard_map/pair/pallas_call | solution.py:279
  39.2 3.7 %all-to-all-start.1 = ((bf16[16,128,256]{2,1,0:T(8,128)(2,1)}), bf16[16,128,256]{2,1,0:T(8,128)(2,1)S(1)}, u32[]{:S(2)}, u32[]{:S(2)}) async-start(bf16[16,128,256]{2,1,0:T(8,128)(2,1)} %get-tuple-element.12), calls=%async_computation.1 | async-start | bytes 2097152 | tf_op jit(solution)/shard_map/all_to_all | solution.py:288
  42.8 0.7 reshape.16
  43.5 3.4 %copy-done = bf16[4096,1024]{1,0:T(8,128)(2,1)S(1)} copy-done((bf16[4096,1024]{1,0:T(8,128)(2,1)S(1)}, bf16[4096,1024]{1,0:T(8,128)(2,1)}, u32[]{:S(2)}) %copy-start) | copy-done | bytes 8388632
  46.9 1.4 %query.1 = (bf16[128,1024]{1,0:T(8,128)(2,1)S(1)}, f32[128,128]{1,0:T(8,128)S(1)}) custom-call(bf16[8,128,512]{2,1,0:T(8,128)(2,1)S(1)} %get-tuple-element.9.normed_ref, bf16[4096,1024]{1,0:T(8,128)(2,1)S(1)} %copy-done, f32[8,1,512]{2,1,0:T(1,128)S(1)} %bitcast.3, bf16[128,512]{1,0:T(8,128)(2,1)S(1)} %compact.1.refs_0_, ...), custom_call_target="tpu_custom_call" | custom-call | flops 1073741824 | bytes 10485760 | tf_op jit(solution)/shard_map/query/pallas_call | solution.py:289
  48.3 0.0 copy-start.3
  48.3 0.0 copy-start.8
  48.3 0.0 copy-start.10
  48.3 11.6 %all-to-all-done.1.pair_ref = bf16[16,128,256]{2,1,0:T(8,128)(2,1)S(1)} async-done(((bf16[16,128,256]{2,1,0:T(8,128)(2,1)}), bf16[16,128,256]{2,1,0:T(8,128)(2,1)S(1)}, u32[]{:S(2)}, u32[]{:S(2)}) %all-to-all-start.1) | async-done | bytes 1048608 | tf_op jit(solution)/shard_map/all_to_all | solution.py:288
  59.9 3.5 %attend.1.refs_0_ = bf16[128,1024]{1,0:T(8,128)(2,1)S(1)} custom-call(f32[8]{0:T(128)S(1)} %copy-done.11, bf16[128,1024]{1,0:T(8,128)(2,1)S(1)} %get-tuple-element.11.query_ref, bf16[16,128,256]{2,1,0:T(8,128)(2,1)S(1)} %all-to-all-done.1.pair_ref), custom_call_target="tpu_custom_call" | custom-call | tf_op jit(solution)/shard_map/attend/pallas_call | solution.py:298
  63.4 0.7 collective-permute-start.12
  64.1 0.1 collective-permute-start.10
  64.2 0.8 collective-permute-start.8
  65.0 2.5 %collective-permute-start.7 = (bf16[128,1024]{1,0:T(8,128)(2,1)S(1)}, bf16[128,1024]{1,0:T(8,128)(2,1)S(1)}, u32[]{:S(2)}, u32[]{:S(2)}) collective-permute-start(bf16[128,1024]{1,0:T(8,128)(2,1)S(1)} %attend.1.refs_0_), channel_id=1, source_target_pairs={{0,1},{1,0},{2,3},{3,2},{4,5},{5,4},{6,7},{7,6},{8,9},{9,8},{10,11... | collective-permute-start | bytes 786440 | tf_op jit(solution)/shard_map/ppermute | solution.py:224
  67.5 2.1 %collective-permute-done.12.refs_6_ = bf16[128,1024]{1,0:T(8,128)(2,1)S(1)} collective-permute-done((bf16[128,1024]{1,0:T(8,128)(2,1)S(1)}, bf16[128,1024]{1,0:T(8,128)(2,1)S(1)}, u32[]{:S(2)}, u32[]{:S(2)}) %collective-permute-start.12) | collective-permute-done | bytes 262176 | tf_op jit(solution)/shard_map/ppermute | solution.py:220
  69.6 4.8 %collective-permute-start.13 = (bf16[128,1024]{1,0:T(8,128)(2,1)S(1)}, bf16[128,1024]{1,0:T(8,128)(2,1)S(1)}, u32[]{:S(2)}, u32[]{:S(2)}) collective-permute-start(bf16[128,1024]{1,0:T(8,128)(2,1)S(1)} %collective-permute-done.12.refs_6_), channel_id=1, source_target_pairs={{0,1},{1,0},{2,3},{3,2},{4,5},{5,4},{6,7},{7,6},{8,9},{9,8},{10,11... | collective-permute-start | bytes 786440 | tf_op jit(solution)/shard_map/ppermute | solution.py:224
  74.4 2.4 %collective-permute-start.11 = (bf16[128,1024]{1,0:T(8,128)(2,1)S(1)}, bf16[128,1024]{1,0:T(8,128)(2,1)S(1)}, u32[]{:S(2)}, u32[]{:S(2)}) collective-permute-start(bf16[128,1024]{1,0:T(8,128)(2,1)S(1)} %collective-permute-done.10.refs_4_), channel_id=1, source_target_pairs={{0,1},{1,0},{2,3},{3,2},{4,5},{5,4},{6,7},{7,6},{8,9},{9,8},{10,11... | collective-permute-start | bytes 786440 | tf_op jit(solution)/shard_map/ppermute | solution.py:224
  76.8 2.7 %collective-permute-done.8.refs_2_ = bf16[128,1024]{1,0:T(8,128)(2,1)S(1)} collective-permute-done((bf16[128,1024]{1,0:T(8,128)(2,1)S(1)}, bf16[128,1024]{1,0:T(8,128)(2,1)S(1)}, u32[]{:S(2)}, u32[]{:S(2)}) %collective-permute-start.8) | collective-permute-done | bytes 262176 | tf_op jit(solution)/shard_map/ppermute | solution.py:220
  79.5 0.5 collective-permute-start.9
  80.0 0.0 collective-permute-done.7.refs_1_
  80.0 1.1 %collective-permute-done.9.refs_3_ = bf16[128,1024]{1,0:T(8,128)(2,1)S(1)} collective-permute-done((bf16[128,1024]{1,0:T(8,128)(2,1)S(1)}, bf16[128,1024]{1,0:T(8,128)(2,1)S(1)}, u32[]{:S(2)}, u32[]{:S(2)}) %collective-permute-start.9) | collective-permute-done | bytes 262176 | tf_op jit(solution)/shard_map/ppermute | solution.py:224
  81.1 3.4 %copy-done.1 = bf16[8192,512]{1,0:T(8,128)(2,1)S(1)} copy-done((bf16[8192,512]{1,0:T(8,128)(2,1)S(1)}, bf16[8192,512]{1,0:T(8,128)(2,1)}, u32[]{:S(2)}) %copy-start.1) | copy-done | bytes 8388632
  84.5 1.9 %project.1 = bf16[16,2,8,512]{3,2,1,0:T(8,128)(2,1)S(1)} custom-call(s32[3,16]{1,0:T(4,128)S(1)} %table.1.table_ref, f32[128,128]{1,0:T(8,128)S(1)} %get-tuple-element.10.gate_ref, bf16[8192,512]{1,0:T(8,128)(2,1)S(1)} %copy-done.1, bf16[128,1024]{1,0:T(8,128)(2,1)S(1)} %attend.1.refs_0_, bf16[128,1024]{1,0:T(8,128)(2,1)S(1)} %collective-permute-done.7.refs_1_, ...), custom_call_target="tpu_custom_call" | custom-call | tf_op jit(solution)/shard_map/project/pallas_call | solution.py:307
  86.4 11.9 %all_to_all.15.back_ref = bf16[16,2,8,512]{3,2,1,0:T(8,128)(2,1)S(1)} all-to-all(bf16[16,2,8,512]{3,2,1,0:T(8,128)(2,1)S(1)} %project.1), channel_id=1, replica_groups=mesh['seq'=16,'mp'=8] {'seq'}, dimensions={0} | all-to-all | bytes 524288 | tf_op jit(solution)/shard_map/all_to_all | solution.py:316
  98.3 1.6 %blend.1 = bf16[1024,512]{1,0:T(8,128)(2,1)} custom-call(s32[16,16]{1,0:T(8,128)S(1)} %copy-done.8, s32[1,256]{1,0:T(1,128)S(1)} %copy-done.10, bf16[1024,512]{1,0:T(8,128)(2,1)S(1)} %copy-done.3, bf16[16,2,8,512]{3,2,1,0:T(8,128)(2,1)S(1)} %all_to_all.15.back_ref), custom_call_target="tpu_custom_call" | custom-call | tf_op jit(solution)/shard_map/blend/pallas_call | solution.py:317
  (19 shorter events, 0.0 us)
Async XLA Ops:
  0.0 1.2 %copy-start.2 = (bf16[1024,512]{1,0:T(8,128)(2,1)S(1)}, bf16[1024,512]{1,0:T(8,128)(2,1)}, u32[]{:S(2)}) copy-start(bf16[1024,512]{1,0:T(8,128)(2,1)} %rows_ref.3) | copy-start | bytes 3145732
  1.2 0.7 copy-start.6
  1.9 0.7 copy-start.9
  4.0 56.0 %copy-start.11 = (f32[8]{0:T(128)S(1)}, f32[8]{0:T(128)}, u32[]{:S(2)}) copy-start(f32[8]{0:T(128)} %sharp_ref.1) | copy-start | bytes 100
  4.0 15.3 %all-to-all-start = ((bf16[16,2,8,512]{3,2,1,0:T(8,128)(2,1)}), bf16[16,2,8,512]{3,2,1,0:T(8,128)(2,1)S(1)}, u32[]{:S(2)}, u32[]{:S(2)}) async-start(bf16[16,2,8,512]{3,2,1,0:T(8,128)(2,1)} %pick.1), calls=%async_computation | async-start | bytes 524288 | tf_op jit(solution)/shard_map/all_to_all | solution.py:269
  11.7 0.7 copy-start.7
  19.8 7.5 %collective-permute-start.5 = (bf16[128,512]{1,0:T(8,128)(2,1)S(1)}, bf16[128,512]{1,0:T(8,128)(2,1)S(1)}, u32[]{:S(2)}, u32[]{:S(2)}) collective-permute-start(bf16[128,512]{1,0:T(8,128)(2,1)S(1)} %compact.1.refs_0_), channel_id=1, source_target_pairs={{0,6},{1,7},{2,0},{3,1},{4,2},{5,3},{6,4},{7,5},{8,14},{9,15},{10,... | collective-permute-start | bytes 393224 | tf_op jit(solution)/shard_map/ppermute | solution.py:220
  23.7 6.6 %collective-permute-start.3 = (bf16[128,512]{1,0:T(8,128)(2,1)S(1)}, bf16[128,512]{1,0:T(8,128)(2,1)S(1)}, u32[]{:S(2)}, u32[]{:S(2)}) collective-permute-start(bf16[128,512]{1,0:T(8,128)(2,1)S(1)} %compact.1.refs_0_), channel_id=1, source_target_pairs={{0,4},{1,5},{2,6},{3,7},{4,0},{5,1},{6,2},{7,3},{8,12},{9,13},{10,... | collective-permute-start | bytes 393224 | tf_op jit(solution)/shard_map/ppermute | solution.py:220
  23.7 9.0 %collective-permute-start.1 = (bf16[128,512]{1,0:T(8,128)(2,1)S(1)}, bf16[128,512]{1,0:T(8,128)(2,1)S(1)}, u32[]{:S(2)}, u32[]{:S(2)}) collective-permute-start(bf16[128,512]{1,0:T(8,128)(2,1)S(1)} %compact.1.refs_0_), channel_id=1, source_target_pairs={{0,2},{1,3},{2,4},{3,5},{4,6},{5,7},{6,0},{7,1},{8,10},{9,11},{10,... | collective-permute-start | bytes 393224 | tf_op jit(solution)/shard_map/ppermute | solution.py:220
  24.4 10.0 %collective-permute-start = (bf16[128,512]{1,0:T(8,128)(2,1)S(1)}, bf16[128,512]{1,0:T(8,128)(2,1)S(1)}, u32[]{:S(2)}, u32[]{:S(2)}) collective-permute-start(bf16[128,512]{1,0:T(8,128)(2,1)S(1)} %compact.1.refs_0_), channel_id=1, source_target_pairs={{0,1},{1,0},{2,3},{3,2},{4,5},{5,4},{6,7},{7,6},{8,9},{9,8},{10,11... | collective-permute-start | bytes 393224 | tf_op jit(solution)/shard_map/ppermute | solution.py:224
  27.3 7.0 %collective-permute-start.6 = (bf16[128,512]{1,0:T(8,128)(2,1)S(1)}, bf16[128,512]{1,0:T(8,128)(2,1)S(1)}, u32[]{:S(2)}, u32[]{:S(2)}) collective-permute-start(bf16[128,512]{1,0:T(8,128)(2,1)S(1)} %collective-permute-done.5.refs_6_), channel_id=1, source_target_pairs={{0,1},{1,0},{2,3},{3,2},{4,5},{5,4},{6,7},{7,6},{8,9},{9,8},{10,11... | collective-permute-start | bytes 393224 | tf_op jit(solution)/shard_map/ppermute | solution.py:224
  30.2 4.1 %collective-permute-start.4 = (bf16[128,512]{1,0:T(8,128)(2,1)S(1)}, bf16[128,512]{1,0:T(8,128)(2,1)S(1)}, u32[]{:S(2)}, u32[]{:S(2)}) collective-permute-start(bf16[128,512]{1,0:T(8,128)(2,1)S(1)} %collective-permute-done.3.refs_4_), channel_id=1, source_target_pairs={{0,1},{1,0},{2,3},{3,2},{4,5},{5,4},{6,7},{7,6},{8,9},{9,8},{10,11... | collective-permute-start | bytes 393224 | tf_op jit(solution)/shard_map/ppermute | solution.py:224
  32.6 2.0 %collective-permute-start.2 = (bf16[128,512]{1,0:T(8,128)(2,1)S(1)}, bf16[128,512]{1,0:T(8,128)(2,1)S(1)}, u32[]{:S(2)}, u32[]{:S(2)}) collective-permute-start(bf16[128,512]{1,0:T(8,128)(2,1)S(1)} %collective-permute-done.1.refs_2_), channel_id=1, source_target_pairs={{0,1},{1,0},{2,3},{3,2},{4,5},{5,4},{6,7},{7,6},{8,9},{9,8},{10,11... | collective-permute-start | bytes 393224 | tf_op jit(solution)/shard_map/ppermute | solution.py:224
  34.6 1.2 %copy-start.4 = (bf16[4096,128]{1,0:T(8,128)(2,1)S(1)}, bf16[4096,128]{1,0:T(8,128)(2,1)}, u32[]{:S(2)}) copy-start(bf16[4096,128]{1,0:T(8,128)(2,1)} %keys_ref.1) | copy-start | bytes 3145732
  35.8 1.2 %copy-start.5 = (bf16[4096,128]{1,0:T(8,128)(2,1)S(1)}, bf16[4096,128]{1,0:T(8,128)(2,1)}, u32[]{:S(2)}) copy-start(bf16[4096,128]{1,0:T(8,128)(2,1)} %values_ref.1) | copy-start | bytes 3145732
  39.2 20.8 %all-to-all-start.1 = ((bf16[16,128,256]{2,1,0:T(8,128)(2,1)}), bf16[16,128,256]{2,1,0:T(8,128)(2,1)S(1)}, u32[]{:S(2)}, u32[]{:S(2)}) async-start(bf16[16,128,256]{2,1,0:T(8,128)(2,1)} %get-tuple-element.12), calls=%async_computation.1 | async-start | bytes 2097152 | tf_op jit(solution)/shard_map/all_to_all | solution.py:288
  43.5 3.4 %copy-start = (bf16[4096,1024]{1,0:T(8,128)(2,1)S(1)}, bf16[4096,1024]{1,0:T(8,128)(2,1)}, u32[]{:S(2)}) copy-start(bf16[4096,1024]{1,0:T(8,128)(2,1)} %weight_ref.2) | copy-start | bytes 25165828
  48.3 50.0 %copy-start.3 = (bf16[1024,512]{1,0:T(8,128)(2,1)S(1)}, bf16[1024,512]{1,0:T(8,128)(2,1)}, u32[]{:S(2)}) copy-start(bf16[1024,512]{1,0:T(8,128)(2,1)} %rows_ref.3) | copy-start | bytes 3145732
  48.3 50.0 %copy-start.8 = (s32[16,16]{1,0:T(8,128)S(1)}, s32[16,16]{1,0:T(8,128)}, u32[]{:S(2)}) copy-start(s32[16,16]{1,0:T(8,128)} %tally_ref.5) | copy-start | bytes 3076
  48.3 50.0 %copy-start.10 = (s32[1,256]{1,0:T(1,128)S(1)}, s32[1,256]{1,0:T(1,128)}, u32[]{:S(2)}) copy-start(s32[1,256]{1,0:T(1,128)} %select_ref.3) | copy-start | bytes 3076
  63.4 6.2 %collective-permute-start.12 = (bf16[128,1024]{1,0:T(8,128)(2,1)S(1)}, bf16[128,1024]{1,0:T(8,128)(2,1)S(1)}, u32[]{:S(2)}, u32[]{:S(2)}) collective-permute-start(bf16[128,1024]{1,0:T(8,128)(2,1)S(1)} %attend.1.refs_0_), channel_id=1, source_target_pairs={{0,6},{1,7},{2,0},{3,1},{4,2},{5,3},{6,4},{7,5},{8,14},{9,15},{10,... | collective-permute-start | bytes 786440 | tf_op jit(solution)/shard_map/ppermute | solution.py:220
  64.1 10.3 %collective-permute-start.10 = (bf16[128,1024]{1,0:T(8,128)(2,1)S(1)}, bf16[128,1024]{1,0:T(8,128)(2,1)S(1)}, u32[]{:S(2)}, u32[]{:S(2)}) collective-permute-start(bf16[128,1024]{1,0:T(8,128)(2,1)S(1)} %attend.1.refs_0_), channel_id=1, source_target_pairs={{0,4},{1,5},{2,6},{3,7},{4,0},{5,1},{6,2},{7,3},{8,12},{9,13},{10,... | collective-permute-start | bytes 786440 | tf_op jit(solution)/shard_map/ppermute | solution.py:220
  64.2 15.3 %collective-permute-start.8 = (bf16[128,1024]{1,0:T(8,128)(2,1)S(1)}, bf16[128,1024]{1,0:T(8,128)(2,1)S(1)}, u32[]{:S(2)}, u32[]{:S(2)}) collective-permute-start(bf16[128,1024]{1,0:T(8,128)(2,1)S(1)} %attend.1.refs_0_), channel_id=1, source_target_pairs={{0,2},{1,3},{2,4},{3,5},{4,6},{5,7},{6,0},{7,1},{8,10},{9,11},{10,... | collective-permute-start | bytes 786440 | tf_op jit(solution)/shard_map/ppermute | solution.py:220
  65.0 15.0 %collective-permute-start.7 = (bf16[128,1024]{1,0:T(8,128)(2,1)S(1)}, bf16[128,1024]{1,0:T(8,128)(2,1)S(1)}, u32[]{:S(2)}, u32[]{:S(2)}) collective-permute-start(bf16[128,1024]{1,0:T(8,128)(2,1)S(1)} %attend.1.refs_0_), channel_id=1, source_target_pairs={{0,1},{1,0},{2,3},{3,2},{4,5},{5,4},{6,7},{7,6},{8,9},{9,8},{10,11... | collective-permute-start | bytes 786440 | tf_op jit(solution)/shard_map/ppermute | solution.py:224
  69.6 10.4 %collective-permute-start.13 = (bf16[128,1024]{1,0:T(8,128)(2,1)S(1)}, bf16[128,1024]{1,0:T(8,128)(2,1)S(1)}, u32[]{:S(2)}, u32[]{:S(2)}) collective-permute-start(bf16[128,1024]{1,0:T(8,128)(2,1)S(1)} %collective-permute-done.12.refs_6_), channel_id=1, source_target_pairs={{0,1},{1,0},{2,3},{3,2},{4,5},{5,4},{6,7},{7,6},{8,9},{9,8},{10,11... | collective-permute-start | bytes 786440 | tf_op jit(solution)/shard_map/ppermute | solution.py:224
  74.4 5.6 %collective-permute-start.11 = (bf16[128,1024]{1,0:T(8,128)(2,1)S(1)}, bf16[128,1024]{1,0:T(8,128)(2,1)S(1)}, u32[]{:S(2)}, u32[]{:S(2)}) collective-permute-start(bf16[128,1024]{1,0:T(8,128)(2,1)S(1)} %collective-permute-done.10.refs_4_), channel_id=1, source_target_pairs={{0,1},{1,0},{2,3},{3,2},{4,5},{5,4},{6,7},{7,6},{8,9},{9,8},{10,11... | collective-permute-start | bytes 786440 | tf_op jit(solution)/shard_map/ppermute | solution.py:224
  79.5 1.7 %collective-permute-start.9 = (bf16[128,1024]{1,0:T(8,128)(2,1)S(1)}, bf16[128,1024]{1,0:T(8,128)(2,1)S(1)}, u32[]{:S(2)}, u32[]{:S(2)}) collective-permute-start(bf16[128,1024]{1,0:T(8,128)(2,1)S(1)} %collective-permute-done.8.refs_2_), channel_id=1, source_target_pairs={{0,1},{1,0},{2,3},{3,2},{4,5},{5,4},{6,7},{7,6},{8,9},{9,8},{10,11... | collective-permute-start | bytes 786440 | tf_op jit(solution)/shard_map/ppermute | solution.py:224
  81.1 3.4 %copy-start.1 = (bf16[8192,512]{1,0:T(8,128)(2,1)S(1)}, bf16[8192,512]{1,0:T(8,128)(2,1)}, u32[]{:S(2)}) copy-start(bf16[8192,512]{1,0:T(8,128)(2,1)} %weight_ref.3) | copy-start | bytes 25165828

commit v2 on v1

--- a/solution.py
+++ b/solution.py
@@ -22,6 +22,8 @@
 
 VMEM = pl.BlockSpec(memory_space=pltpu.VMEM)
 SMEM = pl.BlockSpec(memory_space=pltpu.SMEM)
+HBM = pl.BlockSpec(memory_space=pltpu.HBM)
+ANY = pl.BlockSpec(memory_space=pl.ANY)
 F32 = jnp.float32
 BF16 = jnp.bfloat16
 
@@ -41,7 +43,17 @@
     return before // BLOCK, mine
 
 
-def pick_kernel(tally_ref, select_ref, rows_ref, out_ref):
+def pick_kernel(tally_hbm, select_hbm, rows_hbm, out_ref, tally_ref, select_ref, rows_ref, sems):
+    copies = [
+        pltpu.make_async_copy(source, target, sems.at[k])
+        for k, (source, target) in enumerate(
+            ((tally_hbm, tally_ref), (select_hbm, select_ref), (rows_hbm, rows_ref))
+        )
+    ]
+    for copy in copies:
+        copy.start()
+    copies[0].wait()
+    copies[1].wait()
     first, count = own_span(tally_ref[...], lax.axis_index("seq"))
     listed = select_ref[...]
     slot = lax.broadcasted_iota(jnp.int32, (1, SLOTS), 1)
@@ -51,13 +63,48 @@
     hot = jnp.concatenate(
         [(column == lane + float(128 * k)).astype(F32) for k in range(SRC // 128)], axis=1
     ).astype(BF16)
+    copies[2].wait()
     picked = jnp.dot(hot, rows_ref[...], preferred_element_type=F32)
     for j in range(SLOTS // BLOCK):
         owner = lax.rem(first + j, NSEQ)
         out_ref[owner, j // NSEQ] = picked[BLOCK * j : BLOCK * (j + 1)].astype(BF16)
 
 
-def table_kernel(tally_ref, table_ref):
+def load_kernel(count, *refs):
+    sources, targets, done_ref, sems = refs[:count], refs[-2 - count : -2], refs[-2], refs[-1]
+    copies = [pltpu.make_async_copy(a, b, sems.at[k]) for k, (a, b) in enumerate(zip(sources, targets))]
+    for copy in copies:
+        copy.start()
+    for copy in copies:
+        copy.wait()
+    done_ref[...] = jnp.zeros_like(done_ref)
+
+
+def in_hbm(array):
+    return pltpu.with_memory_space_constraint(array, pltpu.HBM)
+
+
+def in_vmem(array):
+    return pltpu.with_memory_space_constraint(array, pltpu.VMEM)
+
+
+def load(arrays, after, name):
+    count = len(arrays)
+    return pl.pallas_call(
+        functools.partial(load_kernel, count),
+        out_shape=[pltpu.VMEM(a.shape, a.dtype) for a in arrays] + [pltpu.VMEM((8, 128), F32)],
+        in_specs=[HBM] * count + [ANY],
+        out_specs=[VMEM] * (count + 1),
+        scratch_shapes=[pltpu.SemaphoreType.DMA((count,))],
+        compiler_params=params(8),
+        cost_estimate=cost(0, sum(a.size for a in arrays) * 2),
+        name=name,
+    )(*map(in_hbm, arrays), after)
+
+
+def prep_kernel(tally_ref, gain_ref, gate_ref, table_ref, gain_out, gate_out):
+    gain_out[...] = gain_ref[...]
+    gate_out[...] = gate_ref[...]
     shard = lax.axis_index("seq")
     starts = []
     start = jnp.int32(0)
@@ -96,8 +143,14 @@
     return chip * 2 + core
 
 
-def pair_kernel(gain_ref, keys_ref, values_ref, *refs):
-    blocks, (normed_ref, pair_ref) = refs[:NMP], refs[NMP:]
+def pair_kernel(gain_ref, keys_hbm, values_hbm, *refs):
+    blocks, (normed_ref, pair_ref, keys_ref, values_ref, sems) = refs[:NMP], refs[NMP:]
+    copies = [
+        pltpu.make_async_copy(keys_hbm, keys_ref, sems.at[0]),
+        pltpu.make_async_copy(values_hbm, values_ref, sems.at[1]),
+    ]
+    for copy in copies:
+        copy.start()
     squares = jnp.zeros((OWNED, 128), F32)
     for k in range(NMP):
         wide = blocks[k][...].astype(F32)
@@ -105,6 +158,8 @@
         for c in range(FEAT // 128):
             squares = squares + square[:, 128 * c : 128 * (c + 1)]
     inverse = lax.rsqrt(jnp.sum(squares, axis=1, keepdims=True) / WIDTH + 1e-05)
+    for copy in copies:
+        copy.wait()
     keys = jnp.zeros((OWNED, HEAD), F32)
     values = jnp.zeros((OWNED, HEAD), F32)
     for k in range(NMP):
@@ -122,14 +177,18 @@
 
 
 def query_kernel(normed_ref, weight_ref, gate_weight_ref, *refs):
-    blocks, (query_ref, gate_ref) = refs[:NMP], refs[NMP:]
+    blocks, (query_ref, gate_ref, held_ref, sems) = refs[:NMP], refs[NMP:]
+    copies = []
+    for k in range(NMP):
+        rows = pl.ds(pl.multiple_of(block_of(k) * FEAT, FEAT), FEAT)
+        copies.append(pltpu.make_async_copy(weight_ref.at[rows, :], held_ref.at[k], sems.at[k]))
+        copies[k].start()
     total = jnp.zeros((OWNED, GROUP * HEAD), F32)
     routed = jnp.zeros((OWNED, FEAT), F32)
     for k in range(NMP):
-        m = block_of(k)
-        rows = pl.ds(pl.multiple_of(m * FEAT, FEAT), FEAT)
-        total = total + jnp.dot(normed_ref[k], weight_ref[rows, :], preferred_element_type=F32)
-        routed = routed + blocks[k][...].astype(F32) * gate_weight_ref[m]
+        routed = routed + blocks[k][...].astype(F32) * gate_weight_ref[block_of(k)]
+        copies[k].wait()
+        total = total + jnp.dot(normed_ref[k], held_ref[k], preferred_element_type=F32)
     query_ref[...] = total.astype(BF16)
     gate_ref[...] = jnp.broadcast_to(
         jax.nn.sigmoid(jnp.sum(routed, axis=1, keepdims=True)), (OWNED, 128)
@@ -224,8 +283,10 @@
     return lax.ppermute(array, "mp", [(m, m ^ 1) for m in range(NMP)])
 
 
-def gather_mp(array):
+def gather_mp(array, before=None):
     chips = {0: array, 1: z_step(array, 1), 3: z_step(array, 3), 2: z_step(array, 2)}
+    if before is not None:
+        chips[3], _ = lax.optimization_barrier((chips[3], before))
     out = []
     for k in range(4):
         out += [chips[k], other_core(chips[k])]
@@ -248,24 +309,36 @@
     selection_table,
     dispatched_tally_table,
 ):
-    gain = prelayer_gain_vector.astype(F32).reshape(NMP, 1, FEAT)
-    gate_weight = gating_projection.astype(F32).reshape(NMP, 1, FEAT)
     outgoing = pl.pallas_call(
         pick_kernel,
-        out_shape=shape((NSEQ, 2, BLOCK, FEAT)),
-        in_specs=[VMEM] * 3,
+        out_shape=pltpu.VMEM((NSEQ, 2, BLOCK, FEAT), BF16),
+        in_specs=[HBM] * 3,
         out_specs=VMEM,
+        scratch_shapes=[
+            pltpu.VMEM((NSEQ, NSEQ), jnp.int32),
+            pltpu.VMEM((1, SLOTS), jnp.int32),
+            pltpu.VMEM((SRC, FEAT), BF16),
+            pltpu.SemaphoreType.DMA((3,)),
+        ],
         compiler_params=params(16),
         name="pick",
-    )(dispatched_tally_table, selection_table, residual_activations)
-    table = pl.pallas_call(
-        table_kernel,
-        out_shape=shape((3, NSEQ), jnp.int32),
-        in_specs=[SMEM],
-        out_specs=SMEM,
+    )(in_hbm(dispatched_tally_table), in_hbm(selection_table), in_hbm(residual_activations))
+    table, gain, gate_weight = pl.pallas_call(
+        prep_kernel,
+        out_shape=(
+            shape((3, NSEQ), jnp.int32),
+            pltpu.VMEM((NMP, 1, FEAT), F32),
+            pltpu.VMEM((NMP, 1, FEAT), F32),
+        ),
+        in_specs=[SMEM, VMEM, VMEM],
+        out_specs=(SMEM, VMEM, VMEM),
         compiler_params=params(4),
-        name="table",
-    )(dispatched_tally_table)
+        name="prep",
+    )(
+        dispatched_tally_table,
+        prelayer_gain_vector.astype(F32).reshape(NMP, 1, FEAT),
+        gating_projection.astype(F32).reshape(NMP, 1, FEAT),
+    )
     incoming = lax.all_to_all(outgoing, "seq", split_axis=0, concat_axis=0, tiled=True)
     tokens = pl.pallas_call(
         compact_kernel,
@@ -278,23 +351,32 @@
     blocks = gather_mp(tokens)
     normed, pair = pl.pallas_call(
         pair_kernel,
-        out_shape=(shape((NMP, OWNED, FEAT)), shape((NSEQ, OWNED, 2 * HEAD))),
-        in_specs=[VMEM] * (3 + NMP),
+        out_shape=(pltpu.VMEM((NMP, OWNED, FEAT), BF16), pltpu.VMEM((NSEQ, OWNED, 2 * HEAD), BF16)),
+        in_specs=[VMEM, HBM, HBM] + [VMEM] * NMP,
         out_specs=(VMEM, VMEM),
+        scratch_shapes=[
+            pltpu.VMEM((WIDTH, HEAD), BF16),
+            pltpu.VMEM((WIDTH, HEAD), BF16),
+            pltpu.SemaphoreType.DMA((2,)),
+        ],
         compiler_params=params(16),
         cost_estimate=cost(2 * OWNED * WIDTH * 2 * HEAD, 4 * MIB),
         name="pair",
-    )(gain, lookup_projection, content_projection, *blocks)
+    )(gain, in_hbm(lookup_projection), in_hbm(content_projection), *blocks)
     pairs = lax.all_to_all(pair, "seq", split_axis=0, concat_axis=0, tiled=True)
     query, gate = pl.pallas_call(
         query_kernel,
         out_shape=(shape((OWNED, GROUP * HEAD)), shape((OWNED, 128), F32)),
-        in_specs=[VMEM] * (3 + NMP),
+        in_specs=[VMEM, HBM, VMEM] + [VMEM] * NMP,
         out_specs=(VMEM, VMEM),
+        scratch_shapes=[
+            pltpu.VMEM((NMP, FEAT, GROUP * HEAD), BF16),
+            pltpu.SemaphoreType.DMA((NMP,)),
+        ],
         compiler_params=params(24),
         cost_estimate=cost(2 * OWNED * WIDTH * GROUP * HEAD, 10 * MIB),
         name="query",
-    )(normed, asker_projection, gate_weight, *blocks)
+    )(normed, in_hbm(asker_projection), gate_weight, *blocks)
     attended = pl.pallas_call(
         attention_kernel,
         out_shape=shape((OWNED, GROUP * HEAD)),
@@ -303,16 +385,17 @@
         compiler_params=params(24),
         name="attend",
     )(logit_sharpness, query, pairs)
-    heads = gather_mp(attended)
+    final, loaded = load((final_projection,), attended, "load")
+    heads = gather_mp(attended, loaded)
     outgoing_back = pl.pallas_call(
         project_kernel,
-        out_shape=shape((NSEQ, 2, BLOCK, FEAT)),
+        out_shape=pltpu.VMEM((NSEQ, 2, BLOCK, FEAT), BF16),
         in_specs=[SMEM] + [VMEM] * (2 + NMP),
         out_specs=VMEM,
         scratch_shapes=[pltpu.VMEM((NSEQ, BLOCK, FEAT), F32)],
         compiler_params=params(24),
         name="project",
-    )(table, gate, final_projection, *heads)
+    )(table, gate, final, *heads)
     back = lax.all_to_all(outgoing_back, "seq", split_axis=0, concat_axis=0, tiled=True)
     return pl.pallas_call(
         blend_kernel,

time: 101 us -> 97.6 us (0.966)
  local copies, waits for them, and re-layouts: 12.5 us -> 0.72 us
  Pallas kernels: 14.2 us -> 23 us
    unnamed x24 -> x10, local copies, waits for them, and re-layouts: 12.5 us -> 0.72 us
    pallas_call x4 -> x5, Pallas kernels: 7.18 us -> 13.5 us  [the longest x1 3.98 us: load(): pl.pallas_call(functools.partial(load_kernel, count), out_shape=[pltpu.VM...]
    pallas_call x1, Pallas kernels: 1.35 us -> 3.82 us  [on_device(): pl.pallas_call(query_kernel, out_shape=(shape((OWNED, GROUP * HEAD)), sha...]
    all_to_all x1, waiting for transfers between devices: 11.6 us -> 13.3 us  [on_device(): pairs = lax.all_to_all(pair, 'seq', split_axis=0, concat_axis=0, tiled=True)]
    all_to_all x1, waiting for transfers between devices: 5.01 us -> 3.6 us  [on_device(): lax.all_to_all(outgoing, 'seq', split_axis=0, concat_axis=0, tiled=True)]
  transfers between devices with their start and end apart: 16 -> 16, of which waited for: 6 -> 5; matrix products, arithmetic and copies ran while one was open for 1% -> 1% of each run, Pallas kernels for 3% -> 10%
where the time goes in v2:
time: 97.6 us; the launch traced here: 97.1 us
  starting transfers between devices  36.8 us (38%)
  Pallas kernels  23 us (24%)
  waiting for transfers between devices  22.7 us (23%)
  blocking collectives  12.3 us (13%)
  other arithmetic  1.4 us (1%)
    ppermute x8, starting transfers between devices, other_core(): return lax.ppermute(array, 'mp', [(m, m ^ 1) for m in range(NMP)])  19.4 us
    all_to_all x1, waiting for transfers between devices, on_device(): pairs = lax.all_to_all(pair, 'seq', split_axis=0, concat_axis=0, tiled=True)  13.3 us
    all_to_all x1, blocking collectives, on_device(): lax.all_to_all(outgoing_back, 'seq', split_axis=0, concat_axis=0, tiled=T...  12.3 us
    all_to_all x1, starting transfers between devices, on_device(): lax.all_to_all(outgoing, 'seq', split_axis=0, concat_axis=0, tiled=True)  7.6 us
    ppermute x6, starting transfers between devices, z_step(): return lax.ppermute(array, 'mp', pairs)  6.1 us
    ppermute x6, waiting for transfers between devices, z_step(): return lax.ppermute(array, 'mp', pairs)  4.79 us
    pallas_call x1, Pallas kernels, load(): pl.pallas_call(functools.partial(load_kernel, count), out_shape=[pltpu.VM...  3.98 us
    pallas_call x1, Pallas kernels, on_device(): pl.pallas_call(query_kernel, out_shape=(shape((OWNED, GROUP * HEAD)), sha...  3.82 us
  transfers between devices with their start and end apart: 16, of which 5 were waited for; matrix products, arithmetic and copies ran while one was open for 1% of the time, Pallas kernels for 10%

profile of v2, /device:TPU:1, one launch (start us, length us, event | category | flops | bytes accessed | tf_op | source)
XLA Modules:
  0.0 97.1 jit_solution(17007926489106295006)
XLA Ops:
  0.0 2.4 %pick.1 = bf16[16,2,8,512]{3,2,1,0:T(8,128)(2,1)} custom-call(s32[16,16]{1,0:T(8,128)} %tally_ref.3, s32[1,256]{1,0:T(1,128)} %select_ref.1, bf16[1024,512]{1,0:T(8,128)(2,1)} %rows_ref.1), custom_call_target="tpu_custom_call" | custom-call | tf_op jit(solution)/shard_map/pick/pallas_call | solution.py:312
  2.4 0.0 copy-start.4
  2.4 7.6 %all-to-all-start = ((bf16[16,2,8,512]{3,2,1,0:T(8,128)(2,1)}), bf16[16,2,8,512]{3,2,1,0:T(8,128)(2,1)S(1)}, u32[]{:S(2)}, u32[]{:S(2)}) async-start(bf16[16,2,8,512]{3,2,1,0:T(8,128)(2,1)} %pick.1), calls=%async_computation | async-start | bytes 524288 | tf_op jit(solution)/shard_map/all_to_all | solution.py:342
  10.0 0.7 reshape.14
  10.8 0.7 reshape.16
  11.5 0.7 copy-done.1
  12.1 1.8 %prep.1 = (s32[3,16]{1,0:T(4,128)S(1)}, f32[8,1,512]{2,1,0:T(1,128)S(1)}, f32[8,1,512]{2,1,0:T(1,128)S(1)}) custom-call(s32[16,16]{1,0:T(8,128)S(1)} %copy-done.1, f32[8,1,512]{2,1,0:T(1,128)S(1)} %bitcast.2, f32[8,1,512]{2,1,0:T(1,128)S(1)} %bitcast.3), custom_call_target="tpu_custom_call" | custom-call | tf_op jit(solution)/shard_map/prep/pallas_call | solution.py:326
  14.0 3.6 %all-to-all-done.in_ref = bf16[16,2,8,512]{3,2,1,0:T(8,128)(2,1)S(1)} async-done(((bf16[16,2,8,512]{3,2,1,0:T(8,128)(2,1)}), bf16[16,2,8,512]{3,2,1,0:T(8,128)(2,1)S(1)}, u32[]{:S(2)}, u32[]{:S(2)}) %all-to-all-start) | async-done | bytes 262176 | tf_op jit(solution)/shard_map/all_to_all | solution.py:342
  17.6 0.6 compact.1.refs_0_
  18.2 3.8 %collective-permute-start.5 = (bf16[128,512]{1,0:T(8,128)(2,1)S(1)}, bf16[128,512]{1,0:T(8,128)(2,1)S(1)}, u32[]{:S(2)}, u32[]{:S(2)}) collective-permute-start(bf16[128,512]{1,0:T(8,128)(2,1)S(1)} %compact.1.refs_0_), channel_id=1, source_target_pairs={{0,6},{1,7},{2,0},{3,1},{4,2},{5,3},{6,4},{7,5},{8,14},{9,15},{10,... | collective-permute-start | bytes 393224 | tf_op jit(solution)/shard_map/ppermute | solution.py:279
  22.0 0.0 collective-permute-start.3
  22.0 0.7 collective-permute-start.1
  22.7 2.9 %collective-permute-start = (bf16[128,512]{1,0:T(8,128)(2,1)S(1)}, bf16[128,512]{1,0:T(8,128)(2,1)S(1)}, u32[]{:S(2)}, u32[]{:S(2)}) collective-permute-start(bf16[128,512]{1,0:T(8,128)(2,1)S(1)} %compact.1.refs_0_), channel_id=1, source_target_pairs={{0,1},{1,0},{2,3},{3,2},{4,5},{5,4},{6,7},{7,6},{8,9},{9,8},{10,11... | collective-permute-start | bytes 393224 | tf_op jit(solution)/shard_map/ppermute | solution.py:283
  25.7 0.0 collective-permute-done.5.refs_6_
  25.7 2.9 %collective-permute-start.6 = (bf16[128,512]{1,0:T(8,128)(2,1)S(1)}, bf16[128,512]{1,0:T(8,128)(2,1)S(1)}, u32[]{:S(2)}, u32[]{:S(2)}) collective-permute-start(bf16[128,512]{1,0:T(8,128)(2,1)S(1)} %collective-permute-done.5.refs_6_), channel_id=1, source_target_pairs={{0,1},{1,0},{2,3},{3,2},{4,5},{5,4},{6,7},{7,6},{8,9},{9,8},{10,11... | collective-permute-start | bytes 393224 | tf_op jit(solution)/shard_map/ppermute | solution.py:283
  28.6 0.0 collective-permute-done.3.refs_4_
  28.6 2.4 %collective-permute-start.4 = (bf16[128,512]{1,0:T(8,128)(2,1)S(1)}, bf16[128,512]{1,0:T(8,128)(2,1)S(1)}, u32[]{:S(2)}, u32[]{:S(2)}) collective-permute-start(bf16[128,512]{1,0:T(8,128)(2,1)S(1)} %collective-permute-done.3.refs_4_), channel_id=1, source_target_pairs={{0,1},{1,0},{2,3},{3,2},{4,5},{5,4},{6,7},{7,6},{8,9},{9,8},{10,11... | collective-permute-start | bytes 393224 | tf_op jit(solution)/shard_map/ppermute | solution.py:283
  31.0 0.0 collective-permute-done.1.refs_2_
  31.0 1.0 %collective-permute-start.2 = (bf16[128,512]{1,0:T(8,128)(2,1)S(1)}, bf16[128,512]{1,0:T(8,128)(2,1)S(1)}, u32[]{:S(2)}, u32[]{:S(2)}) collective-permute-start(bf16[128,512]{1,0:T(8,128)(2,1)S(1)} %collective-permute-done.1.refs_2_), channel_id=1, source_target_pairs={{0,1},{1,0},{2,3},{3,2},{4,5},{5,4},{6,7},{7,6},{8,9},{9,8},{10,11... | collective-permute-start | bytes 393224 | tf_op jit(solution)/shard_map/ppermute | solution.py:283
  32.0 0.0 collective-permute-done.refs_1_
  32.0 0.0 collective-permute-done.6.refs_7_
  32.0 0.0 collective-permute-done.4.refs_5_
  32.0 1.0 %collective-permute-done.2.refs_3_ = bf16[128,512]{1,0:T(8,128)(2,1)S(1)} collective-permute-done((bf16[128,512]{1,0:T(8,128)(2,1)S(1)}, bf16[128,512]{1,0:T(8,128)(2,1)S(1)}, u32[]{:S(2)}, u32[]{:S(2)}) %collective-permute-start.2) | collective-permute-done | bytes 131104 | tf_op jit(solution)/shard_map/ppermute | solution.py:283
  33.0 3.4 %pair.1 = (bf16[8,128,512]{2,1,0:T(8,128)(2,1)S(1)}, bf16[16,128,256]{2,1,0:T(8,128)(2,1)}) custom-call(f32[8,1,512]{2,1,0:T(1,128)S(1)} %get-tuple-element.14.gain_ref, bf16[4096,128]{1,0:T(8,128)(2,1)} %keys_hbm.1, bf16[4096,128]{1,0:T(8,128)(2,1)} %values_hbm.1, bf16[128,512]{1,0:T(8,128)(2,1)S(1)} %compact.1.refs_0_, ...), custom_call_target="tpu_custom_call" | custom-call | flops 268435456 | bytes 4194304 | tf_op jit(solution)/shard_map/pair/pallas_call | solution.py:352
  36.4 3.7 %all-to-all-start.1 = ((bf16[16,128,256]{2,1,0:T(8,128)(2,1)}), bf16[16,128,256]{2,1,0:T(8,128)(2,1)S(1)}, u32[]{:S(2)}, u32[]{:S(2)}) async-start(bf16[16,128,256]{2,1,0:T(8,128)(2,1)} %get-tuple-element.19), calls=%async_computation.1 | async-start | bytes 2097152 | tf_op jit(solution)/shard_map/all_to_all | solution.py:366
  40.1 3.8 %query.1 = (bf16[128,1024]{1,0:T(8,128)(2,1)S(1)}, f32[128,128]{1,0:T(8,128)S(1)}) custom-call(bf16[8,128,512]{2,1,0:T(8,128)(2,1)S(1)} %get-tuple-element.15.normed_ref, bf16[4096,1024]{1,0:T(8,128)(2,1)} %weight_ref.1, f32[8,1,512]{2,1,0:T(1,128)S(1)} %get-tuple-element.16.gate_weight_ref, bf16[128,512]{1,0:T(8,128)(2,1)S(1)} %compact.1.refs_0_, ...), custom_call_target="tpu_custom_call" | custom-call | flops 1073741824 | bytes 10485760 | tf_op jit(solution)/shard_map/query/pallas_call | solution.py:367
  43.9 13.3 %all-to-all-done.1.pair_ref = bf16[16,128,256]{2,1,0:T(8,128)(2,1)S(1)} async-done(((bf16[16,128,256]{2,1,0:T(8,128)(2,1)}), bf16[16,128,256]{2,1,0:T(8,128)(2,1)S(1)}, u32[]{:S(2)}, u32[]{:S(2)}) %all-to-all-start.1) | async-done | bytes 1048608 | tf_op jit(solution)/shard_map/all_to_all | solution.py:366
  57.2 3.4 %attend.1.refs_1_.refs_0_ = bf16[128,1024]{1,0:T(8,128)(2,1)S(1)} custom-call(f32[8]{0:T(128)S(1)} %copy-done.4, bf16[128,1024]{1,0:T(8,128)(2,1)S(1)} %get-tuple-element.18.query_ref, bf16[16,128,256]{2,1,0:T(8,128)(2,1)S(1)} %all-to-all-done.1.pair_ref), custom_call_target="tpu_custom_call" | custom-call | tf_op jit(solution)/shard_map/attend/pallas_call | solution.py:380
  60.6 0.0 copy-start
  60.6 0.0 copy-start.2
  60.7 0.0 copy-start.3
  60.7 0.7 collective-permute-start.12
  61.4 0.1 collective-permute-start.10
  61.5 0.8 collective-permute-start.8
  62.2 2.5 %collective-permute-start.7 = (bf16[128,1024]{1,0:T(8,128)(2,1)S(1)}, bf16[128,1024]{1,0:T(8,128)(2,1)S(1)}, u32[]{:S(2)}, u32[]{:S(2)}) collective-permute-start(bf16[128,1024]{1,0:T(8,128)(2,1)S(1)} %attend.1.refs_1_.refs_0_), channel_id=1, source_target_pairs={{0,1},{1,0},{2,3},{3,2},{4,5},{5,4},{6,7},{7,6},{8,9},{9,8},{10,11... | collective-permute-start | bytes 786440 | tf_op jit(solution)/shard_map/ppermute | solution.py:283
  64.7 2.1 %collective-permute-done.12.refs_6_ = bf16[128,1024]{1,0:T(8,128)(2,1)S(1)} collective-permute-done((bf16[128,1024]{1,0:T(8,128)(2,1)S(1)}, bf16[128,1024]{1,0:T(8,128)(2,1)S(1)}, u32[]{:S(2)}, u32[]{:S(2)}) %collective-permute-start.12) | collective-permute-done | bytes 262176 | tf_op jit(solution)/shard_map/ppermute | solution.py:279
  66.9 4.8 %collective-permute-start.13 = (bf16[128,1024]{1,0:T(8,128)(2,1)S(1)}, bf16[128,1024]{1,0:T(8,128)(2,1)S(1)}, u32[]{:S(2)}, u32[]{:S(2)}) collective-permute-start(bf16[128,1024]{1,0:T(8,128)(2,1)S(1)} %collective-permute-done.12.refs_6_), channel_id=1, source_target_pairs={{0,1},{1,0},{2,3},{3,2},{4,5},{5,4},{6,7},{7,6},{8,9},{9,8},{10,11... | collective-permute-start | bytes 786440 | tf_op jit(solution)/shard_map/ppermute | solution.py:283
  71.6 0.0 collective-permute-done.10.refs_4_
  71.7 2.4 %collective-permute-start.11 = (bf16[128,1024]{1,0:T(8,128)(2,1)S(1)}, bf16[128,1024]{1,0:T(8,128)(2,1)S(1)}, u32[]{:S(2)}, u32[]{:S(2)}) collective-permute-start(bf16[128,1024]{1,0:T(8,128)(2,1)S(1)} %collective-permute-done.10.refs_4_), channel_id=1, source_target_pairs={{0,1},{1,0},{2,3},{3,2},{4,5},{5,4},{6,7},{7,6},{8,9},{9,8},{10,11... | collective-permute-start | bytes 786440 | tf_op jit(solution)/shard_map/ppermute | solution.py:283
  74.1 2.7 %collective-permute-done.8.refs_2_ = bf16[128,1024]{1,0:T(8,128)(2,1)S(1)} collective-permute-done((bf16[128,1024]{1,0:T(8,128)(2,1)S(1)}, bf16[128,1024]{1,0:T(8,128)(2,1)S(1)}, u32[]{:S(2)}, u32[]{:S(2)}) %collective-permute-start.8) | collective-permute-done | bytes 262176 | tf_op jit(solution)/shard_map/ppermute | solution.py:279
  76.7 0.5 collective-permute-start.9
  77.2 4.0 %load.1 = (bf16[8192,512]{1,0:T(8,128)(2,1)S(1)}, f32[8,128]{1,0:T(8,128)}) custom-call(bf16[8192,512]{1,0:T(8,128)(2,1)} %refs_0_.1, bf16[128,1024]{1,0:T(8,128)(2,1)S(1)} %attend.1.refs_1_.refs_0_), custom_call_target="tpu_custom_call" | custom-call | bytes 8388608 | tf_op jit(solution)/shard_map/load/pallas_call | solution.py:93
  81.2 0.0 collective-permute-done.7.refs_1_
  81.2 0.0 collective-permute-done.13.refs_7_
  81.2 0.0 collective-permute-done.9.refs_3_
  81.2 1.9 %project.1 = bf16[16,2,8,512]{3,2,1,0:T(8,128)(2,1)S(1)} custom-call(s32[3,16]{1,0:T(4,128)S(1)} %get-tuple-element.13.table_ref, f32[128,128]{1,0:T(8,128)S(1)} %get-tuple-element.17.gate_ref, bf16[8192,512]{1,0:T(8,128)(2,1)S(1)} %get-tuple-element.20.weight_ref, bf16[128,1024]{1,0:T(8,128)(2,1)S(1)} %attend.1.refs_1_.refs_0_, ...), custom_call_target="tpu_custom_call" | custom-call | tf_op jit(solution)/shard_map/project/pallas_call | solution.py:390
  83.1 12.3 %all_to_all.15.back_ref = bf16[16,2,8,512]{3,2,1,0:T(8,128)(2,1)S(1)} all-to-all(bf16[16,2,8,512]{3,2,1,0:T(8,128)(2,1)S(1)} %project.1), channel_id=1, replica_groups=mesh['seq'=16,'mp'=8] {'seq'}, dimensions={0} | all-to-all | bytes 524288 | tf_op jit(solution)/shard_map/all_to_all | solution.py:399
  95.5 1.6 %blend.1 = bf16[1024,512]{1,0:T(8,128)(2,1)} custom-call(s32[16,16]{1,0:T(8,128)S(1)} %copy-done.2, s32[1,256]{1,0:T(1,128)S(1)} %copy-done.3, bf16[1024,512]{1,0:T(8,128)(2,1)S(1)} %copy-done, bf16[16,2,8,512]{3,2,1,0:T(8,128)(2,1)S(1)} %all_to_all.15.back_ref), custom_call_target="tpu_custom_call" | custom-call | tf_op jit(solution)/shard_map/blend/pallas_call | solution.py:400
  (6 shorter events, 0.0 us)
Async XLA Ops:
  2.4 54.7 %copy-start.4 = (f32[8]{0:T(128)S(1)}, f32[8]{0:T(128)}, u32[]{:S(2)}) copy-start(f32[8]{0:T(128)} %sharp_ref.1) | copy-start | bytes 100
  2.4 15.1 %all-to-all-start = ((bf16[16,2,8,512]{3,2,1,0:T(8,128)(2,1)}), bf16[16,2,8,512]{3,2,1,0:T(8,128)(2,1)S(1)}, u32[]{:S(2)}, u32[]{:S(2)}) async-start(bf16[16,2,8,512]{3,2,1,0:T(8,128)(2,1)} %pick.1), calls=%async_computation | async-start | bytes 524288 | tf_op jit(solution)/shard_map/all_to_all | solution.py:342
  11.4 0.7 copy-start.1
  18.2 7.5 %collective-permute-start.5 = (bf16[128,512]{1,0:T(8,128)(2,1)S(1)}, bf16[128,512]{1,0:T(8,128)(2,1)S(1)}, u32[]{:S(2)}, u32[]{:S(2)}) collective-permute-start(bf16[128,512]{1,0:T(8,128)(2,1)S(1)} %compact.1.refs_0_), channel_id=1, source_target_pairs={{0,6},{1,7},{2,0},{3,1},{4,2},{5,3},{6,4},{7,5},{8,14},{9,15},{10,... | collective-permute-start | bytes 393224 | tf_op jit(solution)/shard_map/ppermute | solution.py:279
  22.0 6.6 %collective-permute-start.3 = (bf16[128,512]{1,0:T(8,128)(2,1)S(1)}, bf16[128,512]{1,0:T(8,128)(2,1)S(1)}, u32[]{:S(2)}, u32[]{:S(2)}) collective-permute-start(bf16[128,512]{1,0:T(8,128)(2,1)S(1)} %compact.1.refs_0_), channel_id=1, source_target_pairs={{0,4},{1,5},{2,6},{3,7},{4,0},{5,1},{6,2},{7,3},{8,12},{9,13},{10,... | collective-permute-start | bytes 393224 | tf_op jit(solution)/shard_map/ppermute | solution.py:279
  22.0 9.0 %collective-permute-start.1 = (bf16[128,512]{1,0:T(8,128)(2,1)S(1)}, bf16[128,512]{1,0:T(8,128)(2,1)S(1)}, u32[]{:S(2)}, u32[]{:S(2)}) collective-permute-start(bf16[128,512]{1,0:T(8,128)(2,1)S(1)} %compact.1.refs_0_), channel_id=1, source_target_pairs={{0,2},{1,3},{2,4},{3,5},{4,6},{5,7},{6,0},{7,1},{8,10},{9,11},{10,... | collective-permute-start | bytes 393224 | tf_op jit(solution)/shard_map/ppermute | solution.py:279
  22.7 9.3 %collective-permute-start = (bf16[128,512]{1,0:T(8,128)(2,1)S(1)}, bf16[128,512]{1,0:T(8,128)(2,1)S(1)}, u32[]{:S(2)}, u32[]{:S(2)}) collective-permute-start(bf16[128,512]{1,0:T(8,128)(2,1)S(1)} %compact.1.refs_0_), channel_id=1, source_target_pairs={{0,1},{1,0},{2,3},{3,2},{4,5},{5,4},{6,7},{7,6},{8,9},{9,8},{10,11... | collective-permute-start | bytes 393224 | tf_op jit(solution)/shard_map/ppermute | solution.py:283
  25.7 6.3 %collective-permute-start.6 = (bf16[128,512]{1,0:T(8,128)(2,1)S(1)}, bf16[128,512]{1,0:T(8,128)(2,1)S(1)}, u32[]{:S(2)}, u32[]{:S(2)}) collective-permute-start(bf16[128,512]{1,0:T(8,128)(2,1)S(1)} %collective-permute-done.5.refs_6_), channel_id=1, source_target_pairs={{0,1},{1,0},{2,3},{3,2},{4,5},{5,4},{6,7},{7,6},{8,9},{9,8},{10,11... | collective-permute-start | bytes 393224 | tf_op jit(solution)/shard_map/ppermute | solution.py:283
  28.6 3.4 %collective-permute-start.4 = (bf16[128,512]{1,0:T(8,128)(2,1)S(1)}, bf16[128,512]{1,0:T(8,128)(2,1)S(1)}, u32[]{:S(2)}, u32[]{:S(2)}) collective-permute-start(bf16[128,512]{1,0:T(8,128)(2,1)S(1)} %collective-permute-done.3.refs_4_), channel_id=1, source_target_pairs={{0,1},{1,0},{2,3},{3,2},{4,5},{5,4},{6,7},{7,6},{8,9},{9,8},{10,11... | collective-permute-start | bytes 393224 | tf_op jit(solution)/shard_map/ppermute | solution.py:283
  31.0 2.0 %collective-permute-start.2 = (bf16[128,512]{1,0:T(8,128)(2,1)S(1)}, bf16[128,512]{1,0:T(8,128)(2,1)S(1)}, u32[]{:S(2)}, u32[]{:S(2)}) collective-permute-start(bf16[128,512]{1,0:T(8,128)(2,1)S(1)} %collective-permute-done.1.refs_2_), channel_id=1, source_target_pairs={{0,1},{1,0},{2,3},{3,2},{4,5},{5,4},{6,7},{7,6},{8,9},{9,8},{10,11... | collective-permute-start | bytes 393224 | tf_op jit(solution)/shard_map/ppermute | solution.py:283
  36.4 20.8 %all-to-all-start.1 = ((bf16[16,128,256]{2,1,0:T(8,128)(2,1)}), bf16[16,128,256]{2,1,0:T(8,128)(2,1)S(1)}, u32[]{:S(2)}, u32[]{:S(2)}) async-start(bf16[16,128,256]{2,1,0:T(8,128)(2,1)} %get-tuple-element.19), calls=%async_computation.1 | async-start | bytes 2097152 | tf_op jit(solution)/shard_map/all_to_all | solution.py:366
  60.6 34.8 %copy-start = (bf16[1024,512]{1,0:T(8,128)(2,1)S(1)}, bf16[1024,512]{1,0:T(8,128)(2,1)}, u32[]{:S(2)}) copy-start(bf16[1024,512]{1,0:T(8,128)(2,1)} %rows_ref.1) | copy-start | bytes 3145732
  60.6 34.8 %copy-start.2 = (s32[16,16]{1,0:T(8,128)S(1)}, s32[16,16]{1,0:T(8,128)}, u32[]{:S(2)}) copy-start(s32[16,16]{1,0:T(8,128)} %tally_ref.3) | copy-start | bytes 3076
  60.7 34.8 %copy-start.3 = (s32[1,256]{1,0:T(1,128)S(1)}, s32[1,256]{1,0:T(1,128)}, u32[]{:S(2)}) copy-start(s32[1,256]{1,0:T(1,128)} %select_ref.1) | copy-start | bytes 3076
  60.7 6.2 %collective-permute-start.12 = (bf16[128,1024]{1,0:T(8,128)(2,1)S(1)}, bf16[128,1024]{1,0:T(8,128)(2,1)S(1)}, u32[]{:S(2)}, u32[]{:S(2)}) collective-permute-start(bf16[128,1024]{1,0:T(8,128)(2,1)S(1)} %attend.1.refs_1_.refs_0_), channel_id=1, source_target_pairs={{0,6},{1,7},{2,0},{3,1},{4,2},{5,3},{6,4},{7,5},{8,14},{9,15},{10,... | collective-permute-start | bytes 786440 | tf_op jit(solution)/shard_map/ppermute | solution.py:279
  61.4 10.3 %collective-permute-start.10 = (bf16[128,1024]{1,0:T(8,128)(2,1)S(1)}, bf16[128,1024]{1,0:T(8,128)(2,1)S(1)}, u32[]{:S(2)}, u32[]{:S(2)}) collective-permute-start(bf16[128,1024]{1,0:T(8,128)(2,1)S(1)} %attend.1.refs_1_.refs_0_), channel_id=1, source_target_pairs={{0,4},{1,5},{2,6},{3,7},{4,0},{5,1},{6,2},{7,3},{8,12},{9,13},{10,... | collective-permute-start | bytes 786440 | tf_op jit(solution)/shard_map/ppermute | solution.py:279
  61.5 15.2 %collective-permute-start.8 = (bf16[128,1024]{1,0:T(8,128)(2,1)S(1)}, bf16[128,1024]{1,0:T(8,128)(2,1)S(1)}, u32[]{:S(2)}, u32[]{:S(2)}) collective-permute-start(bf16[128,1024]{1,0:T(8,128)(2,1)S(1)} %attend.1.refs_1_.refs_0_), channel_id=1, source_target_pairs={{0,2},{1,3},{2,4},{3,5},{4,6},{5,7},{6,0},{7,1},{8,10},{9,11},{10,... | collective-permute-start | bytes 786440 | tf_op jit(solution)/shard_map/ppermute | solution.py:279
  62.2 19.0 %collective-permute-start.7 = (bf16[128,1024]{1,0:T(8,128)(2,1)S(1)}, bf16[128,1024]{1,0:T(8,128)(2,1)S(1)}, u32[]{:S(2)}, u32[]{:S(2)}) collective-permute-start(bf16[128,1024]{1,0:T(8,128)(2,1)S(1)} %attend.1.refs_1_.refs_0_), channel_id=1, source_target_pairs={{0,1},{1,0},{2,3},{3,2},{4,5},{5,4},{6,7},{7,6},{8,9},{9,8},{10,11... | collective-permute-start | bytes 786440 | tf_op jit(solution)/shard_map/ppermute | solution.py:283
  66.9 14.3 %collective-permute-start.13 = (bf16[128,1024]{1,0:T(8,128)(2,1)S(1)}, bf16[128,1024]{1,0:T(8,128)(2,1)S(1)}, u32[]{:S(2)}, u32[]{:S(2)}) collective-permute-start(bf16[128,1024]{1,0:T(8,128)(2,1)S(1)} %collective-permute-done.12.refs_6_), channel_id=1, source_target_pairs={{0,1},{1,0},{2,3},{3,2},{4,5},{5,4},{6,7},{7,6},{8,9},{9,8},{10,11... | collective-permute-start | bytes 786440 | tf_op jit(solution)/shard_map/ppermute | solution.py:283
  71.7 9.6 %collective-permute-start.11 = (bf16[128,1024]{1,0:T(8,128)(2,1)S(1)}, bf16[128,1024]{1,0:T(8,128)(2,1)S(1)}, u32[]{:S(2)}, u32[]{:S(2)}) collective-permute-start(bf16[128,1024]{1,0:T(8,128)(2,1)S(1)} %collective-permute-done.10.refs_4_), channel_id=1, source_target_pairs={{0,1},{1,0},{2,3},{3,2},{4,5},{5,4},{6,7},{7,6},{8,9},{9,8},{10,11... | collective-permute-start | bytes 786440 | tf_op jit(solution)/shard_map/ppermute | solution.py:283
  76.7 4.5 %collective-permute-start.9 = (bf16[128,1024]{1,0:T(8,128)(2,1)S(1)}, bf16[128,1024]{1,0:T(8,128)(2,1)S(1)}, u32[]{:S(2)}, u32[]{:S(2)}) collective-permute-start(bf16[128,1024]{1,0:T(8,128)(2,1)S(1)} %collective-permute-done.8.refs_2_), channel_id=1, source_target_pairs={{0,1},{1,0},{2,3},{3,2},{4,5},{5,4},{6,7},{7,6},{8,9},{9,8},{10,11... | collective-permute-start | bytes 786440 | tf_op jit(solution)/shard_map/ppermute | solution.py:283

commit v3 on v2

--- a/solution.py
+++ b/solution.py
@@ -143,56 +143,37 @@
     return chip * 2 + core
 
 
-def pair_kernel(gain_ref, keys_hbm, values_hbm, *refs):
-    blocks, (normed_ref, pair_ref, keys_ref, values_ref, sems) = refs[:NMP], refs[NMP:]
-    copies = [
-        pltpu.make_async_copy(keys_hbm, keys_ref, sems.at[0]),
-        pltpu.make_async_copy(values_hbm, values_ref, sems.at[1]),
-    ]
-    for copy in copies:
-        copy.start()
+def project_in_kernel(gain_ref, gate_weight_ref, query_weight_ref, keys_ref, values_ref, *refs):
+    blocks, (query_ref, gate_ref, pair_ref) = refs[:NMP], refs[NMP:]
     squares = jnp.zeros((OWNED, 128), F32)
+    routed = jnp.zeros((OWNED, 128), F32)
     for k in range(NMP):
         wide = blocks[k][...].astype(F32)
         square = wide * wide
+        weighted = wide * gate_weight_ref[block_of(k)]
         for c in range(FEAT // 128):
             squares = squares + square[:, 128 * c : 128 * (c + 1)]
+            routed = routed + weighted[:, 128 * c : 128 * (c + 1)]
     inverse = lax.rsqrt(jnp.sum(squares, axis=1, keepdims=True) / WIDTH + 1e-05)
-    for copy in copies:
-        copy.wait()
+    gate_ref[...] = jnp.broadcast_to(
+        jax.nn.sigmoid(jnp.sum(routed, axis=1, keepdims=True)), (OWNED, 128)
+    )
+    query = jnp.zeros((OWNED, GROUP * HEAD), F32)
     keys = jnp.zeros((OWNED, HEAD), F32)
     values = jnp.zeros((OWNED, HEAD), F32)
     for k in range(NMP):
         m = block_of(k)
         rows = pl.ds(pl.multiple_of(m * FEAT, FEAT), FEAT)
         normed = (blocks[k][...].astype(F32) * inverse * gain_ref[m]).astype(BF16)
-        normed_ref[k] = normed
         keys = keys + jnp.dot(normed, keys_ref[rows, :], preferred_element_type=F32)
         values = values + jnp.dot(normed, values_ref[rows, :], preferred_element_type=F32)
+        query = query + jnp.dot(normed, query_weight_ref[rows, :], preferred_element_type=F32)
+    query_ref[...] = query.astype(BF16)
     keys = keys.astype(BF16)
     values = values.astype(BF16)
     for d in range(NSEQ):
         pair_ref[d, :, :HEAD] = keys
         pair_ref[d, :, HEAD:] = values
-
-
-def query_kernel(normed_ref, weight_ref, gate_weight_ref, *refs):
-    blocks, (query_ref, gate_ref, held_ref, sems) = refs[:NMP], refs[NMP:]
-    copies = []
-    for k in range(NMP):
-        rows = pl.ds(pl.multiple_of(block_of(k) * FEAT, FEAT), FEAT)
-        copies.append(pltpu.make_async_copy(weight_ref.at[rows, :], held_ref.at[k], sems.at[k]))
-        copies[k].start()
-    total = jnp.zeros((OWNED, GROUP * HEAD), F32)
-    routed = jnp.zeros((OWNED, FEAT), F32)
-    for k in range(NMP):
-        routed = routed + blocks[k][...].astype(F32) * gate_weight_ref[block_of(k)]
-        copies[k].wait()
-        total = total + jnp.dot(normed_ref[k], held_ref[k], preferred_element_type=F32)
-    query_ref[...] = total.astype(BF16)
-    gate_ref[...] = jnp.broadcast_to(
-        jax.nn.sigmoid(jnp.sum(routed, axis=1, keepdims=True)), (OWNED, 128)
-    )
 
 
 def attention_kernel(sharp_ref, query_ref, pair_ref, out_ref):
@@ -283,14 +264,27 @@
     return lax.ppermute(array, "mp", [(m, m ^ 1) for m in range(NMP)])
 
 
-def gather_mp(array, before=None):
+def hand_on_kernel(in_ref, token_ref, out_ref):
+    out_ref[...] = in_ref[...]
+
+
+def hand_on(array, token):
+    return pl.pallas_call(
+        hand_on_kernel,
+        out_shape=pltpu.VMEM(array.shape, array.dtype),
+        in_specs=[VMEM, ANY],
+        out_specs=VMEM,
+        compiler_params=params(4),
+        name="hand_on",
+    )(array, token)
+
+
+def gather_mp(array, token):
     chips = {0: array, 1: z_step(array, 1), 3: z_step(array, 3), 2: z_step(array, 2)}
-    if before is not None:
-        chips[3], _ = lax.optimization_barrier((chips[3], before))
-    out = []
-    for k in range(4):
-        out += [chips[k], other_core(chips[k])]
-    return out
+    other = {0: other_core(array)}
+    for k in (3, 1, 2):
+        other[k] = other_core(hand_on(chips[k], token) if k == 3 else chips[k])
+    return [part[k] for k in range(4) for part in (chips, other)]
 
 
 def shape(dims, dtype=BF16):
@@ -348,35 +342,24 @@
         compiler_params=params(4),
         name="compact",
     )(table, incoming)
-    blocks = gather_mp(tokens)
-    normed, pair = pl.pallas_call(
-        pair_kernel,
-        out_shape=(pltpu.VMEM((NMP, OWNED, FEAT), BF16), pltpu.VMEM((NSEQ, OWNED, 2 * HEAD), BF16)),
-        in_specs=[VMEM, HBM, HBM] + [VMEM] * NMP,
-        out_specs=(VMEM, VMEM),
-        scratch_shapes=[
-            pltpu.VMEM((WIDTH, HEAD), BF16),
-            pltpu.VMEM((WIDTH, HEAD), BF16),
-            pltpu.SemaphoreType.DMA((2,)),
-        ],
+    asker, lookup, content, loaded = load(
+        (asker_projection, lookup_projection, content_projection), tokens, "load_in"
+    )
+    blocks = gather_mp(tokens, loaded)
+    query, gate, pair = pl.pallas_call(
+        project_in_kernel,
+        out_shape=(
+            pltpu.VMEM((OWNED, GROUP * HEAD), BF16),
+            pltpu.VMEM((OWNED, 128), F32),
+            pltpu.VMEM((NSEQ, OWNED, 2 * HEAD), BF16),
+        ),
+        in_specs=[VMEM] * (5 + NMP),
+        out_specs=(VMEM, VMEM, VMEM),
         compiler_params=params(16),
-        cost_estimate=cost(2 * OWNED * WIDTH * 2 * HEAD, 4 * MIB),
-        name="pair",
-    )(gain, in_hbm(lookup_projection), in_hbm(content_projection), *blocks)
+        cost_estimate=cost(2 * OWNED * WIDTH * 10 * HEAD, 4 * MIB),
+        name="project_in",
+    )(gain, gate_weight, asker, lookup, content, *blocks)
     pairs = lax.all_to_all(pair, "seq", split_axis=0, concat_axis=0, tiled=True)
-    query, gate = pl.pallas_call(
-        query_kernel,
-        out_shape=(shape((OWNED, GROUP * HEAD)), shape((OWNED, 128), F32)),
-        in_specs=[VMEM, HBM, VMEM] + [VMEM] * NMP,
-        out_specs=(VMEM, VMEM),
-        scratch_shapes=[
-            pltpu.VMEM((NMP, FEAT, GROUP * HEAD), BF16),
-            pltpu.SemaphoreType.DMA((NMP,)),
-        ],
-        compiler_params=params(24),
-        cost_estimate=cost(2 * OWNED * WIDTH * GROUP * HEAD, 10 * MIB),
-        name="query",
-    )(normed, in_hbm(asker_projection), gate_weight, *blocks)
     attended = pl.pallas_call(
         attention_kernel,
         out_shape=shape((OWNED, GROUP * HEAD)),
@@ -385,7 +368,7 @@
         compiler_params=params(24),
         name="attend",
     )(logit_sharpness, query, pairs)
-    final, loaded = load((final_projection,), attended, "load")
+    final, loaded = load((final_projection,), attended, "load_out")
     heads = gather_mp(attended, loaded)
     outgoing_back = pl.pallas_call(
         project_kernel,

time: 97.6 us -> 91.1 us (0.933)
  blocking collectives: 12.3 us -> 30.5 us
  waiting for transfers between devices: 22.7 us -> 8.97 us
  starting transfers between devices: 36.8 us -> 27.4 us
  Pallas kernels: 23 us -> 21.5 us
    all_to_all x0 -> x1, blocking collectives: none -> 19.2 us  [on_device(): pairs = lax.all_to_all(pair, 'seq', split_axis=0, concat_axis=0, tiled=True)]
    all_to_all x1 -> x0, waiting for transfers between devices: 13.3 us -> none  [on_device(): pairs = lax.all_to_all(pair, 'seq', split_axis=0, concat_axis=0, tiled=True)]
    ppermute x8, starting transfers between devices: 19.4 us -> 10.6 us  [other_core(): return lax.ppermute(array, 'mp', [(m, m ^ 1) for m in range(NMP)])]
    pallas_call x2 -> x3, Pallas kernels: 7.22 us -> 2.3 us  [the longest x1 2.28 us: on_device(): pl.pallas_call(project_in_kernel, out_shape=(pltpu.VMEM((OWNED, GROUP * H...]
    all_to_all x1 -> x0, starting transfers between devices: 3.67 us -> none  [on_device(): pairs = lax.all_to_all(pair, 'seq', split_axis=0, concat_axis=0, tiled=True)]
    pallas_call x1 -> x2, Pallas kernels: 3.98 us -> 7.32 us  [load(): pl.pallas_call(functools.partial(load_kernel, count), out_shape=[pltpu.VM...]
    ppermute x6, starting transfers between devices: 6.1 us -> 9.18 us  [z_step(): return lax.ppermute(array, 'mp', pairs)]
    ppermute x6, waiting for transfers between devices: 4.79 us -> 2.62 us  [z_step(): return lax.ppermute(array, 'mp', pairs)]
  transfers between devices with their start and end apart: 16 -> 15, of which waited for: 5 -> 7; matrix products, arithmetic and copies ran while one was open for 1% -> 2% of each run, Pallas kernels for 10% -> 10%
where the time goes in v3:
time: 91.1 us; the launch traced here: 90.6 us
  blocking collectives  30.5 us (33%)
  starting transfers between devices  27.4 us (30%)
  Pallas kernels  21.5 us (24%)
  waiting for transfers between devices  8.97 us (10%)
  other arithmetic  1.4 us (2%)
    all_to_all x1, blocking collectives, on_device(): pairs = lax.all_to_all(pair, 'seq', split_axis=0, concat_axis=0, tiled=True)  19.2 us
    all_to_all x1, blocking collectives, on_device(): lax.all_to_all(outgoing_back, 'seq', split_axis=0, concat_axis=0, tiled=T...  11.2 us
    ppermute x8, starting transfers between devices, other_core(): return lax.ppermute(array, 'mp', [(m, m ^ 1) for m in range(NMP)])  10.6 us
    ppermute x6, starting transfers between devices, z_step(): return lax.ppermute(array, 'mp', pairs)  9.18 us
    all_to_all x1, starting transfers between devices, on_device(): lax.all_to_all(outgoing, 'seq', split_axis=0, concat_axis=0, tiled=True)  7.6 us
    pallas_call x2, Pallas kernels, load(): pl.pallas_call(functools.partial(load_kernel, count), out_shape=[pltpu.VM...  7.32 us
    all_to_all x1, waiting for transfers between devices, on_device(): lax.all_to_all(outgoing, 'seq', split_axis=0, concat_axis=0, tiled=True)  3.6 us
    pallas_call x1, Pallas kernels, on_device(): pl.pallas_call(attention_kernel, out_shape=shape((OWNED, GROUP * HEAD)),...  3.52 us
  transfers between devices with their start and end apart: 15, of which 7 were waited for; matrix products, arithmetic and copies ran while one was open for 2% of the time, Pallas kernels for 10%

profile of v3, /device:TPU:1, one launch (start us, length us, event | category | flops | bytes accessed | tf_op | source)
XLA Modules:
  0.0 90.6 jit_solution(17194502394952835020)
XLA Ops:
  0.0 2.4 %pick.1 = bf16[16,2,8,512]{3,2,1,0:T(8,128)(2,1)} custom-call(s32[16,16]{1,0:T(8,128)} %tally_ref.3, s32[1,256]{1,0:T(1,128)} %select_ref.1, bf16[1024,512]{1,0:T(8,128)(2,1)} %rows_ref.1), custom_call_target="tpu_custom_call" | custom-call | tf_op jit(solution)/shard_map/pick/pallas_call | solution.py:306
  2.4 7.6 %all-to-all-start = ((bf16[16,2,8,512]{3,2,1,0:T(8,128)(2,1)}), bf16[16,2,8,512]{3,2,1,0:T(8,128)(2,1)S(1)}, u32[]{:S(2)}, u32[]{:S(2)}) async-start(bf16[16,2,8,512]{3,2,1,0:T(8,128)(2,1)} %pick.1), calls=%async_computation | async-start | bytes 524288 | tf_op jit(solution)/shard_map/all_to_all | solution.py:336
  10.0 0.7 reshape.14
  10.7 0.7 reshape.16
  11.4 0.7 copy-done.1
  12.1 1.8 %prep.1 = (s32[3,16]{1,0:T(4,128)S(1)}, f32[8,1,512]{2,1,0:T(1,128)S(1)}, f32[8,1,512]{2,1,0:T(1,128)S(1)}) custom-call(s32[16,16]{1,0:T(8,128)S(1)} %copy-done.1, f32[8,1,512]{2,1,0:T(1,128)S(1)} %bitcast.2, f32[8,1,512]{2,1,0:T(1,128)S(1)} %bitcast.3), custom_call_target="tpu_custom_call" | custom-call | tf_op jit(solution)/shard_map/prep/pallas_call | solution.py:320
  14.0 3.6 %all-to-all-done.in_ref = bf16[16,2,8,512]{3,2,1,0:T(8,128)(2,1)S(1)} async-done(((bf16[16,2,8,512]{3,2,1,0:T(8,128)(2,1)}), bf16[16,2,8,512]{3,2,1,0:T(8,128)(2,1)S(1)}, u32[]{:S(2)}, u32[]{:S(2)}) %all-to-all-start) | async-done | bytes 262176 | tf_op jit(solution)/shard_map/all_to_all | solution.py:336
  17.6 0.6 compact.1.refs_3_.refs_0_
  18.2 3.7 %collective-permute-start.3 = (bf16[128,512]{1,0:T(8,128)(2,1)S(1)}, bf16[128,512]{1,0:T(8,128)(2,1)S(1)}, u32[]{:S(2)}, u32[]{:S(2)}) collective-permute-start(bf16[128,512]{1,0:T(8,128)(2,1)S(1)} %compact.1.refs_3_.refs_0_), channel_id=1, source_target_pairs={{0,4},{1,5},{2,6},{3,7},{4,0},{5,1},{6,2},{7,3},{8,12},{9,13},{10,... | collective-permute-start | bytes 393224 | tf_op jit(solution)/shard_map/ppermute | solution.py:260
  21.9 0.7 collective-permute-start.1
  22.6 1.9 %collective-permute-start.5 = (bf16[128,512]{1,0:T(8,128)(2,1)S(1)}, bf16[128,512]{1,0:T(8,128)(2,1)S(1)}, u32[]{:S(2)}, u32[]{:S(2)}) collective-permute-start(bf16[128,512]{1,0:T(8,128)(2,1)S(1)} %compact.1.refs_3_.refs_0_), channel_id=1, source_target_pairs={{0,6},{1,7},{2,0},{3,1},{4,2},{5,3},{6,4},{7,5},{8,14},{9,15},{10,... | collective-permute-start | bytes 393224 | tf_op jit(solution)/shard_map/ppermute | solution.py:260
  24.5 2.9 %collective-permute-start = (bf16[128,512]{1,0:T(8,128)(2,1)S(1)}, bf16[128,512]{1,0:T(8,128)(2,1)S(1)}, u32[]{:S(2)}, u32[]{:S(2)}) collective-permute-start(bf16[128,512]{1,0:T(8,128)(2,1)S(1)} %compact.1.refs_3_.refs_0_), channel_id=1, source_target_pairs={{0,1},{1,0},{2,3},{3,2},{4,5},{5,4},{6,7},{7,6},{8,9},{9,8},{10,11... | collective-permute-start | bytes 393224 | tf_op jit(solution)/shard_map/ppermute | solution.py:264
  27.5 3.9 %load_in.1 = (bf16[4096,1024]{1,0:T(8,128)(2,1)S(1)}, bf16[4096,128]{1,0:T(8,128)(2,1)S(1)}, bf16[4096,128]{1,0:T(8,128)(2,1)S(1)}, f32[8,128]{1,0:T(8,128)S(1)}) custom-call(bf16[4096,1024]{1,0:T(8,128)(2,1)} %refs_0_.2, bf16[4096,128]{1,0:T(8,128)(2,1)} %refs_1_.1, bf16[4096,128]{1,0:T(8,128)(2,1)} %refs_2_.1, bf16[128,512]{1,0:T(8,128)(2,1)S(1)} %compact.1.refs_3_.refs_0_), custom_call_target="tpu_custom_call" | custom-call | bytes 10485760 | tf_op jit(solution)/shard_map/load_in/pallas_call | solution.py:93
  31.4 0.0 copy-start.4
  31.4 0.0 collective-permute-done.3.refs_4_
  31.4 0.1 collective-permute-start.4
  31.5 0.0 collective-permute-done.1.refs_2_
  31.6 0.5 collective-permute-start.2
  32.0 0.0 collective-permute-done.5.in_ref.refs_6_
  32.1 0.2 collective-permute-start.6
  32.2 0.0 collective-permute-done.refs_1_
  32.2 0.6 collective-permute-done.4.refs_5_
  32.9 0.2 collective-permute-done.2.refs_3_
  33.1 0.4 collective-permute-done.6.refs_7_
  33.5 2.3 %project_in.1 = (bf16[128,1024]{1,0:T(8,128)(2,1)S(1)}, f32[128,128]{1,0:T(8,128)S(1)}, bf16[16,128,256]{2,1,0:T(8,128)(2,1)S(1)}) custom-call(f32[8,1,512]{2,1,0:T(1,128)S(1)} %get-tuple-element.18.gain_ref, f32[8,1,512]{2,1,0:T(1,128)S(1)} %get-tuple-element.19.gate_weight_ref, bf16[4096,1024]{1,0:T(8,128)(2,1)S(1)} %get-tuple-element.20.query_weight_ref, ...), custom_call_target="tpu_custom_call" | custom-call | flops 1342177280 | bytes 4194304 | tf_op jit(solution)/shard_map/project_in/pallas_call | solution.py:349
  35.8 19.2 %all_to_all.15.pair_ref = bf16[16,128,256]{2,1,0:T(8,128)(2,1)S(1)} all-to-all(bf16[16,128,256]{2,1,0:T(8,128)(2,1)S(1)} %get-tuple-element.26), channel_id=1, replica_groups=mesh['seq'=16,'mp'=8] {'seq'}, dimensions={0} | all-to-all | bytes 2097152 | tf_op jit(solution)/shard_map/all_to_all | solution.py:362
  55.0 3.5 %attend.1.refs_1_.refs_0_ = bf16[128,1024]{1,0:T(8,128)(2,1)S(1)} custom-call(f32[8]{0:T(128)S(1)} %copy-done.4, bf16[128,1024]{1,0:T(8,128)(2,1)S(1)} %get-tuple-element.25.query_ref, bf16[16,128,256]{2,1,0:T(8,128)(2,1)S(1)} %all_to_all.15.pair_ref), custom_call_target="tpu_custom_call" | custom-call | tf_op jit(solution)/shard_map/attend/pallas_call | solution.py:363
  58.5 0.0 copy-start
  58.5 0.0 copy-start.2
  58.5 0.0 copy-start.3
  58.6 0.1 collective-permute-start.10
  58.6 1.3 %collective-permute-start.8 = (bf16[128,1024]{1,0:T(8,128)(2,1)S(1)}, bf16[128,1024]{1,0:T(8,128)(2,1)S(1)}, u32[]{:S(2)}, u32[]{:S(2)}) collective-permute-start(bf16[128,1024]{1,0:T(8,128)(2,1)S(1)} %attend.1.refs_1_.refs_0_), channel_id=1, source_target_pairs={{0,2},{1,3},{2,4},{3,5},{4,6},{5,7},{6,0},{7,1},{8,10},{9,11},{10,... | collective-permute-start | bytes 786440 | tf_op jit(solution)/shard_map/ppermute | solution.py:260
  60.0 1.4 %collective-permute-start.12 = (bf16[128,1024]{1,0:T(8,128)(2,1)S(1)}, bf16[128,1024]{1,0:T(8,128)(2,1)S(1)}, u32[]{:S(2)}, u32[]{:S(2)}) collective-permute-start(bf16[128,1024]{1,0:T(8,128)(2,1)S(1)} %attend.1.refs_1_.refs_0_), channel_id=1, source_target_pairs={{0,6},{1,7},{2,0},{3,1},{4,2},{5,3},{6,4},{7,5},{8,14},{9,15},{10,... | collective-permute-start | bytes 786440 | tf_op jit(solution)/shard_map/ppermute | solution.py:260
  61.4 2.2 %collective-permute-start.7 = (bf16[128,1024]{1,0:T(8,128)(2,1)S(1)}, bf16[128,1024]{1,0:T(8,128)(2,1)S(1)}, u32[]{:S(2)}, u32[]{:S(2)}) collective-permute-start(bf16[128,1024]{1,0:T(8,128)(2,1)S(1)} %attend.1.refs_1_.refs_0_), channel_id=1, source_target_pairs={{0,1},{1,0},{2,3},{3,2},{4,5},{5,4},{6,7},{7,6},{8,9},{9,8},{10,11... | collective-permute-start | bytes 786440 | tf_op jit(solution)/shard_map/ppermute | solution.py:264
  63.6 3.4 %load_out.1 = (bf16[8192,512]{1,0:T(8,128)(2,1)S(1)}, f32[8,128]{1,0:T(8,128)S(1)}) custom-call(bf16[8192,512]{1,0:T(8,128)(2,1)} %refs_0_.3, bf16[128,1024]{1,0:T(8,128)(2,1)S(1)} %attend.1.refs_1_.refs_0_), custom_call_target="tpu_custom_call" | custom-call | bytes 8388608 | tf_op jit(solution)/shard_map/load_out/pallas_call | solution.py:93
  67.0 0.0 collective-permute-done.10.refs_4_
  67.0 3.9 %collective-permute-start.11 = (bf16[128,1024]{1,0:T(8,128)(2,1)S(1)}, bf16[128,1024]{1,0:T(8,128)(2,1)S(1)}, u32[]{:S(2)}, u32[]{:S(2)}) collective-permute-start(bf16[128,1024]{1,0:T(8,128)(2,1)S(1)} %collective-permute-done.10.refs_4_), channel_id=1, source_target_pairs={{0,1},{1,0},{2,3},{3,2},{4,5},{5,4},{6,7},{7,6},{8,9},{9,8},{10,11... | collective-permute-start | bytes 786440 | tf_op jit(solution)/shard_map/ppermute | solution.py:264
  71.0 2.6 %collective-permute-done.8.refs_2_ = bf16[128,1024]{1,0:T(8,128)(2,1)S(1)} collective-permute-done((bf16[128,1024]{1,0:T(8,128)(2,1)S(1)}, bf16[128,1024]{1,0:T(8,128)(2,1)S(1)}, u32[]{:S(2)}, u32[]{:S(2)}) %collective-permute-start.8) | collective-permute-done | bytes 262176 | tf_op jit(solution)/shard_map/ppermute | solution.py:260
  73.6 0.7 collective-permute-start.9
  74.3 0.0 collective-permute-done.12.in_ref.refs_6_
  74.3 0.1 collective-permute-start.13
  74.4 0.0 collective-permute-done.7.refs_1_
  74.4 0.0 collective-permute-done.11.refs_5_
  74.4 1.0 %collective-permute-done.9.refs_3_ = bf16[128,1024]{1,0:T(8,128)(2,1)S(1)} collective-permute-done((bf16[128,1024]{1,0:T(8,128)(2,1)S(1)}, bf16[128,1024]{1,0:T(8,128)(2,1)S(1)}, u32[]{:S(2)}, u32[]{:S(2)}) %collective-permute-start.9) | collective-permute-done | bytes 262176 | tf_op jit(solution)/shard_map/ppermute | solution.py:264
  75.4 0.5 collective-permute-done.13.refs_7_
  75.9 1.9 %project.1 = bf16[16,2,8,512]{3,2,1,0:T(8,128)(2,1)S(1)} custom-call(s32[3,16]{1,0:T(4,128)S(1)} %get-tuple-element.17.table_ref, f32[128,128]{1,0:T(8,128)S(1)} %get-tuple-element.24.gate_ref, bf16[8192,512]{1,0:T(8,128)(2,1)S(1)} %get-tuple-element.27.weight_ref, bf16[128,1024]{1,0:T(8,128)(2,1)S(1)} %attend.1.refs_1_.refs_0_, ...), custom_call_target="tpu_custom_call" | custom-call | tf_op jit(solution)/shard_map/project/pallas_call | solution.py:373
  77.8 11.2 %all_to_all.16.back_ref = bf16[16,2,8,512]{3,2,1,0:T(8,128)(2,1)S(1)} all-to-all(bf16[16,2,8,512]{3,2,1,0:T(8,128)(2,1)S(1)} %project.1), channel_id=1, replica_groups=mesh['seq'=16,'mp'=8] {'seq'}, dimensions={0} | all-to-all | bytes 524288 | tf_op jit(solution)/shard_map/all_to_all | solution.py:382
  89.0 1.6 %blend.1 = bf16[1024,512]{1,0:T(8,128)(2,1)} custom-call(s32[16,16]{1,0:T(8,128)S(1)} %copy-done.2, s32[1,256]{1,0:T(1,128)S(1)} %copy-done.3, bf16[1024,512]{1,0:T(8,128)(2,1)S(1)} %copy-done, bf16[16,2,8,512]{3,2,1,0:T(8,128)(2,1)S(1)} %all_to_all.16.back_ref), custom_call_target="tpu_custom_call" | custom-call | tf_op jit(solution)/shard_map/blend/pallas_call | solution.py:383
  (7 shorter events, 0.0 us)
Async XLA Ops:
  2.4 15.1 %all-to-all-start = ((bf16[16,2,8,512]{3,2,1,0:T(8,128)(2,1)}), bf16[16,2,8,512]{3,2,1,0:T(8,128)(2,1)S(1)}, u32[]{:S(2)}, u32[]{:S(2)}) async-start(bf16[16,2,8,512]{3,2,1,0:T(8,128)(2,1)} %pick.1), calls=%async_computation | async-start | bytes 524288 | tf_op jit(solution)/shard_map/all_to_all | solution.py:336
  11.4 0.7 copy-start.1
  18.2 13.3 %collective-permute-start.3 = (bf16[128,512]{1,0:T(8,128)(2,1)S(1)}, bf16[128,512]{1,0:T(8,128)(2,1)S(1)}, u32[]{:S(2)}, u32[]{:S(2)}) collective-permute-start(bf16[128,512]{1,0:T(8,128)(2,1)S(1)} %compact.1.refs_3_.refs_0_), channel_id=1, source_target_pairs={{0,4},{1,5},{2,6},{3,7},{4,0},{5,1},{6,2},{7,3},{8,12},{9,13},{10,... | collective-permute-start | bytes 393224 | tf_op jit(solution)/shard_map/ppermute | solution.py:260
  21.9 9.7 %collective-permute-start.1 = (bf16[128,512]{1,0:T(8,128)(2,1)S(1)}, bf16[128,512]{1,0:T(8,128)(2,1)S(1)}, u32[]{:S(2)}, u32[]{:S(2)}) collective-permute-start(bf16[128,512]{1,0:T(8,128)(2,1)S(1)} %compact.1.refs_3_.refs_0_), channel_id=1, source_target_pairs={{0,2},{1,3},{2,4},{3,5},{4,6},{5,7},{6,0},{7,1},{8,10},{9,11},{10,... | collective-permute-start | bytes 393224 | tf_op jit(solution)/shard_map/ppermute | solution.py:260
  22.6 9.4 %collective-permute-start.5 = (bf16[128,512]{1,0:T(8,128)(2,1)S(1)}, bf16[128,512]{1,0:T(8,128)(2,1)S(1)}, u32[]{:S(2)}, u32[]{:S(2)}) collective-permute-start(bf16[128,512]{1,0:T(8,128)(2,1)S(1)} %compact.1.refs_3_.refs_0_), channel_id=1, source_target_pairs={{0,6},{1,7},{2,0},{3,1},{4,2},{5,3},{6,4},{7,5},{8,14},{9,15},{10,... | collective-permute-start | bytes 393224 | tf_op jit(solution)/shard_map/ppermute | solution.py:260
  24.5 7.7 %collective-permute-start = (bf16[128,512]{1,0:T(8,128)(2,1)S(1)}, bf16[128,512]{1,0:T(8,128)(2,1)S(1)}, u32[]{:S(2)}, u32[]{:S(2)}) collective-permute-start(bf16[128,512]{1,0:T(8,128)(2,1)S(1)} %compact.1.refs_3_.refs_0_), channel_id=1, source_target_pairs={{0,1},{1,0},{2,3},{3,2},{4,5},{5,4},{6,7},{7,6},{8,9},{9,8},{10,11... | collective-permute-start | bytes 393224 | tf_op jit(solution)/shard_map/ppermute | solution.py:264
  31.4 23.6 %copy-start.4 = (f32[8]{0:T(128)S(1)}, f32[8]{0:T(128)}, u32[]{:S(2)}) copy-start(f32[8]{0:T(128)} %sharp_ref.1) | copy-start | bytes 100
  31.4 1.4 %collective-permute-start.4 = (bf16[128,512]{1,0:T(8,128)(2,1)S(1)}, bf16[128,512]{1,0:T(8,128)(2,1)S(1)}, u32[]{:S(2)}, u32[]{:S(2)}) collective-permute-start(bf16[128,512]{1,0:T(8,128)(2,1)S(1)} %collective-permute-done.3.refs_4_), channel_id=1, source_target_pairs={{0,1},{1,0},{2,3},{3,2},{4,5},{5,4},{6,7},{7,6},{8,9},{9,8},{10,11... | collective-permute-start | bytes 393224 | tf_op jit(solution)/shard_map/ppermute | solution.py:264
  31.6 1.5 %collective-permute-start.2 = (bf16[128,512]{1,0:T(8,128)(2,1)S(1)}, bf16[128,512]{1,0:T(8,128)(2,1)S(1)}, u32[]{:S(2)}, u32[]{:S(2)}) collective-permute-start(bf16[128,512]{1,0:T(8,128)(2,1)S(1)} %collective-permute-done.1.refs_2_), channel_id=1, source_target_pairs={{0,1},{1,0},{2,3},{3,2},{4,5},{5,4},{6,7},{7,6},{8,9},{9,8},{10,11... | collective-permute-start | bytes 393224 | tf_op jit(solution)/shard_map/ppermute | solution.py:264
  32.1 1.4 %collective-permute-start.6 = (bf16[128,512]{1,0:T(8,128)(2,1)S(1)}, bf16[128,512]{1,0:T(8,128)(2,1)S(1)}, u32[]{:S(2)}, u32[]{:S(2)}) collective-permute-start(bf16[128,512]{1,0:T(8,128)(2,1)S(1)} %hand_on.2), channel_id=1, source_target_pairs={{0,1},{1,0},{2,3},{3,2},{4,5},{5,4},{6,7},{7,6},{8,9},{9,8},{10,11... | collective-permute-start | bytes 393224 | tf_op jit(solution)/shard_map/ppermute | solution.py:264
  58.5 30.5 %copy-start = (bf16[1024,512]{1,0:T(8,128)(2,1)S(1)}, bf16[1024,512]{1,0:T(8,128)(2,1)}, u32[]{:S(2)}) copy-start(bf16[1024,512]{1,0:T(8,128)(2,1)} %rows_ref.1) | copy-start | bytes 3145732
  58.5 30.5 %copy-start.2 = (s32[16,16]{1,0:T(8,128)S(1)}, s32[16,16]{1,0:T(8,128)}, u32[]{:S(2)}) copy-start(s32[16,16]{1,0:T(8,128)} %tally_ref.3) | copy-start | bytes 3076
  58.5 30.5 %copy-start.3 = (s32[1,256]{1,0:T(1,128)S(1)}, s32[1,256]{1,0:T(1,128)}, u32[]{:S(2)}) copy-start(s32[1,256]{1,0:T(1,128)} %select_ref.1) | copy-start | bytes 3076
  58.6 8.5 %collective-permute-start.10 = (bf16[128,1024]{1,0:T(8,128)(2,1)S(1)}, bf16[128,1024]{1,0:T(8,128)(2,1)S(1)}, u32[]{:S(2)}, u32[]{:S(2)}) collective-permute-start(bf16[128,1024]{1,0:T(8,128)(2,1)S(1)} %attend.1.refs_1_.refs_0_), channel_id=1, source_target_pairs={{0,4},{1,5},{2,6},{3,7},{4,0},{5,1},{6,2},{7,3},{8,12},{9,13},{10,... | collective-permute-start | bytes 786440 | tf_op jit(solution)/shard_map/ppermute | solution.py:260
  58.6 14.9 %collective-permute-start.8 = (bf16[128,1024]{1,0:T(8,128)(2,1)S(1)}, bf16[128,1024]{1,0:T(8,128)(2,1)S(1)}, u32[]{:S(2)}, u32[]{:S(2)}) collective-permute-start(bf16[128,1024]{1,0:T(8,128)(2,1)S(1)} %attend.1.refs_1_.refs_0_), channel_id=1, source_target_pairs={{0,2},{1,3},{2,4},{3,5},{4,6},{5,7},{6,0},{7,1},{8,10},{9,11},{10,... | collective-permute-start | bytes 786440 | tf_op jit(solution)/shard_map/ppermute | solution.py:260
  60.0 14.3 %collective-permute-start.12 = (bf16[128,1024]{1,0:T(8,128)(2,1)S(1)}, bf16[128,1024]{1,0:T(8,128)(2,1)S(1)}, u32[]{:S(2)}, u32[]{:S(2)}) collective-permute-start(bf16[128,1024]{1,0:T(8,128)(2,1)S(1)} %attend.1.refs_1_.refs_0_), channel_id=1, source_target_pairs={{0,6},{1,7},{2,0},{3,1},{4,2},{5,3},{6,4},{7,5},{8,14},{9,15},{10,... | collective-permute-start | bytes 786440 | tf_op jit(solution)/shard_map/ppermute | solution.py:260
  61.4 13.0 %collective-permute-start.7 = (bf16[128,1024]{1,0:T(8,128)(2,1)S(1)}, bf16[128,1024]{1,0:T(8,128)(2,1)S(1)}, u32[]{:S(2)}, u32[]{:S(2)}) collective-permute-start(bf16[128,1024]{1,0:T(8,128)(2,1)S(1)} %attend.1.refs_1_.refs_0_), channel_id=1, source_target_pairs={{0,1},{1,0},{2,3},{3,2},{4,5},{5,4},{6,7},{7,6},{8,9},{9,8},{10,11... | collective-permute-start | bytes 786440 | tf_op jit(solution)/shard_map/ppermute | solution.py:264
  67.0 7.4 %collective-permute-start.11 = (bf16[128,1024]{1,0:T(8,128)(2,1)S(1)}, bf16[128,1024]{1,0:T(8,128)(2,1)S(1)}, u32[]{:S(2)}, u32[]{:S(2)}) collective-permute-start(bf16[128,1024]{1,0:T(8,128)(2,1)S(1)} %collective-permute-done.10.refs_4_), channel_id=1, source_target_pairs={{0,1},{1,0},{2,3},{3,2},{4,5},{5,4},{6,7},{7,6},{8,9},{9,8},{10,11... | collective-permute-start | bytes 786440 | tf_op jit(solution)/shard_map/ppermute | solution.py:264
  73.6 1.9 %collective-permute-start.9 = (bf16[128,1024]{1,0:T(8,128)(2,1)S(1)}, bf16[128,1024]{1,0:T(8,128)(2,1)S(1)}, u32[]{:S(2)}, u32[]{:S(2)}) collective-permute-start(bf16[128,1024]{1,0:T(8,128)(2,1)S(1)} %collective-permute-done.8.refs_2_), channel_id=1, source_target_pairs={{0,1},{1,0},{2,3},{3,2},{4,5},{5,4},{6,7},{7,6},{8,9},{9,8},{10,11... | collective-permute-start | bytes 786440 | tf_op jit(solution)/shard_map/ppermute | solution.py:264
  74.3 1.6 %collective-permute-start.13 = (bf16[128,1024]{1,0:T(8,128)(2,1)S(1)}, bf16[128,1024]{1,0:T(8,128)(2,1)S(1)}, u32[]{:S(2)}, u32[]{:S(2)}) collective-permute-start(bf16[128,1024]{1,0:T(8,128)(2,1)S(1)} %hand_on.3), channel_id=1, source_target_pairs={{0,1},{1,0},{2,3},{3,2},{4,5},{5,4},{6,7},{7,6},{8,9},{9,8},{10,11... | collective-permute-start | bytes 786440 | tf_op jit(solution)/shard_map/ppermute | solution.py:264

commit v4 on v3

v4 whole, which is shorter than its diff:
```python
import functools
import math

import jax
import jax.numpy as jnp
from jax import lax
from jax.experimental import pallas as pl
from jax.experimental.pallas import tpu as pltpu
from jax.sharding import PartitionSpec as P

NSEQ = 16
NMP = 8
BLOCK = 8
OWNED = 128
SLOTS = 256
SRC = 1024
FEAT = 512
WIDTH = 4096
HEAD = 128
GROUP = 8
MIB = 1 << 20

VMEM = pl.BlockSpec(memory_space=pltpu.VMEM)
SMEM = pl.BlockSpec(memory_space=pltpu.SMEM)
HBM = pl.BlockSpec(memory_space=pltpu.HBM)
ANY = pl.BlockSpec(memory_space=pl.ANY)
F32 = jnp.float32
BF16 = jnp.bfloat16


def params(mib):
    return pltpu.CompilerParams(vmem_limit_bytes=mib * MIB)


def cost(flops, bytes_accessed, transcendentals=0):
    return pl.CostEstimate(flops=flops, bytes_accessed=bytes_accessed, transcendentals=transcendentals)


def own_span(tally, shard):
    row = lax.broadcasted_iota(jnp.int32, (NSEQ, NSEQ), 0)
    before = jnp.sum(jnp.where(row < shard, tally, 0))
    mine = jnp.sum(jnp.where(row == shard, tally, 0))
    return before // BLOCK, mine


def deal(tally, shard):
    row = lax.broadcasted_iota(jnp.int32, (NSEQ, NSEQ), 0)
    lane = lax.broadcasted_iota(jnp.int32, (NSEQ, NSEQ), 1)
    total = jnp.right_shift(jnp.sum(tally, axis=1, keepdims=True), 3)
    across = jnp.sum(jnp.where(row == lane, total, 0), axis=0, keepdims=True)
    start = jnp.sum(jnp.where(lane < row, across, 0), axis=1, keepdims=True)
    start_across = jnp.sum(jnp.where(row < lane, total, 0), axis=0, keepdims=True)
    block = lane[:1] * NSEQ + shard
    past = start <= block
    source = jnp.sum(past.astype(jnp.int32), axis=0, keepdims=True) - 1
    begin = jnp.max(jnp.where(past, start, 0), axis=0, keepdims=True)
    return jnp.concatenate([start_across, source, jnp.right_shift(block - begin, 4)], axis=0)


def pick_kernel(tally_hbm, select_hbm, rows_hbm, out_ref, table_ref, tally_ref, select_ref, rows_ref, sems):
    parts = rows_ref.shape[0]
    wide = SRC // parts
    copies = [
        pltpu.make_async_copy(tally_hbm, tally_ref, sems.at[parts]),
        pltpu.make_async_copy(select_hbm, select_ref, sems.at[parts + 1]),
    ] + [
        pltpu.make_async_copy(rows_hbm.at[pl.ds(wide * p, wide), :], rows_ref.at[p], sems.at[p])
        for p in range(parts)
    ]
    for copy in copies:
        copy.start()
    copies[0].wait()
    copies[1].wait()
    tally = tally_ref[...]
    shard = lax.axis_index("seq")
    first, count = own_span(tally, shard)
    table_ref[...] = deal(tally, shard)
    listed = select_ref[...]
    slot = lax.broadcasted_iota(jnp.int32, (1, SLOTS), 1)
    listed = jnp.where(slot < count, listed, -1).astype(F32)
    column = jnp.broadcast_to(listed, (128, SLOTS)).T
    lane = lax.broadcasted_iota(jnp.int32, (SLOTS, 128), 1).astype(F32)
    picked = jnp.zeros((SLOTS, FEAT), F32)
    for p in range(parts):
        hot = jnp.concatenate(
            [(column == lane + float(wide * p + 128 * k)).astype(F32) for k in range(wide // 128)],
            axis=1,
        ).astype(BF16)
        copies[2 + p].wait()
        picked = picked + jnp.dot(hot, rows_ref[p], preferred_element_type=F32)
    for j in range(SLOTS // BLOCK):
        owner = lax.rem(first + j, NSEQ)
        out_ref[owner, j // NSEQ] = picked[BLOCK * j : BLOCK * (j + 1)].astype(BF16)


def load_kernel(count, *refs):
    sources, targets, done_ref, sems = refs[:count], refs[-2 - count : -2], refs[-2], refs[-1]
    copies = [pltpu.make_async_copy(a, b, sems.at[k]) for k, (a, b) in enumerate(zip(sources, targets))]
    for copy in copies:
        copy.start()
    for copy in copies:
        copy.wait()
    done_ref[...] = jnp.zeros_like(done_ref)


def in_hbm(array):
    return pltpu.with_memory_space_constraint(array, pltpu.HBM)


def in_vmem(array):
    return pltpu.with_memory_space_constraint(array, pltpu.VMEM)


def load(arrays, after, name):
    count = len(arrays)
    return pl.pallas_call(
        functools.partial(load_kernel, count),
        out_shape=[pltpu.VMEM(a.shape, a.dtype) for a in arrays] + [pltpu.VMEM((8, 128), F32)],
        in_specs=[HBM] * count + [ANY],
        out_specs=[VMEM] * (count + 1),
        scratch_shapes=[pltpu.SemaphoreType.DMA((count,))],
        compiler_params=params(8),
        cost_estimate=cost(0, sum(a.size for a in arrays) * 2),
        name=name,
    )(*map(in_hbm, arrays), after)


def compact_kernel(table_ref, in_ref, out_ref):
    for i in range(0, NSEQ, 2):
        pair = [
            in_ref[table_ref[1, k], table_ref[2, k]].astype(F32) for k in (i, i + 1)
        ]
        out_ref[BLOCK * i : BLOCK * (i + 2)] = jnp.concatenate(pair, axis=0).astype(BF16)


def block_of(k):
    me = lax.axis_index("mp")
    chip = lax.rem(me // 2 + (4 - k // 2), 4)
    core = lax.rem(lax.rem(me, 2) + k % 2, 2)
    return chip * 2 + core


def spread(packed_ref, spread_ref):
    wide = packed_ref[...].astype(F32)
    parts = FEAT // 128
    for r in range(WIDTH // 128):
        spread_ref[r // parts, r % parts : r % parts + 1] = wide[r : r + 1]


def project_in_kernel(gain_in, query_weight_ref, keys_ref, values_ref, *refs):
    blocks, (query_ref, pair_ref, gain_ref) = refs[:NMP], refs[NMP:]
    parts = FEAT // 128
    spread(gain_in, gain_ref)
    squares = jnp.zeros((OWNED, 128), F32)
    for k in range(NMP):
        for c in range(parts):
            wide = blocks[k][:, 128 * c : 128 * (c + 1)].astype(F32)
            squares = squares + wide * wide
    inverse = lax.rsqrt(jnp.sum(squares, axis=1, keepdims=True) / WIDTH + 1e-05)
    query = jnp.zeros((OWNED, GROUP * HEAD), F32)
    keys = jnp.zeros((OWNED, HEAD), F32)
    values = jnp.zeros((OWNED, HEAD), F32)
    for k in range(NMP):
        m = block_of(k)
        rows = pl.ds(pl.multiple_of(m * FEAT, FEAT), FEAT)
        gain = gain_ref[m]
        normed = jnp.concatenate(
            [
                (
                    blocks[k][:, 128 * c : 128 * (c + 1)].astype(F32) * inverse * gain[c : c + 1]
                ).astype(BF16)
                for c in range(parts)
            ],
            axis=1,
        )
        keys = keys + jnp.dot(normed, keys_ref[rows, :], preferred_element_type=F32)
        values = values + jnp.dot(normed, values_ref[rows, :], preferred_element_type=F32)
        query = query + jnp.dot(normed, query_weight_ref[rows, :], preferred_element_type=F32)
    query_ref[...] = query.astype(BF16)
    keys = keys.astype(BF16)
    values = values.astype(BF16)
    for d in range(NSEQ):
        pair_ref[d, :, :HEAD] = keys
        pair_ref[d, :, HEAD:] = values


def attention_kernel(sharp_ref, query_ref, pair_ref, out_ref):
    shard = lax.axis_index("seq")
    step = 4 * BLOCK
    rows = GROUP * step
    many = NSEQ * step
    scale = jnp.concatenate(
        [
            jnp.full((step, 1), sharp_ref[h] * (math.log2(math.e) / math.sqrt(HEAD)), F32)
            for h in range(GROUP)
        ],
        axis=0,
    )
    q_row = lax.rem(lax.broadcasted_iota(jnp.int32, (rows, 1), 0), step)
    q_place = (q_row // BLOCK * NSEQ + shard) * BLOCK + q_row % BLOCK
    k_row = lax.broadcasted_iota(jnp.int32, (1, many), 1)
    k_place = ((k_row % step) // BLOCK * NSEQ + k_row // step) * BLOCK + k_row % BLOCK
    allowed = k_place <= q_place

    def scores_of(j):
        query = jnp.concatenate(
            [query_ref[step * j : step * (j + 1), HEAD * h : HEAD * (h + 1)] for h in range(GROUP)],
            axis=0,
        )
        scores = []
        for c in range(j + 1):
            keys = pair_ref[:, step * c : step * (c + 1), :HEAD].reshape(many, HEAD)
            score = lax.dot_general(
                query, keys, (((1,), (1,)), ((), ())), preferred_element_type=F32
            )
            scores.append(jnp.where(allowed, score, -1e30) if c == j else score)
        return scores

    later = scores_of(3)
    for j in (3, 2, 1, 0):
        scores = later
        if j:
            later = scores_of(j - 1)
        best = functools.reduce(
            jnp.maximum, [jnp.max(score, axis=1, keepdims=True) for score in scores]
        )
        offset = best * scale
        total = jnp.zeros((rows, 1), F32)
        mixed = jnp.zeros((rows, HEAD), F32)
        for c, score in enumerate(scores):
            weight = jnp.exp2(score * scale - offset)
            total = total + jnp.sum(weight, axis=1, keepdims=True)
            values = pair_ref[:, step * c : step * (c + 1), HEAD:].reshape(many, HEAD)
            mixed = mixed + jnp.dot(weight.astype(BF16), values, preferred_element_type=F32)
        mixed = (mixed / total).astype(BF16)
        for h in range(GROUP):
            out_ref[step * j : step * (j + 1), HEAD * h : HEAD * (h + 1)] = mixed[
                step * h : step * (h + 1)
            ]


EARLY, MIDDLE, LAST = (0, 1), (2, 3, 4, 5, 6), (7,)


def head_sum(which, weight_ref, blocks):
    wide = GROUP * HEAD
    total = jnp.zeros((OWNED, FEAT), F32)
    for k, block in zip(which, blocks):
        rows = pl.ds(pl.multiple_of(block_of(k) * wide, wide), wide)
        total = total + jnp.dot(block[...], weight_ref[rows, :], preferred_element_type=F32)
    return total


def project_early_kernel(weight_ref, gate_in, *refs):
    tokens, heads, (total_ref, gate_ref, gate_weight_ref) = refs[:NMP], refs[NMP:-3], refs[-3:]
    spread(gate_in, gate_weight_ref)
    routed = jnp.zeros((OWNED, 128), F32)
    for k in range(NMP):
        weights = gate_weight_ref[block_of(k)]
        for c in range(FEAT // 128):
            routed = routed + tokens[k][:, 128 * c : 128 * (c + 1)].astype(F32) * weights[c : c + 1]
    gate_ref[...] = jnp.broadcast_to(
        jax.nn.sigmoid(jnp.sum(routed, axis=1, keepdims=True)), (OWNED, 128)
    )
    total_ref[...] = head_sum(EARLY, weight_ref, heads)


def project_middle_kernel(total_in, weight_ref, *refs):
    refs[-1][...] = total_in[...] + head_sum(MIDDLE, weight_ref, refs[:-1])


def project_last_kernel(table_ref, gate_ref, total_ref, weight_ref, *refs):
    blocks, (out_ref, delta_ref) = refs[:-2], refs[-2:]
    shard = lax.axis_index("seq")
    delta = (total_ref[...] + head_sum(LAST, weight_ref, blocks)) * gate_ref[:, :1]
    for i in range(NSEQ):
        delta_ref[i] = delta[BLOCK * i : BLOCK * (i + 1)]
    for s in range(NSEQ):
        first = table_ref[0, s]
        counter = lax.rem(shard + NSEQ * NSEQ - first, NSEQ)
        for half in range(2):
            place = jnp.minimum((first + counter) // NSEQ + half, NSEQ - 1)
            out_ref[s, half] = delta_ref[place].astype(BF16)


def blend_kernel(tally_ref, select_ref, rows_ref, back_ref, out_hbm, update_ref, out_ref, sems):
    first, count = own_span(tally_ref[...], lax.axis_index("seq"))
    for j in range(0, SLOTS // BLOCK, 2):
        pair = [
            back_ref[lax.rem(first + k, NSEQ), k // NSEQ].astype(F32) for k in (j, j + 1)
        ]
        update_ref[BLOCK * j : BLOCK * (j + 2)] = jnp.concatenate(pair, axis=0).astype(BF16)
    slot = lax.broadcasted_iota(jnp.int32, (1, SLOTS), 1)
    listed = jnp.where(slot < count, select_ref[...], -1)
    parts = out_ref.shape[0]
    wide = SRC // parts
    token = lax.broadcasted_iota(jnp.int32, (wide, 1), 0)
    copies = []
    for p in range(parts):
        here = slice(wide * p, wide * (p + 1))
        hot = (listed == token + wide * p).astype(F32).astype(BF16)
        added = jnp.dot(hot, update_ref[...], preferred_element_type=F32)
        out_ref[p] = (rows_ref[here].astype(F32) + added).astype(BF16)
        copies.append(pltpu.make_async_copy(out_ref.at[p], out_hbm.at[pl.ds(wide * p, wide), :], sems.at[p]))
        copies[p].start()
    for copy in copies:
        copy.wait()


def z_step(array, steps):
    pairs = [(z * 2 + c, (z + steps) % 4 * 2 + c) for z in range(4) for c in range(2)]
    return lax.ppermute(array, "mp", pairs)


def other_core(array):
    return lax.ppermute(array, "mp", [(m, m ^ 1) for m in range(NMP)])


def hand_on_kernel(in_ref, token_ref, out_ref):
    out_ref[...] = in_ref[...]


def hand_on(array, token):
    return pl.pallas_call(
        hand_on_kernel,
        out_shape=pltpu.VMEM(array.shape, array.dtype),
        in_specs=[VMEM, ANY],
        out_specs=VMEM,
        compiler_params=params(4),
        name="hand_on",
    )(array, token)


def z_blocks(array):
    return {0: array, 2: z_step(array, 1), 6: z_step(array, 3), 4: z_step(array, 2)}


def add_cores(blocks, token):
    for k in (6, 2, 4):
        blocks[k + 1] = other_core(hand_on(blocks[k], token) if k == 6 else blocks[k])


def shape(dims, dtype=BF16):
    return jax.ShapeDtypeStruct(dims, dtype)


def on_device(
    residual_activations,
    prelayer_gain_vector,
    gating_projection,
    asker_projection,
    lookup_projection,
    content_projection,
    final_projection,
    logit_sharpness,
    selection_table,
    dispatched_tally_table,
):
    outgoing, table = pl.pallas_call(
        pick_kernel,
        out_shape=(pltpu.VMEM((NSEQ, 2, BLOCK, FEAT), BF16), shape((3, NSEQ), jnp.int32)),
        in_specs=[HBM] * 3,
        out_specs=(VMEM, VMEM),
        scratch_shapes=[
            pltpu.VMEM((NSEQ, NSEQ), jnp.int32),
            pltpu.VMEM((1, SLOTS), jnp.int32),
            pltpu.VMEM((4, SRC // 4, FEAT), BF16),
            pltpu.SemaphoreType.DMA((6,)),
        ],
        compiler_params=params(16),
        name="pick",
    )(in_hbm(dispatched_tally_table), in_hbm(selection_table), in_hbm(residual_activations))
    incoming = lax.all_to_all(outgoing, "seq", split_axis=0, concat_axis=0, tiled=True)
    tokens = pl.pallas_call(
        compact_kernel,
        out_shape=shape((OWNED, FEAT)),
        in_specs=[SMEM, VMEM],
        out_specs=VMEM,
        compiler_params=params(4),
        name="compact",
    )(table, incoming)
    asker, lookup, content, loaded = load(
        (asker_projection, lookup_projection, content_projection), tokens, "load_in"
    )
    blocks = z_blocks(tokens)
    blocks[1] = other_core(tokens)
    add_cores(blocks, loaded)
    blocks = [blocks[k] for k in range(NMP)]
    query, pair = pl.pallas_call(
        project_in_kernel,
        out_shape=(
            pltpu.VMEM((OWNED, GROUP * HEAD), BF16),
            pltpu.VMEM((NSEQ, OWNED, 2 * HEAD), BF16),
        ),
        in_specs=[VMEM] * (4 + NMP),
        out_specs=[VMEM] * 2,
        scratch_shapes=[pltpu.VMEM((NMP, FEAT // 128, 128), F32)],
        compiler_params=params(16),
        cost_estimate=cost(2 * OWNED * WIDTH * 10 * HEAD, 4 * MIB),
        name="project_in",
    )(
        prelayer_gain_vector.reshape(WIDTH // 128, 128),
        asker,
        lookup,
        content,
        *blocks,
    )
    pairs = lax.all_to_all(pair, "seq", split_axis=0, concat_axis=0, tiled=True)

    attended = pl.pallas_call(
        attention_kernel,
        out_shape=shape((OWNED, GROUP * HEAD)),
        in_specs=[SMEM, VMEM, VMEM],
        out_specs=VMEM,
        compiler_params=params(24),
        name="attend",
    )(logit_sharpness, query, pairs)
    final, _ = load((final_projection,), attended, "load_out")
    heads = z_blocks(attended)
    heads[1] = other_core(attended)
    total, gate = pl.pallas_call(
        project_early_kernel,
        out_shape=(pltpu.VMEM((OWNED, FEAT), F32), pltpu.VMEM((OWNED, 128), F32)),
        in_specs=[VMEM] * (2 + NMP + len(EARLY)),
        out_specs=(VMEM, VMEM),
        scratch_shapes=[pltpu.VMEM((NMP, FEAT // 128, 128), F32)],
        compiler_params=params(16),
        name="project_early",
    )(final, gating_projection.reshape(WIDTH // 128, 128), *blocks, *(heads[k] for k in EARLY))
    add_cores(heads, total)
    total = pl.pallas_call(
        project_middle_kernel,
        out_shape=pltpu.VMEM((OWNED, FEAT), F32),
        in_specs=[VMEM] * (2 + len(MIDDLE)),
        out_specs=VMEM,
        compiler_params=params(16),
        name="project_middle",
    )(total, final, *(heads[k] for k in MIDDLE))
    outgoing_back = pl.pallas_call(
        project_last_kernel,
        out_shape=pltpu.VMEM((NSEQ, 2, BLOCK, FEAT), BF16),
        in_specs=[SMEM] + [VMEM] * (3 + len(LAST)),
        out_specs=VMEM,
        scratch_shapes=[pltpu.VMEM((NSEQ, BLOCK, FEAT), F32)],
        compiler_params=params(16),
        name="project_last",
    )(table, gate, total, final, *(heads[k] for k in LAST))
    back = lax.all_to_all(outgoing_back, "seq", split_axis=0, concat_axis=0, tiled=True)
    return pl.pallas_call(
        blend_kernel,
        out_shape=shape((SRC, FEAT)),
        in_specs=[VMEM] * 4,
        out_specs=HBM,
        scratch_shapes=[
            pltpu.VMEM((SLOTS, FEAT), BF16),
            pltpu.VMEM((4, SRC // 4, FEAT), BF16),
            pltpu.SemaphoreType.DMA((4,)),
        ],
        compiler_params=params(16),
        name="blend",
    )(dispatched_tally_table, selection_table, residual_activations, back)


def solution(mesh):
    placed = (
        P("seq", "mp"),
        P(),
        P(),
        P(None, "mp"),
        P(None, "mp"),
        P(None, "mp"),
        P(None, "mp"),
        P("mp"),
        P("seq", None),
        P(),
    )
    return jax.shard_map(
        on_device, mesh=mesh, in_specs=placed, out_specs=P("seq", "mp"), check_vma=False
    )
```

time: 91.1 us -> 88.6 us (0.973)
  blocking collectives: 30.5 us -> 45.5 us
  starting transfers between devices: 27.4 us -> 19.3 us
  waiting for transfers between devices: 8.97 us -> 4.53 us
  Pallas kernels: 21.5 us -> 18.9 us
  other arithmetic: 1.4 us -> 0 us
    all_to_all x0 -> x1, blocking collectives: none -> 14.9 us  [on_device(): lax.all_to_all(outgoing, 'seq', split_axis=0, concat_axis=0, tiled=True)]
    all_to_all x1 -> x0, starting transfers between devices: 7.6 us -> none  [on_device(): lax.all_to_all(outgoing, 'seq', split_axis=0, concat_axis=0, tiled=True)]
    all_to_all x1 -> x0, waiting for transfers between devices: 3.6 us -> none  [on_device(): lax.all_to_all(outgoing, 'seq', split_axis=0, concat_axis=0, tiled=True)]
    pallas_call x3 -> x4, Pallas kernels: 6.13 us -> 4 us  [the longest x1 1.69 us: on_device(): pl.pallas_call(pick_kernel, out_shape=(pltpu.VMEM((NSEQ, 2, BLOCK, FEAT),...]
    reshape x2 -> x0, other arithmetic: 1.4 us -> none  [the longest x1 0.7 us: on_device(): prelayer_gain_vector.astype(F32).reshape(NMP, 1, FEAT)]
  transfers between devices with their start and end apart: 15 -> 14, of which waited for: 7 -> 6; matrix products, arithmetic and copies ran while one was open for 2% -> 0% of each run, Pallas kernels for 10% -> 11%
where the time goes in v4:
time: 88.6 us; the launch traced here: 88.3 us
  blocking collectives  45.5 us (51%)
  starting transfers between devices  19.3 us (22%)
  Pallas kernels  18.9 us (21%)
  waiting for transfers between devices  4.53 us (5%)
    all_to_all x1, blocking collectives, on_device(): pairs = lax.all_to_all(pair, 'seq', split_axis=0, concat_axis=0, tiled=True)  19.2 us
    all_to_all x1, blocking collectives, on_device(): lax.all_to_all(outgoing, 'seq', split_axis=0, concat_axis=0, tiled=True)  14.9 us
    all_to_all x1, blocking collectives, on_device(): lax.all_to_all(outgoing_back, 'seq', split_axis=0, concat_axis=0, tiled=T...  11.4 us
    ppermute x8, starting transfers between devices, other_core(): return lax.ppermute(array, 'mp', [(m, m ^ 1) for m in range(NMP)])  10.4 us
    ppermute x6, starting transfers between devices, z_step(): return lax.ppermute(array, 'mp', pairs)  8.82 us
    pallas_call x2, Pallas kernels, load(): pl.pallas_call(functools.partial(load_kernel, count), out_shape=[pltpu.VM...  7.92 us
    pallas_call x1, Pallas kernels, on_device(): pl.pallas_call(attention_kernel, out_shape=shape((OWNED, GROUP * HEAD)),...  2.69 us
    ppermute x6, waiting for transfers between devices, z_step(): return lax.ppermute(array, 'mp', pairs)  2.62 us
  transfers between devices with their start and end apart: 14, of which 6 were waited for; matrix products, arithmetic and copies ran while one was open for 0% of the time, Pallas kernels for 11%

profile of v4, /device:TPU:1, one launch (start us, length us, event | category | flops | bytes accessed | tf_op | source)
XLA Modules:
  0.0 88.3 jit_solution(6641061499980057344)
XLA Ops:
  0.0 1.7 %pick.1 = (bf16[16,2,8,512]{3,2,1,0:T(8,128)(2,1)S(1)}, s32[3,16]{1,0:T(4,128)S(1)}) custom-call(s32[16,16]{1,0:T(8,128)} %tally_ref.1, s32[1,256]{1,0:T(1,128)} %select_ref.1, bf16[1024,512]{1,0:T(8,128)(2,1)} %rows_ref.1), custom_call_target="tpu_custom_call" | custom-call | tf_op jit(solution)/shard_map/pick/pallas_call | solution.py:359
  1.7 14.9 %all_to_all.15.in_ref = bf16[16,2,8,512]{3,2,1,0:T(8,128)(2,1)S(1)} all-to-all(bf16[16,2,8,512]{3,2,1,0:T(8,128)(2,1)S(1)} %get-tuple-element.17), channel_id=1, replica_groups=mesh['seq'=16,'mp'=8] {'seq'}, dimensions={0} | all-to-all | bytes 524288 | tf_op jit(solution)/shard_map/all_to_all | solution.py:373
  16.6 0.6 compact.1.refs_3_.refs_0_
  17.2 3.7 %collective-permute-start.3 = (bf16[128,512]{1,0:T(8,128)(2,1)S(1)}, bf16[128,512]{1,0:T(8,128)(2,1)S(1)}, u32[]{:S(2)}, u32[]{:S(2)}) collective-permute-start(bf16[128,512]{1,0:T(8,128)(2,1)S(1)} %compact.1.refs_3_.refs_0_), channel_id=1, source_target_pairs={{0,4},{1,5},{2,6},{3,7},{4,0},{5,1},{6,2},{7,3},{8,12},{9,13},{10,... | collective-permute-start | bytes 393224 | tf_op jit(solution)/shard_map/ppermute | solution.py:312
  20.9 0.7 collective-permute-start.1
  21.7 1.9 %collective-permute-start.5 = (bf16[128,512]{1,0:T(8,128)(2,1)S(1)}, bf16[128,512]{1,0:T(8,128)(2,1)S(1)}, u32[]{:S(2)}, u32[]{:S(2)}) collective-permute-start(bf16[128,512]{1,0:T(8,128)(2,1)S(1)} %compact.1.refs_3_.refs_0_), channel_id=1, source_target_pairs={{0,6},{1,7},{2,0},{3,1},{4,2},{5,3},{6,4},{7,5},{8,14},{9,15},{10,... | collective-permute-start | bytes 393224 | tf_op jit(solution)/shard_map/ppermute | solution.py:312
  23.6 2.9 %collective-permute-start = (bf16[128,512]{1,0:T(8,128)(2,1)S(1)}, bf16[128,512]{1,0:T(8,128)(2,1)S(1)}, u32[]{:S(2)}, u32[]{:S(2)}) collective-permute-start(bf16[128,512]{1,0:T(8,128)(2,1)S(1)} %compact.1.refs_3_.refs_0_), channel_id=1, source_target_pairs={{0,1},{1,0},{2,3},{3,2},{4,5},{5,4},{6,7},{7,6},{8,9},{9,8},{10,11... | collective-permute-start | bytes 393224 | tf_op jit(solution)/shard_map/ppermute | solution.py:316
  26.5 3.9 %load_in.1 = (bf16[4096,1024]{1,0:T(8,128)(2,1)S(1)}, bf16[4096,128]{1,0:T(8,128)(2,1)S(1)}, bf16[4096,128]{1,0:T(8,128)(2,1)S(1)}, f32[8,128]{1,0:T(8,128)S(1)}) custom-call(bf16[4096,1024]{1,0:T(8,128)(2,1)} %refs_0_.2, bf16[4096,128]{1,0:T(8,128)(2,1)} %refs_1_.1, bf16[4096,128]{1,0:T(8,128)(2,1)} %refs_2_.1, bf16[128,512]{1,0:T(8,128)(2,1)S(1)} %compact.1.refs_3_.refs_0_), custom_call_target="tpu_custom_call" | custom-call | bytes 10485760 | tf_op jit(solution)/shard_map/load_in/pallas_call | solution.py:116
  30.5 0.0 copy-start.5
  30.5 0.0 collective-permute-done.3.refs_4_
  30.5 0.1 collective-permute-start.4
  30.6 0.0 collective-permute-done.1.refs_2_
  30.6 0.5 collective-permute-start.2
  31.1 0.0 collective-permute-done.5.in_ref.refs_6_
  31.1 0.2 collective-permute-start.6
  31.3 0.0 collective-permute-done.refs_1_
  31.3 0.6 collective-permute-done.4.refs_5_
  31.9 0.2 collective-permute-done.2.refs_3_
  32.1 0.4 collective-permute-done.6.refs_7_
  32.5 0.0 copy-done.2
  32.5 2.2 %project_in.1 = (bf16[128,1024]{1,0:T(8,128)(2,1)S(1)}, bf16[16,128,256]{2,1,0:T(8,128)(2,1)S(1)}) custom-call(bf16[32,128]{1,0:T(8,128)(2,1)S(1)} %bitcast.2, bf16[4096,1024]{1,0:T(8,128)(2,1)S(1)} %get-tuple-element.18.query_weight_ref, bf16[4096,128]{1,0:T(8,128)(2,1)S(1)} %get-tuple-element.19.keys_ref, ...), custom_call_target="tpu_custom_call" | custom-call | flops 1342177280 | bytes 4194304 | tf_op jit(solution)/shard_map/project_in/pallas_call | solution.py:389
  34.7 0.0 copy-start.3
  34.7 19.2 %all_to_all.16.pair_ref = bf16[16,128,256]{2,1,0:T(8,128)(2,1)S(1)} all-to-all(bf16[16,128,256]{2,1,0:T(8,128)(2,1)S(1)} %get-tuple-element.23), channel_id=1, replica_groups=mesh['seq'=16,'mp'=8] {'seq'}, dimensions={0} | all-to-all | bytes 2097152 | tf_op jit(solution)/shard_map/all_to_all | solution.py:408
  53.9 2.7 %attend.1.refs_1_.refs_8_ = bf16[128,1024]{1,0:T(8,128)(2,1)S(1)} custom-call(f32[8]{0:T(128)S(1)} %copy-done.5, bf16[128,1024]{1,0:T(8,128)(2,1)S(1)} %get-tuple-element.22.query_ref, bf16[16,128,256]{2,1,0:T(8,128)(2,1)S(1)} %all_to_all.16.pair_ref), custom_call_target="tpu_custom_call" | custom-call | tf_op jit(solution)/shard_map/attend/pallas_call | solution.py:410
  56.6 0.1 collective-permute-start.10
  56.7 1.4 %collective-permute-start.8 = (bf16[128,1024]{1,0:T(8,128)(2,1)S(1)}, bf16[128,1024]{1,0:T(8,128)(2,1)S(1)}, u32[]{:S(2)}, u32[]{:S(2)}) collective-permute-start(bf16[128,1024]{1,0:T(8,128)(2,1)S(1)} %attend.1.refs_1_.refs_8_), channel_id=1, source_target_pairs={{0,2},{1,3},{2,4},{3,5},{4,6},{5,7},{6,0},{7,1},{8,10},{9,11},{10,... | collective-permute-start | bytes 786440 | tf_op jit(solution)/shard_map/ppermute | solution.py:312
  58.0 2.3 %collective-permute-start.7 = (bf16[128,1024]{1,0:T(8,128)(2,1)S(1)}, bf16[128,1024]{1,0:T(8,128)(2,1)S(1)}, u32[]{:S(2)}, u32[]{:S(2)}) collective-permute-start(bf16[128,1024]{1,0:T(8,128)(2,1)S(1)} %attend.1.refs_1_.refs_8_), channel_id=1, source_target_pairs={{0,1},{1,0},{2,3},{3,2},{4,5},{5,4},{6,7},{7,6},{8,9},{9,8},{10,11... | collective-permute-start | bytes 786440 | tf_op jit(solution)/shard_map/ppermute | solution.py:316
  60.3 1.0 %collective-permute-start.12 = (bf16[128,1024]{1,0:T(8,128)(2,1)S(1)}, bf16[128,1024]{1,0:T(8,128)(2,1)S(1)}, u32[]{:S(2)}, u32[]{:S(2)}) collective-permute-start(bf16[128,1024]{1,0:T(8,128)(2,1)S(1)} %attend.1.refs_1_.refs_8_), channel_id=1, source_target_pairs={{0,6},{1,7},{2,0},{3,1},{4,2},{5,3},{6,4},{7,5},{8,14},{9,15},{10,... | collective-permute-start | bytes 786440 | tf_op jit(solution)/shard_map/ppermute | solution.py:312
  61.4 4.0 %load_out.1 = (bf16[8192,512]{1,0:T(8,128)(2,1)S(1)}, f32[8,128]{1,0:T(8,128)}) custom-call(bf16[8192,512]{1,0:T(8,128)(2,1)} %refs_0_.3, bf16[128,1024]{1,0:T(8,128)(2,1)S(1)} %attend.1.refs_1_.refs_8_), custom_call_target="tpu_custom_call" | custom-call | bytes 8388608 | tf_op jit(solution)/shard_map/load_out/pallas_call | solution.py:116
  65.4 0.0 collective-permute-done.10.refs_2_
  65.4 3.6 %collective-permute-start.11 = (bf16[128,1024]{1,0:T(8,128)(2,1)S(1)}, bf16[128,1024]{1,0:T(8,128)(2,1)S(1)}, u32[]{:S(2)}, u32[]{:S(2)}) collective-permute-start(bf16[128,1024]{1,0:T(8,128)(2,1)S(1)} %collective-permute-done.10.refs_2_), channel_id=1, source_target_pairs={{0,1},{1,0},{2,3},{3,2},{4,5},{5,4},{6,7},{7,6},{8,9},{9,8},{10,11... | collective-permute-start | bytes 786440 | tf_op jit(solution)/shard_map/ppermute | solution.py:316
  69.0 2.6 %collective-permute-done.8.refs_0_ = bf16[128,1024]{1,0:T(8,128)(2,1)S(1)} collective-permute-done((bf16[128,1024]{1,0:T(8,128)(2,1)S(1)}, bf16[128,1024]{1,0:T(8,128)(2,1)S(1)}, u32[]{:S(2)}, u32[]{:S(2)}) %collective-permute-start.8) | collective-permute-done | bytes 262176 | tf_op jit(solution)/shard_map/ppermute | solution.py:312
  71.6 0.7 collective-permute-start.9
  72.3 0.0 collective-permute-done.7.refs_9_
  72.3 0.5 project_early.1
  72.8 0.0 collective-permute-done.12.refs_4_.in_ref
  72.9 0.0 copy-start
  72.9 0.0 copy-start.1
  72.9 0.0 copy-start.4
  72.9 0.1 collective-permute-start.13
  73.0 0.0 collective-permute-done.11.refs_3_
  73.0 0.4 collective-permute-done.9.refs_1_
  73.4 0.8 project_middle.1.total_ref
  74.3 0.2 collective-permute-done.13.refs_0_
  74.5 0.9 %project_last.1 = bf16[16,2,8,512]{3,2,1,0:T(8,128)(2,1)S(1)} custom-call(s32[3,16]{1,0:T(4,128)S(1)} %get-tuple-element.16.table_ref, f32[128,128]{1,0:T(8,128)S(1)} %get-tuple-element.25.gate_ref, f32[128,512]{1,0:T(8,128)S(1)} %project_middle.1.total_ref, bf16[8192,512]{1,0:T(8,128)(2,1)S(1)} %get-tuple-element.24.weight_ref, ...), custom_call_target="tpu_custom_call" | custom-call | tf_op jit(solution)/shard_map/project_last/pallas_call | solution.py:439
  75.5 11.4 %all_to_all.17.back_ref = bf16[16,2,8,512]{3,2,1,0:T(8,128)(2,1)S(1)} all-to-all(bf16[16,2,8,512]{3,2,1,0:T(8,128)(2,1)S(1)} %project_last.1), channel_id=1, replica_groups=mesh['seq'=16,'mp'=8] {'seq'}, dimensions={0} | all-to-all | bytes 524288 | tf_op jit(solution)/shard_map/all_to_all | solution.py:448
  86.9 0.0 copy-done.1
  86.9 1.4 %blend.1 = bf16[1024,512]{1,0:T(8,128)(2,1)} custom-call(s32[16,16]{1,0:T(8,128)S(1)} %copy-done.1, s32[1,256]{1,0:T(1,128)S(1)} %copy-done.4, bf16[1024,512]{1,0:T(8,128)(2,1)S(1)} %copy-done, bf16[16,2,8,512]{3,2,1,0:T(8,128)(2,1)S(1)} %all_to_all.17.back_ref), custom_call_target="tpu_custom_call" | custom-call | tf_op jit(solution)/shard_map/blend/pallas_call | solution.py:449
  (7 shorter events, 0.1 us)
Async XLA Ops:
  0.0 32.5 %copy-start.2 = (bf16[4096]{0:T(1024)(128)(2,1)S(1)}, bf16[4096]{0:T(1024)(128)(2,1)}, u32[]{:S(2)}) copy-start(bf16[4096]{0:T(1024)(128)(2,1)} %param.11) | copy-start | bytes 24580
  17.2 13.3 %collective-permute-start.3 = (bf16[128,512]{1,0:T(8,128)(2,1)S(1)}, bf16[128,512]{1,0:T(8,128)(2,1)S(1)}, u32[]{:S(2)}, u32[]{:S(2)}) collective-permute-start(bf16[128,512]{1,0:T(8,128)(2,1)S(1)} %compact.1.refs_3_.refs_0_), channel_id=1, source_target_pairs={{0,4},{1,5},{2,6},{3,7},{4,0},{5,1},{6,2},{7,3},{8,12},{9,13},{10,... | collective-permute-start | bytes 393224 | tf_op jit(solution)/shard_map/ppermute | solution.py:312
  20.9 9.7 %collective-permute-start.1 = (bf16[128,512]{1,0:T(8,128)(2,1)S(1)}, bf16[128,512]{1,0:T(8,128)(2,1)S(1)}, u32[]{:S(2)}, u32[]{:S(2)}) collective-permute-start(bf16[128,512]{1,0:T(8,128)(2,1)S(1)} %compact.1.refs_3_.refs_0_), channel_id=1, source_target_pairs={{0,2},{1,3},{2,4},{3,5},{4,6},{5,7},{6,0},{7,1},{8,10},{9,11},{10,... | collective-permute-start | bytes 393224 | tf_op jit(solution)/shard_map/ppermute | solution.py:312
  21.7 9.4 %collective-permute-start.5 = (bf16[128,512]{1,0:T(8,128)(2,1)S(1)}, bf16[128,512]{1,0:T(8,128)(2,1)S(1)}, u32[]{:S(2)}, u32[]{:S(2)}) collective-permute-start(bf16[128,512]{1,0:T(8,128)(2,1)S(1)} %compact.1.refs_3_.refs_0_), channel_id=1, source_target_pairs={{0,6},{1,7},{2,0},{3,1},{4,2},{5,3},{6,4},{7,5},{8,14},{9,15},{10,... | collective-permute-start | bytes 393224 | tf_op jit(solution)/shard_map/ppermute | solution.py:312
  23.6 7.7 %collective-permute-start = (bf16[128,512]{1,0:T(8,128)(2,1)S(1)}, bf16[128,512]{1,0:T(8,128)(2,1)S(1)}, u32[]{:S(2)}, u32[]{:S(2)}) collective-permute-start(bf16[128,512]{1,0:T(8,128)(2,1)S(1)} %compact.1.refs_3_.refs_0_), channel_id=1, source_target_pairs={{0,1},{1,0},{2,3},{3,2},{4,5},{5,4},{6,7},{7,6},{8,9},{9,8},{10,11... | collective-permute-start | bytes 393224 | tf_op jit(solution)/shard_map/ppermute | solution.py:316
  30.5 23.4 %copy-start.5 = (f32[8]{0:T(128)S(1)}, f32[8]{0:T(128)}, u32[]{:S(2)}) copy-start(f32[8]{0:T(128)} %sharp_ref.1) | copy-start | bytes 100
  30.5 1.4 %collective-permute-start.4 = (bf16[128,512]{1,0:T(8,128)(2,1)S(1)}, bf16[128,512]{1,0:T(8,128)(2,1)S(1)}, u32[]{:S(2)}, u32[]{:S(2)}) collective-permute-start(bf16[128,512]{1,0:T(8,128)(2,1)S(1)} %collective-permute-done.3.refs_4_), channel_id=1, source_target_pairs={{0,1},{1,0},{2,3},{3,2},{4,5},{5,4},{6,7},{7,6},{8,9},{9,8},{10,11... | collective-permute-start | bytes 393224 | tf_op jit(solution)/shard_map/ppermute | solution.py:316
  30.6 1.5 %collective-permute-start.2 = (bf16[128,512]{1,0:T(8,128)(2,1)S(1)}, bf16[128,512]{1,0:T(8,128)(2,1)S(1)}, u32[]{:S(2)}, u32[]{:S(2)}) collective-permute-start(bf16[128,512]{1,0:T(8,128)(2,1)S(1)} %collective-permute-done.1.refs_2_), channel_id=1, source_target_pairs={{0,1},{1,0},{2,3},{3,2},{4,5},{5,4},{6,7},{7,6},{8,9},{9,8},{10,11... | collective-permute-start | bytes 393224 | tf_op jit(solution)/shard_map/ppermute | solution.py:316
  31.1 1.4 %collective-permute-start.6 = (bf16[128,512]{1,0:T(8,128)(2,1)S(1)}, bf16[128,512]{1,0:T(8,128)(2,1)S(1)}, u32[]{:S(2)}, u32[]{:S(2)}) collective-permute-start(bf16[128,512]{1,0:T(8,128)(2,1)S(1)} %hand_on.2), channel_id=1, source_target_pairs={{0,1},{1,0},{2,3},{3,2},{4,5},{5,4},{6,7},{7,6},{8,9},{9,8},{10,11... | collective-permute-start | bytes 393224 | tf_op jit(solution)/shard_map/ppermute | solution.py:316
  34.7 37.6 %copy-start.3 = (bf16[4096]{0:T(1024)(128)(2,1)S(1)}, bf16[4096]{0:T(1024)(128)(2,1)}, u32[]{:S(2)}) copy-start(bf16[4096]{0:T(1024)(128)(2,1)} %param.12) | copy-start | bytes 24580
  56.6 8.8 %collective-permute-start.10 = (bf16[128,1024]{1,0:T(8,128)(2,1)S(1)}, bf16[128,1024]{1,0:T(8,128)(2,1)S(1)}, u32[]{:S(2)}, u32[]{:S(2)}) collective-permute-start(bf16[128,1024]{1,0:T(8,128)(2,1)S(1)} %attend.1.refs_1_.refs_8_), channel_id=1, source_target_pairs={{0,4},{1,5},{2,6},{3,7},{4,0},{5,1},{6,2},{7,3},{8,12},{9,13},{10,... | collective-permute-start | bytes 786440 | tf_op jit(solution)/shard_map/ppermute | solution.py:312
  56.7 14.9 %collective-permute-start.8 = (bf16[128,1024]{1,0:T(8,128)(2,1)S(1)}, bf16[128,1024]{1,0:T(8,128)(2,1)S(1)}, u32[]{:S(2)}, u32[]{:S(2)}) collective-permute-start(bf16[128,1024]{1,0:T(8,128)(2,1)S(1)} %attend.1.refs_1_.refs_8_), channel_id=1, source_target_pairs={{0,2},{1,3},{2,4},{3,5},{4,6},{5,7},{6,0},{7,1},{8,10},{9,11},{10,... | collective-permute-start | bytes 786440 | tf_op jit(solution)/shard_map/ppermute | solution.py:312
  58.0 14.3 %collective-permute-start.7 = (bf16[128,1024]{1,0:T(8,128)(2,1)S(1)}, bf16[128,1024]{1,0:T(8,128)(2,1)S(1)}, u32[]{:S(2)}, u32[]{:S(2)}) collective-permute-start(bf16[128,1024]{1,0:T(8,128)(2,1)S(1)} %attend.1.refs_1_.refs_8_), channel_id=1, source_target_pairs={{0,1},{1,0},{2,3},{3,2},{4,5},{5,4},{6,7},{7,6},{8,9},{9,8},{10,11... | collective-permute-start | bytes 786440 | tf_op jit(solution)/shard_map/ppermute | solution.py:316
  60.3 12.5 %collective-permute-start.12 = (bf16[128,1024]{1,0:T(8,128)(2,1)S(1)}, bf16[128,1024]{1,0:T(8,128)(2,1)S(1)}, u32[]{:S(2)}, u32[]{:S(2)}) collective-permute-start(bf16[128,1024]{1,0:T(8,128)(2,1)S(1)} %attend.1.refs_1_.refs_8_), channel_id=1, source_target_pairs={{0,6},{1,7},{2,0},{3,1},{4,2},{5,3},{6,4},{7,5},{8,14},{9,15},{10,... | collective-permute-start | bytes 786440 | tf_op jit(solution)/shard_map/ppermute | solution.py:312
  65.4 7.7 %collective-permute-start.11 = (bf16[128,1024]{1,0:T(8,128)(2,1)S(1)}, bf16[128,1024]{1,0:T(8,128)(2,1)S(1)}, u32[]{:S(2)}, u32[]{:S(2)}) collective-permute-start(bf16[128,1024]{1,0:T(8,128)(2,1)S(1)} %collective-permute-done.10.refs_2_), channel_id=1, source_target_pairs={{0,1},{1,0},{2,3},{3,2},{4,5},{5,4},{6,7},{7,6},{8,9},{9,8},{10,11... | collective-permute-start | bytes 786440 | tf_op jit(solution)/shard_map/ppermute | solution.py:316
  71.6 1.9 %collective-permute-start.9 = (bf16[128,1024]{1,0:T(8,128)(2,1)S(1)}, bf16[128,1024]{1,0:T(8,128)(2,1)S(1)}, u32[]{:S(2)}, u32[]{:S(2)}) collective-permute-start(bf16[128,1024]{1,0:T(8,128)(2,1)S(1)} %collective-permute-done.8.refs_0_), channel_id=1, source_target_pairs={{0,1},{1,0},{2,3},{3,2},{4,5},{5,4},{6,7},{7,6},{8,9},{9,8},{10,11... | collective-permute-start | bytes 786440 | tf_op jit(solution)/shard_map/ppermute | solution.py:316
  72.9 14.0 %copy-start = (bf16[1024,512]{1,0:T(8,128)(2,1)S(1)}, bf16[1024,512]{1,0:T(8,128)(2,1)}, u32[]{:S(2)}) copy-start(bf16[1024,512]{1,0:T(8,128)(2,1)} %rows_ref.1) | copy-start | bytes 3145732
  72.9 14.0 %copy-start.1 = (s32[16,16]{1,0:T(8,128)S(1)}, s32[16,16]{1,0:T(8,128)}, u32[]{:S(2)}) copy-start(s32[16,16]{1,0:T(8,128)} %tally_ref.1) | copy-start | bytes 3076
  72.9 14.0 %copy-start.4 = (s32[1,256]{1,0:T(1,128)S(1)}, s32[1,256]{1,0:T(1,128)}, u32[]{:S(2)}) copy-start(s32[1,256]{1,0:T(1,128)} %select_ref.1) | copy-start | bytes 3076
  72.9 1.6 %collective-permute-start.13 = (bf16[128,1024]{1,0:T(8,128)(2,1)S(1)}, bf16[128,1024]{1,0:T(8,128)(2,1)S(1)}, u32[]{:S(2)}, u32[]{:S(2)}) collective-permute-start(bf16[128,1024]{1,0:T(8,128)(2,1)S(1)} %hand_on.3), channel_id=1, source_target_pairs={{0,1},{1,0},{2,3},{3,2},{4,5},{5,4},{6,7},{7,6},{8,9},{9,8},{10,11... | collective-permute-start | bytes 786440 | tf_op jit(solution)/shard_map/ppermute | solution.py:316

commit v5 on v4

--- a/solution.py
+++ b/solution.py
@@ -57,7 +57,9 @@
     return jnp.concatenate([start_across, source, jnp.right_shift(block - begin, 4)], axis=0)
 
 
-def pick_kernel(tally_hbm, select_hbm, rows_hbm, out_ref, table_ref, tally_ref, select_ref, rows_ref, sems):
+def pick_kernel(
+    tally_hbm, select_hbm, rows_hbm, sharp_hbm, out_ref, table_out, sharp_out, table_ref, tally_ref, select_ref, rows_ref, sems
+):
     parts = rows_ref.shape[0]
     wide = SRC // parts
     copies = [
@@ -67,6 +69,7 @@
         pltpu.make_async_copy(rows_hbm.at[pl.ds(wide * p, wide), :], rows_ref.at[p], sems.at[p])
         for p in range(parts)
     ]
+    copies.append(pltpu.make_async_copy(sharp_hbm, sharp_out, sems.at[parts + 3]))
     for copy in copies:
         copy.start()
     copies[0].wait()
@@ -75,6 +78,8 @@
     shard = lax.axis_index("seq")
     first, count = own_span(tally, shard)
     table_ref[...] = deal(tally, shard)
+    dealt = pltpu.make_async_copy(table_ref, table_out, sems.at[parts + 2])
+    dealt.start()
     listed = select_ref[...]
     slot = lax.broadcasted_iota(jnp.int32, (1, SLOTS), 1)
     listed = jnp.where(slot < count, listed, -1).astype(F32)
@@ -91,38 +96,38 @@
     for j in range(SLOTS // BLOCK):
         owner = lax.rem(first + j, NSEQ)
         out_ref[owner, j // NSEQ] = picked[BLOCK * j : BLOCK * (j + 1)].astype(BF16)
-
-
-def load_kernel(count, *refs):
-    sources, targets, done_ref, sems = refs[:count], refs[-2 - count : -2], refs[-2], refs[-1]
-    copies = [pltpu.make_async_copy(a, b, sems.at[k]) for k, (a, b) in enumerate(zip(sources, targets))]
+    dealt.wait()
+    copies[-1].wait()
+
+
+def in_hbm(array):
+    return pltpu.with_memory_space_constraint(array, pltpu.HBM)
+
+
+def block_rows(k, wide):
+    return pl.ds(pl.multiple_of(block_of(k) * wide, wide), wide)
+
+
+def fetch(source, target, sems, first, parts):
+    wide = source.shape[0] // parts
+    copies = [
+        pltpu.make_async_copy(
+            source.at[pl.ds(wide * p, wide), :], target.at[pl.ds(wide * p, wide), :], sems.at[first + p]
+        )
+        for p in range(parts)
+    ]
     for copy in copies:
         copy.start()
+    return copies
+
+
+def load_in_kernel(keys_hbm, values_hbm, query_hbm, after_ref, keys_ref, values_ref, query_ref, done_ref, sems):
+    copies = fetch(keys_hbm, keys_ref, sems, 0, 2)
+    copies += fetch(values_hbm, values_ref, sems, 2, 2)
+    copies += fetch(query_hbm, query_ref, sems, 4, 8)
+    done_ref[...] = jnp.zeros_like(done_ref)
     for copy in copies:
         copy.wait()
-    done_ref[...] = jnp.zeros_like(done_ref)
-
-
-def in_hbm(array):
-    return pltpu.with_memory_space_constraint(array, pltpu.HBM)
-
-
-def in_vmem(array):
-    return pltpu.with_memory_space_constraint(array, pltpu.VMEM)
-
-
-def load(arrays, after, name):
-    count = len(arrays)
-    return pl.pallas_call(
-        functools.partial(load_kernel, count),
-        out_shape=[pltpu.VMEM(a.shape, a.dtype) for a in arrays] + [pltpu.VMEM((8, 128), F32)],
-        in_specs=[HBM] * count + [ANY],
-        out_specs=[VMEM] * (count + 1),
-        scratch_shapes=[pltpu.SemaphoreType.DMA((count,))],
-        compiler_params=params(8),
-        cost_estimate=cost(0, sum(a.size for a in arrays) * 2),
-        name=name,
-    )(*map(in_hbm, arrays), after)
 
 
 def compact_kernel(table_ref, in_ref, out_ref):
@@ -162,7 +167,7 @@
     values = jnp.zeros((OWNED, HEAD), F32)
     for k in range(NMP):
         m = block_of(k)
-        rows = pl.ds(pl.multiple_of(m * FEAT, FEAT), FEAT)
+        rows = block_rows(k, FEAT)
         gain = gain_ref[m]
         normed = jnp.concatenate(
             [
@@ -239,20 +244,22 @@
             ]
 
 
-EARLY, MIDDLE, LAST = (0, 1), (2, 3, 4, 5, 6), (7,)
+MIDDLE, LAST = (1, 2, 3, 4, 5, 6), (7,)
 
 
 def head_sum(which, weight_ref, blocks):
     wide = GROUP * HEAD
     total = jnp.zeros((OWNED, FEAT), F32)
     for k, block in zip(which, blocks):
-        rows = pl.ds(pl.multiple_of(block_of(k) * wide, wide), wide)
-        total = total + jnp.dot(block[...], weight_ref[rows, :], preferred_element_type=F32)
+        total = total + jnp.dot(
+            block[...], weight_ref[block_rows(k, wide), :], preferred_element_type=F32
+        )
     return total
 
 
-def project_early_kernel(weight_ref, gate_in, *refs):
-    tokens, heads, (total_ref, gate_ref, gate_weight_ref) = refs[:NMP], refs[NMP:-3], refs[-3:]
+def load_out_kernel(weight_hbm, tally_ref, select_ref, gate_in, own_ref, *refs):
+    tokens, (weight_ref, total_ref, gate_ref, hot_ref, gate_weight_ref, sems) = refs[:NMP], refs[NMP:]
+    copies = fetch(weight_hbm, weight_ref, sems, 0, 8)
     spread(gate_in, gate_weight_ref)
     routed = jnp.zeros((OWNED, 128), F32)
     for k in range(NMP):
@@ -262,7 +269,14 @@
     gate_ref[...] = jnp.broadcast_to(
         jax.nn.sigmoid(jnp.sum(routed, axis=1, keepdims=True)), (OWNED, 128)
     )
-    total_ref[...] = head_sum(EARLY, weight_ref, heads)
+    first, count = own_span(tally_ref[...], lax.axis_index("seq"))
+    slot = lax.broadcasted_iota(jnp.int32, (1, SLOTS), 1)
+    listed = jnp.where(slot < count, select_ref[...], -1)
+    token = lax.broadcasted_iota(jnp.int32, (SRC, 1), 0)
+    hot_ref[...] = (listed == token).astype(F32).astype(BF16)
+    for copy in copies:
+        copy.wait()
+    total_ref[...] = head_sum((0,), weight_ref, (own_ref,))
 
 
 def project_middle_kernel(total_in, weight_ref, *refs):
@@ -283,23 +297,19 @@
             out_ref[s, half] = delta_ref[place].astype(BF16)
 
 
-def blend_kernel(tally_ref, select_ref, rows_ref, back_ref, out_hbm, update_ref, out_ref, sems):
-    first, count = own_span(tally_ref[...], lax.axis_index("seq"))
+def blend_kernel(table_ref, hot_ref, rows_ref, back_ref, out_hbm, update_ref, out_ref, sems):
+    first = table_ref[0, lax.axis_index("seq")]
     for j in range(0, SLOTS // BLOCK, 2):
         pair = [
             back_ref[lax.rem(first + k, NSEQ), k // NSEQ].astype(F32) for k in (j, j + 1)
         ]
         update_ref[BLOCK * j : BLOCK * (j + 2)] = jnp.concatenate(pair, axis=0).astype(BF16)
-    slot = lax.broadcasted_iota(jnp.int32, (1, SLOTS), 1)
-    listed = jnp.where(slot < count, select_ref[...], -1)
     parts = out_ref.shape[0]
     wide = SRC // parts
-    token = lax.broadcasted_iota(jnp.int32, (wide, 1), 0)
     copies = []
     for p in range(parts):
         here = slice(wide * p, wide * (p + 1))
-        hot = (listed == token + wide * p).astype(F32).astype(BF16)
-        added = jnp.dot(hot, update_ref[...], preferred_element_type=F32)
+        added = jnp.dot(hot_ref[here], update_ref[...], preferred_element_type=F32)
         out_ref[p] = (rows_ref[here].astype(F32) + added).astype(BF16)
         copies.append(pltpu.make_async_copy(out_ref.at[p], out_hbm.at[pl.ds(wide * p, wide), :], sems.at[p]))
         copies[p].start()
@@ -356,20 +366,30 @@
     selection_table,
     dispatched_tally_table,
 ):
-    outgoing, table = pl.pallas_call(
+    outgoing, table, sharpness = pl.pallas_call(
         pick_kernel,
-        out_shape=(pltpu.VMEM((NSEQ, 2, BLOCK, FEAT), BF16), shape((3, NSEQ), jnp.int32)),
-        in_specs=[HBM] * 3,
-        out_specs=(VMEM, VMEM),
+        out_shape=(
+            pltpu.VMEM((NSEQ, 2, BLOCK, FEAT), BF16),
+            pltpu.SMEM((3, NSEQ), jnp.int32),
+            pltpu.SMEM((GROUP,), F32),
+        ),
+        in_specs=[HBM] * 4,
+        out_specs=(VMEM, SMEM, SMEM),
         scratch_shapes=[
+            pltpu.VMEM((3, NSEQ), jnp.int32),
             pltpu.VMEM((NSEQ, NSEQ), jnp.int32),
             pltpu.VMEM((1, SLOTS), jnp.int32),
             pltpu.VMEM((4, SRC // 4, FEAT), BF16),
-            pltpu.SemaphoreType.DMA((6,)),
+            pltpu.SemaphoreType.DMA((8,)),
         ],
         compiler_params=params(16),
         name="pick",
-    )(in_hbm(dispatched_tally_table), in_hbm(selection_table), in_hbm(residual_activations))
+    )(
+        in_hbm(dispatched_tally_table),
+        in_hbm(selection_table),
+        in_hbm(residual_activations),
+        in_hbm(logit_sharpness),
+    )
     incoming = lax.all_to_all(outgoing, "seq", split_axis=0, concat_axis=0, tiled=True)
     tokens = pl.pallas_call(
         compact_kernel,
@@ -379,9 +399,20 @@
         compiler_params=params(4),
         name="compact",
     )(table, incoming)
-    asker, lookup, content, loaded = load(
-        (asker_projection, lookup_projection, content_projection), tokens, "load_in"
-    )
+    lookup, content, asker, loaded = pl.pallas_call(
+        load_in_kernel,
+        out_shape=(
+            pltpu.VMEM((WIDTH, HEAD), BF16),
+            pltpu.VMEM((WIDTH, HEAD), BF16),
+            pltpu.VMEM((WIDTH, GROUP * HEAD), BF16),
+            pltpu.VMEM((8, 128), F32),
+        ),
+        in_specs=[HBM] * 3 + [ANY],
+        out_specs=[VMEM] * 4,
+        scratch_shapes=[pltpu.SemaphoreType.DMA((12,))],
+        compiler_params=params(8),
+        name="load_in",
+    )(in_hbm(lookup_projection), in_hbm(content_projection), in_hbm(asker_projection), tokens)
     blocks = z_blocks(tokens)
     blocks[1] = other_core(tokens)
     add_cores(blocks, loaded)
@@ -414,19 +445,30 @@
         out_specs=VMEM,
         compiler_params=params(24),
         name="attend",
-    )(logit_sharpness, query, pairs)
-    final, _ = load((final_projection,), attended, "load_out")
+    )(sharpness, query, pairs)
+    final, total, gate, hot = pl.pallas_call(
+        load_out_kernel,
+        out_shape=(
+            pltpu.VMEM((NMP * GROUP * HEAD, FEAT), BF16),
+            pltpu.VMEM((OWNED, FEAT), F32),
+            pltpu.VMEM((OWNED, 128), F32),
+            pltpu.VMEM((SRC, SLOTS), BF16),
+        ),
+        in_specs=[HBM] + [VMEM] * (4 + NMP),
+        out_specs=[VMEM] * 4,
+        scratch_shapes=[pltpu.VMEM((NMP, FEAT // 128, 128), F32), pltpu.SemaphoreType.DMA((8,))],
+        compiler_params=params(8),
+        name="load_out",
+    )(
+        in_hbm(final_projection),
+        dispatched_tally_table,
+        selection_table,
+        gating_projection.reshape(WIDTH // 128, 128),
+        attended,
+        *blocks,
+    )
     heads = z_blocks(attended)
     heads[1] = other_core(attended)
-    total, gate = pl.pallas_call(
-        project_early_kernel,
-        out_shape=(pltpu.VMEM((OWNED, FEAT), F32), pltpu.VMEM((OWNED, 128), F32)),
-        in_specs=[VMEM] * (2 + NMP + len(EARLY)),
-        out_specs=(VMEM, VMEM),
-        scratch_shapes=[pltpu.VMEM((NMP, FEAT // 128, 128), F32)],
-        compiler_params=params(16),
-        name="project_early",
-    )(final, gating_projection.reshape(WIDTH // 128, 128), *blocks, *(heads[k] for k in EARLY))
     add_cores(heads, total)
     total = pl.pallas_call(
         project_middle_kernel,
@@ -449,7 +491,7 @@
     return pl.pallas_call(
         blend_kernel,
         out_shape=shape((SRC, FEAT)),
-        in_specs=[VMEM] * 4,
+        in_specs=[SMEM] + [VMEM] * 3,
         out_specs=HBM,
         scratch_shapes=[
             pltpu.VMEM((SLOTS, FEAT), BF16),
@@ -458,7 +500,7 @@
         ],
         compiler_params=params(16),
         name="blend",
-    )(dispatched_tally_table, selection_table, residual_activations, back)
+    )(table, hot, residual_activations, back)
 
 
 def solution(mesh):

time: 88.6 us -> 86.6 us (0.977)
  Pallas kernels: 18.9 us -> 16.7 us
    pallas_call x4 -> x3, Pallas kernels: 9.9 us -> 9.35 us  [the longest x1 4.11 us: on_device(): pl.pallas_call(load_in_kernel, out_shape=(pltpu.VMEM((WIDTH, HEAD), BF16)...]
  transfers between devices with their start and end apart: 14 -> 14, of which waited for: 6 -> 5; matrix products, arithmetic and copies ran while one was open for 0% -> 0% of each run, Pallas kernels for 11% -> 11%
where the time goes in v5:
time: 86.6 us; the launch traced here: 86.3 us
  blocking collectives  45.2 us (52%)
  starting transfers between devices  19.2 us (22%)
  Pallas kernels  16.7 us (19%)
  waiting for transfers between devices  4.9 us (6%)
    all_to_all x1, blocking collectives, on_device(): pairs = lax.all_to_all(pair, 'seq', split_axis=0, concat_axis=0, tiled=True)  19.2 us
    all_to_all x1, blocking collectives, on_device(): lax.all_to_all(outgoing, 'seq', split_axis=0, concat_axis=0, tiled=True)  14.9 us
    all_to_all x1, blocking collectives, on_device(): lax.all_to_all(outgoing_back, 'seq', split_axis=0, concat_axis=0, tiled=T...  11.2 us
    ppermute x8, starting transfers between devices, other_core(): return lax.ppermute(array, 'mp', [(m, m ^ 1) for m in range(NMP)])  10 us
    ppermute x6, starting transfers between devices, z_step(): return lax.ppermute(array, 'mp', pairs)  9.19 us
    pallas_call x1, Pallas kernels, on_device(): pl.pallas_call(load_in_kernel, out_shape=(pltpu.VMEM((WIDTH, HEAD), BF16)...  4.11 us
    pallas_call x1, Pallas kernels, on_device(): pl.pallas_call(load_out_kernel, out_shape=(pltpu.VMEM((NMP * GROUP * HEAD...  3.98 us
    ppermute x6, waiting for transfers between devices, z_step(): return lax.ppermute(array, 'mp', pairs)  2.62 us
  transfers between devices with their start and end apart: 14, of which 5 were waited for; matrix products, arithmetic and copies ran while one was open for 0% of the time, Pallas kernels for 11%

profile of v5, /device:TPU:1, one launch (start us, length us, event | category | flops | bytes accessed | tf_op | source)
XLA Modules:
  0.0 86.3 jit_solution(13962115489584042175)
XLA Ops:
  0.0 0.0 copy-start.2
  0.0 1.7 %pick.1 = (bf16[16,2,8,512]{3,2,1,0:T(8,128)(2,1)S(1)}, s32[3,16]{1,0:T(4,128)S(4)}, f32[8]{0:T(128)S(4)}) custom-call(s32[16,16]{1,0:T(8,128)} %tally_ref.1, s32[1,256]{1,0:T(1,128)} %select_ref.1, bf16[1024,512]{1,0:T(8,128)(2,1)} %rows_ref.1, f32[8]{0:T(128)} %sharp_hbm.1), custom_call_target="tpu_custom_call" | custom-call | tf_op jit(solution)/shard_map/pick/pallas_call | solution.py:369
  1.7 14.9 %all_to_all.15.in_ref = bf16[16,2,8,512]{3,2,1,0:T(8,128)(2,1)S(1)} all-to-all(bf16[16,2,8,512]{3,2,1,0:T(8,128)(2,1)S(1)} %get-tuple-element.20), channel_id=1, replica_groups=mesh['seq'=16,'mp'=8] {'seq'}, dimensions={0} | all-to-all | bytes 524288 | tf_op jit(solution)/shard_map/all_to_all | solution.py:393
  16.7 3.7 %collective-permute-start.3 = (bf16[128,512]{1,0:T(8,128)(2,1)S(1)}, bf16[128,512]{1,0:T(8,128)(2,1)S(1)}, u32[]{:S(2)}, u32[]{:S(2)}) collective-permute-start(bf16[128,512]{1,0:T(8,128)(2,1)S(1)} %compact.1.after_ref.refs_0_), channel_id=1, source_target_pairs={{0,4},{1,5},{2,6},{3,7},{4,0},{5,1},{6,2},{7,3},{8,12},{9,13},{10,... | collective-permute-start | bytes 393224 | tf_op jit(solution)/shard_map/ppermute | solution.py:322
  20.4 0.7 collective-permute-start.1
  21.1 1.9 %collective-permute-start.5 = (bf16[128,512]{1,0:T(8,128)(2,1)S(1)}, bf16[128,512]{1,0:T(8,128)(2,1)S(1)}, u32[]{:S(2)}, u32[]{:S(2)}) collective-permute-start(bf16[128,512]{1,0:T(8,128)(2,1)S(1)} %compact.1.after_ref.refs_0_), channel_id=1, source_target_pairs={{0,6},{1,7},{2,0},{3,1},{4,2},{5,3},{6,4},{7,5},{8,14},{9,15},{10,... | collective-permute-start | bytes 393224 | tf_op jit(solution)/shard_map/ppermute | solution.py:322
  23.0 2.9 %collective-permute-start = (bf16[128,512]{1,0:T(8,128)(2,1)S(1)}, bf16[128,512]{1,0:T(8,128)(2,1)S(1)}, u32[]{:S(2)}, u32[]{:S(2)}) collective-permute-start(bf16[128,512]{1,0:T(8,128)(2,1)S(1)} %compact.1.after_ref.refs_0_), channel_id=1, source_target_pairs={{0,1},{1,0},{2,3},{3,2},{4,5},{5,4},{6,7},{7,6},{8,9},{9,8},{10,11... | collective-permute-start | bytes 393224 | tf_op jit(solution)/shard_map/ppermute | solution.py:326
  26.0 4.1 %load_in.1 = (bf16[4096,128]{1,0:T(8,128)(2,1)S(1)}, bf16[4096,128]{1,0:T(8,128)(2,1)S(1)}, bf16[4096,1024]{1,0:T(8,128)(2,1)S(1)}, f32[8,128]{1,0:T(8,128)S(1)}) custom-call(bf16[4096,128]{1,0:T(8,128)(2,1)} %keys_hbm.1, bf16[4096,128]{1,0:T(8,128)(2,1)} %values_hbm.1, bf16[4096,1024]{1,0:T(8,128)(2,1)} %query_hbm.1, ...), custom_call_target="tpu_custom_call" | custom-call | tf_op jit(solution)/shard_map/load_in/pallas_call | solution.py:402
  30.1 0.0 copy-start.1
  30.1 0.0 copy-start.3
  30.1 0.0 copy-start.4
  30.1 0.0 collective-permute-done.3.refs_4_
  30.2 0.1 collective-permute-start.4
  30.2 0.0 collective-permute-done.1.refs_2_
  30.3 0.5 collective-permute-start.2
  30.7 0.0 collective-permute-done.5.in_ref.refs_6_
  30.8 0.2 collective-permute-start.6
  30.9 0.0 collective-permute-done.refs_1_
  30.9 0.6 collective-permute-done.4.refs_5_
  31.6 0.2 collective-permute-done.2.refs_3_
  31.8 0.4 collective-permute-done.6.refs_7_
  32.2 0.0 copy-done.2
  32.2 2.2 %project_in.1 = (bf16[128,1024]{1,0:T(8,128)(2,1)S(1)}, bf16[16,128,256]{2,1,0:T(8,128)(2,1)S(1)}) custom-call(bf16[32,128]{1,0:T(8,128)(2,1)S(1)} %bitcast.2, bf16[4096,1024]{1,0:T(8,128)(2,1)S(1)} %get-tuple-element.21.query_weight_ref, bf16[4096,128]{1,0:T(8,128)(2,1)S(1)} %get-tuple-element.22.keys_ref, ...), custom_call_target="tpu_custom_call" | custom-call | flops 1342177280 | bytes 4194304 | tf_op jit(solution)/shard_map/project_in/pallas_call | solution.py:420
  34.4 19.2 %all_to_all.16.pair_ref = bf16[16,128,256]{2,1,0:T(8,128)(2,1)S(1)} all-to-all(bf16[16,128,256]{2,1,0:T(8,128)(2,1)S(1)} %get-tuple-element.26), channel_id=1, replica_groups=mesh['seq'=16,'mp'=8] {'seq'}, dimensions={0} | all-to-all | bytes 2097152 | tf_op jit(solution)/shard_map/all_to_all | solution.py:439
  53.5 2.1 %attend.1.own_ref = bf16[128,1024]{1,0:T(8,128)(2,1)S(1)} custom-call(f32[8]{0:T(128)S(4)} %get-tuple-element.19.sharp_ref, bf16[128,1024]{1,0:T(8,128)(2,1)S(1)} %get-tuple-element.25.query_ref, bf16[16,128,256]{2,1,0:T(8,128)(2,1)S(1)} %all_to_all.16.pair_ref), custom_call_target="tpu_custom_call" | custom-call | tf_op jit(solution)/shard_map/attend/pallas_call | solution.py:441
  55.6 0.1 collective-permute-start.10
  55.7 1.2 %collective-permute-start.8 = (bf16[128,1024]{1,0:T(8,128)(2,1)S(1)}, bf16[128,1024]{1,0:T(8,128)(2,1)S(1)}, u32[]{:S(2)}, u32[]{:S(2)}) collective-permute-start(bf16[128,1024]{1,0:T(8,128)(2,1)S(1)} %attend.1.own_ref), channel_id=1, source_target_pairs={{0,2},{1,3},{2,4},{3,5},{4,6},{5,7},{6,0},{7,1},{8,10},{9,11},{10,... | collective-permute-start | bytes 786440 | tf_op jit(solution)/shard_map/ppermute | solution.py:322
  56.9 1.6 %collective-permute-start.12 = (bf16[128,1024]{1,0:T(8,128)(2,1)S(1)}, bf16[128,1024]{1,0:T(8,128)(2,1)S(1)}, u32[]{:S(2)}, u32[]{:S(2)}) collective-permute-start(bf16[128,1024]{1,0:T(8,128)(2,1)S(1)} %attend.1.own_ref), channel_id=1, source_target_pairs={{0,6},{1,7},{2,0},{3,1},{4,2},{5,3},{6,4},{7,5},{8,14},{9,15},{10,... | collective-permute-start | bytes 786440 | tf_op jit(solution)/shard_map/ppermute | solution.py:322
  58.5 2.1 %collective-permute-start.7 = (bf16[128,1024]{1,0:T(8,128)(2,1)S(1)}, bf16[128,1024]{1,0:T(8,128)(2,1)S(1)}, u32[]{:S(2)}, u32[]{:S(2)}) collective-permute-start(bf16[128,1024]{1,0:T(8,128)(2,1)S(1)} %attend.1.own_ref), channel_id=1, source_target_pairs={{0,1},{1,0},{2,3},{3,2},{4,5},{5,4},{6,7},{7,6},{8,9},{9,8},{10,11... | collective-permute-start | bytes 786440 | tf_op jit(solution)/shard_map/ppermute | solution.py:326
  60.6 0.0 copy-done.1
  60.6 0.0 copy-done.3
  60.6 0.0 copy-done.4
  60.6 4.0 %load_out.1 = (bf16[8192,512]{1,0:T(8,128)(2,1)S(1)}, f32[128,512]{1,0:T(8,128)S(1)}, f32[128,128]{1,0:T(8,128)S(1)}, bf16[1024,256]{1,0:T(8,128)(2,1)S(1)}) custom-call(bf16[8192,512]{1,0:T(8,128)(2,1)} %weight_hbm.1, s32[16,16]{1,0:T(8,128)S(1)} %copy-done.1, s32[1,256]{1,0:T(1,128)S(1)} %copy-done.4, bf16[32,128]{1,0:T(8,128)(2,1)S(1)} %bitcast.3, ...), custom_call_target="tpu_custom_call" | custom-call | tf_op jit(solution)/shard_map/load_out/pallas_call | solution.py:449
  64.6 0.0 collective-permute-done.10.refs_3_
  64.6 3.4 %collective-permute-start.11 = (bf16[128,1024]{1,0:T(8,128)(2,1)S(1)}, bf16[128,1024]{1,0:T(8,128)(2,1)S(1)}, u32[]{:S(2)}, u32[]{:S(2)}) collective-permute-start(bf16[128,1024]{1,0:T(8,128)(2,1)S(1)} %collective-permute-done.10.refs_3_), channel_id=1, source_target_pairs={{0,1},{1,0},{2,3},{3,2},{4,5},{5,4},{6,7},{7,6},{8,9},{9,8},{10,11... | collective-permute-start | bytes 786440 | tf_op jit(solution)/shard_map/ppermute | solution.py:326
  68.0 2.6 %collective-permute-done.8.refs_1_ = bf16[128,1024]{1,0:T(8,128)(2,1)S(1)} collective-permute-done((bf16[128,1024]{1,0:T(8,128)(2,1)S(1)}, bf16[128,1024]{1,0:T(8,128)(2,1)S(1)}, u32[]{:S(2)}, u32[]{:S(2)}) %collective-permute-start.8) | collective-permute-done | bytes 262176 | tf_op jit(solution)/shard_map/ppermute | solution.py:322
  70.6 0.7 collective-permute-start.9
  71.3 0.0 collective-permute-done.12.refs_5_.in_ref
  71.4 0.1 collective-permute-start.13
  71.5 0.0 collective-permute-done.7.refs_0_
  71.5 0.0 collective-permute-done.11.refs_4_
  71.5 1.0 %collective-permute-done.9.refs_2_ = bf16[128,1024]{1,0:T(8,128)(2,1)S(1)} collective-permute-done((bf16[128,1024]{1,0:T(8,128)(2,1)S(1)}, bf16[128,1024]{1,0:T(8,128)(2,1)S(1)}, u32[]{:S(2)}, u32[]{:S(2)}) %collective-permute-start.9) | collective-permute-done | bytes 262176 | tf_op jit(solution)/shard_map/ppermute | solution.py:326
  72.5 1.0 %project_middle.1.total_ref = f32[128,512]{1,0:T(8,128)S(1)} custom-call(f32[128,512]{1,0:T(8,128)S(1)} %get-tuple-element.29.total_in.token_ref, bf16[8192,512]{1,0:T(8,128)(2,1)S(1)} %get-tuple-element.30.weight_ref, bf16[128,1024]{1,0:T(8,128)(2,1)S(1)} %collective-permute-done.7.refs_0_, bf16[128,1024]{1,0:T(8,128)(2,1)S(1)} %collective-permute-done.8.refs_1_, ...), custom_call_target="tpu_custom_call" | custom-call | tf_op jit(solution)/shard_map/project_middle/pallas_call | solution.py:473
  73.5 0.0 collective-permute-done.13.refs_0_
  73.5 0.4 project_last.1
  73.9 11.2 %all_to_all.17.back_ref = bf16[16,2,8,512]{3,2,1,0:T(8,128)(2,1)S(1)} all-to-all(bf16[16,2,8,512]{3,2,1,0:T(8,128)(2,1)S(1)} %project_last.1), channel_id=1, replica_groups=mesh['seq'=16,'mp'=8] {'seq'}, dimensions={0} | all-to-all | bytes 524288 | tf_op jit(solution)/shard_map/all_to_all | solution.py:490
  85.0 0.0 copy-done
  85.0 1.3 %blend.1 = bf16[1024,512]{1,0:T(8,128)(2,1)} custom-call(s32[3,16]{1,0:T(4,128)S(4)} %get-tuple-element.18.table_ref, bf16[1024,256]{1,0:T(8,128)(2,1)S(1)} %get-tuple-element.27.hot_ref, bf16[1024,512]{1,0:T(8,128)(2,1)S(1)} %copy-done, bf16[16,2,8,512]{3,2,1,0:T(8,128)(2,1)S(1)} %all_to_all.17.back_ref), custom_call_target="tpu_custom_call" | custom-call | tf_op jit(solution)/shard_map/blend/pallas_call | solution.py:491
  (4 shorter events, 0.1 us)
Async XLA Ops:
  0.0 32.2 %copy-start.2 = (bf16[4096]{0:T(1024)(128)(2,1)S(1)}, bf16[4096]{0:T(1024)(128)(2,1)}, u32[]{:S(2)}) copy-start(bf16[4096]{0:T(1024)(128)(2,1)} %param.11) | copy-start | bytes 24580
  16.7 13.5 %collective-permute-start.3 = (bf16[128,512]{1,0:T(8,128)(2,1)S(1)}, bf16[128,512]{1,0:T(8,128)(2,1)S(1)}, u32[]{:S(2)}, u32[]{:S(2)}) collective-permute-start(bf16[128,512]{1,0:T(8,128)(2,1)S(1)} %compact.1.after_ref.refs_0_), channel_id=1, source_target_pairs={{0,4},{1,5},{2,6},{3,7},{4,0},{5,1},{6,2},{7,3},{8,12},{9,13},{10,... | collective-permute-start | bytes 393224 | tf_op jit(solution)/shard_map/ppermute | solution.py:322
  20.4 9.9 %collective-permute-start.1 = (bf16[128,512]{1,0:T(8,128)(2,1)S(1)}, bf16[128,512]{1,0:T(8,128)(2,1)S(1)}, u32[]{:S(2)}, u32[]{:S(2)}) collective-permute-start(bf16[128,512]{1,0:T(8,128)(2,1)S(1)} %compact.1.after_ref.refs_0_), channel_id=1, source_target_pairs={{0,2},{1,3},{2,4},{3,5},{4,6},{5,7},{6,0},{7,1},{8,10},{9,11},{10,... | collective-permute-start | bytes 393224 | tf_op jit(solution)/shard_map/ppermute | solution.py:322
  21.1 9.6 %collective-permute-start.5 = (bf16[128,512]{1,0:T(8,128)(2,1)S(1)}, bf16[128,512]{1,0:T(8,128)(2,1)S(1)}, u32[]{:S(2)}, u32[]{:S(2)}) collective-permute-start(bf16[128,512]{1,0:T(8,128)(2,1)S(1)} %compact.1.after_ref.refs_0_), channel_id=1, source_target_pairs={{0,6},{1,7},{2,0},{3,1},{4,2},{5,3},{6,4},{7,5},{8,14},{9,15},{10,... | collective-permute-start | bytes 393224 | tf_op jit(solution)/shard_map/ppermute | solution.py:322
  23.0 7.9 %collective-permute-start = (bf16[128,512]{1,0:T(8,128)(2,1)S(1)}, bf16[128,512]{1,0:T(8,128)(2,1)S(1)}, u32[]{:S(2)}, u32[]{:S(2)}) collective-permute-start(bf16[128,512]{1,0:T(8,128)(2,1)S(1)} %compact.1.after_ref.refs_0_), channel_id=1, source_target_pairs={{0,1},{1,0},{2,3},{3,2},{4,5},{5,4},{6,7},{7,6},{8,9},{9,8},{10,11... | collective-permute-start | bytes 393224 | tf_op jit(solution)/shard_map/ppermute | solution.py:326
  30.1 30.5 %copy-start.1 = (s32[16,16]{1,0:T(8,128)S(1)}, s32[16,16]{1,0:T(8,128)}, u32[]{:S(2)}) copy-start(s32[16,16]{1,0:T(8,128)} %tally_ref.1) | copy-start | bytes 3076
  30.1 30.5 %copy-start.3 = (bf16[4096]{0:T(1024)(128)(2,1)S(1)}, bf16[4096]{0:T(1024)(128)(2,1)}, u32[]{:S(2)}) copy-start(bf16[4096]{0:T(1024)(128)(2,1)} %param.12) | copy-start | bytes 24580
  30.1 30.5 %copy-start.4 = (s32[1,256]{1,0:T(1,128)S(1)}, s32[1,256]{1,0:T(1,128)}, u32[]{:S(2)}) copy-start(s32[1,256]{1,0:T(1,128)} %select_ref.1) | copy-start | bytes 3076
  30.2 1.4 %collective-permute-start.4 = (bf16[128,512]{1,0:T(8,128)(2,1)S(1)}, bf16[128,512]{1,0:T(8,128)(2,1)S(1)}, u32[]{:S(2)}, u32[]{:S(2)}) collective-permute-start(bf16[128,512]{1,0:T(8,128)(2,1)S(1)} %collective-permute-done.3.refs_4_), channel_id=1, source_target_pairs={{0,1},{1,0},{2,3},{3,2},{4,5},{5,4},{6,7},{7,6},{8,9},{9,8},{10,11... | collective-permute-start | bytes 393224 | tf_op jit(solution)/shard_map/ppermute | solution.py:326
  30.3 1.5 %collective-permute-start.2 = (bf16[128,512]{1,0:T(8,128)(2,1)S(1)}, bf16[128,512]{1,0:T(8,128)(2,1)S(1)}, u32[]{:S(2)}, u32[]{:S(2)}) collective-permute-start(bf16[128,512]{1,0:T(8,128)(2,1)S(1)} %collective-permute-done.1.refs_2_), channel_id=1, source_target_pairs={{0,1},{1,0},{2,3},{3,2},{4,5},{5,4},{6,7},{7,6},{8,9},{9,8},{10,11... | collective-permute-start | bytes 393224 | tf_op jit(solution)/shard_map/ppermute | solution.py:326
  30.8 1.4 %collective-permute-start.6 = (bf16[128,512]{1,0:T(8,128)(2,1)S(1)}, bf16[128,512]{1,0:T(8,128)(2,1)S(1)}, u32[]{:S(2)}, u32[]{:S(2)}) collective-permute-start(bf16[128,512]{1,0:T(8,128)(2,1)S(1)} %hand_on.2), channel_id=1, source_target_pairs={{0,1},{1,0},{2,3},{3,2},{4,5},{5,4},{6,7},{7,6},{8,9},{9,8},{10,11... | collective-permute-start | bytes 393224 | tf_op jit(solution)/shard_map/ppermute | solution.py:326
  55.6 9.0 %collective-permute-start.10 = (bf16[128,1024]{1,0:T(8,128)(2,1)S(1)}, bf16[128,1024]{1,0:T(8,128)(2,1)S(1)}, u32[]{:S(2)}, u32[]{:S(2)}) collective-permute-start(bf16[128,1024]{1,0:T(8,128)(2,1)S(1)} %attend.1.own_ref), channel_id=1, source_target_pairs={{0,4},{1,5},{2,6},{3,7},{4,0},{5,1},{6,2},{7,3},{8,12},{9,13},{10,... | collective-permute-start | bytes 786440 | tf_op jit(solution)/shard_map/ppermute | solution.py:322
  55.7 14.9 %collective-permute-start.8 = (bf16[128,1024]{1,0:T(8,128)(2,1)S(1)}, bf16[128,1024]{1,0:T(8,128)(2,1)S(1)}, u32[]{:S(2)}, u32[]{:S(2)}) collective-permute-start(bf16[128,1024]{1,0:T(8,128)(2,1)S(1)} %attend.1.own_ref), channel_id=1, source_target_pairs={{0,2},{1,3},{2,4},{3,5},{4,6},{5,7},{6,0},{7,1},{8,10},{9,11},{10,... | collective-permute-start | bytes 786440 | tf_op jit(solution)/shard_map/ppermute | solution.py:322
  56.9 14.5 %collective-permute-start.12 = (bf16[128,1024]{1,0:T(8,128)(2,1)S(1)}, bf16[128,1024]{1,0:T(8,128)(2,1)S(1)}, u32[]{:S(2)}, u32[]{:S(2)}) collective-permute-start(bf16[128,1024]{1,0:T(8,128)(2,1)S(1)} %attend.1.own_ref), channel_id=1, source_target_pairs={{0,6},{1,7},{2,0},{3,1},{4,2},{5,3},{6,4},{7,5},{8,14},{9,15},{10,... | collective-permute-start | bytes 786440 | tf_op jit(solution)/shard_map/ppermute | solution.py:322
  58.5 13.0 %collective-permute-start.7 = (bf16[128,1024]{1,0:T(8,128)(2,1)S(1)}, bf16[128,1024]{1,0:T(8,128)(2,1)S(1)}, u32[]{:S(2)}, u32[]{:S(2)}) collective-permute-start(bf16[128,1024]{1,0:T(8,128)(2,1)S(1)} %attend.1.own_ref), channel_id=1, source_target_pairs={{0,1},{1,0},{2,3},{3,2},{4,5},{5,4},{6,7},{7,6},{8,9},{9,8},{10,11... | collective-permute-start | bytes 786440 | tf_op jit(solution)/shard_map/ppermute | solution.py:326
  64.6 6.9 %collective-permute-start.11 = (bf16[128,1024]{1,0:T(8,128)(2,1)S(1)}, bf16[128,1024]{1,0:T(8,128)(2,1)S(1)}, u32[]{:S(2)}, u32[]{:S(2)}) collective-permute-start(bf16[128,1024]{1,0:T(8,128)(2,1)S(1)} %collective-permute-done.10.refs_3_), channel_id=1, source_target_pairs={{0,1},{1,0},{2,3},{3,2},{4,5},{5,4},{6,7},{7,6},{8,9},{9,8},{10,11... | collective-permute-start | bytes 786440 | tf_op jit(solution)/shard_map/ppermute | solution.py:326
  70.6 1.9 %collective-permute-start.9 = (bf16[128,1024]{1,0:T(8,128)(2,1)S(1)}, bf16[128,1024]{1,0:T(8,128)(2,1)S(1)}, u32[]{:S(2)}, u32[]{:S(2)}) collective-permute-start(bf16[128,1024]{1,0:T(8,128)(2,1)S(1)} %collective-permute-done.8.refs_1_), channel_id=1, source_target_pairs={{0,1},{1,0},{2,3},{3,2},{4,5},{5,4},{6,7},{7,6},{8,9},{9,8},{10,11... | collective-permute-start | bytes 786440 | tf_op jit(solution)/shard_map/ppermute | solution.py:326
  71.4 2.1 %collective-permute-start.13 = (bf16[128,1024]{1,0:T(8,128)(2,1)S(1)}, bf16[128,1024]{1,0:T(8,128)(2,1)S(1)}, u32[]{:S(2)}, u32[]{:S(2)}) collective-permute-start(bf16[128,1024]{1,0:T(8,128)(2,1)S(1)} %hand_on.3), channel_id=1, source_target_pairs={{0,1},{1,0},{2,3},{3,2},{4,5},{5,4},{6,7},{7,6},{8,9},{9,8},{10,11... | collective-permute-start | bytes 786440 | tf_op jit(solution)/shard_map/ppermute | solution.py:326
  72.5 12.5 %copy-start = (bf16[1024,512]{1,0:T(8,128)(2,1)S(1)}, bf16[1024,512]{1,0:T(8,128)(2,1)}, u32[]{:S(2)}) copy-start(bf16[1024,512]{1,0:T(8,128)(2,1)} %rows_ref.1) | copy-start | bytes 3145732

commit v6 on v5

--- a/solution.py
+++ b/solution.py
@@ -244,7 +244,7 @@
             ]
 
 
-MIDDLE, LAST = (1, 2, 3, 4, 5, 6), (7,)
+MIDDLE, LAST = (1, 2, 4, 5, 6), (3, 7)
 
 
 def head_sum(which, weight_ref, blocks):

time: 86.6 us -> 86.2 us (level)
  transfers between devices with their start and end apart: 14 -> 14, of which waited for: 5 -> 6; matrix products, arithmetic and copies ran while one was open for 0% -> 0% of each run, Pallas kernels for 11% -> 10%
where the time goes in v6:
time: 86.2 us; the launch traced here: 86 us
  blocking collectives  45.4 us (53%)
  starting transfers between devices  19.2 us (22%)
  Pallas kernels  16.7 us (19%)
  waiting for transfers between devices  4.48 us (5%)
    all_to_all x1, blocking collectives, on_device(): pairs = lax.all_to_all(pair, 'seq', split_axis=0, concat_axis=0, tiled=True)  19.2 us
    all_to_all x1, blocking collectives, on_device(): lax.all_to_all(outgoing, 'seq', split_axis=0, concat_axis=0, tiled=True)  14.9 us
    all_to_all x1, blocking collectives, on_device(): lax.all_to_all(outgoing_back, 'seq', split_axis=0, concat_axis=0, tiled=T...  11.3 us
    ppermute x8, starting transfers between devices, other_core(): return lax.ppermute(array, 'mp', [(m, m ^ 1) for m in range(NMP)])  10 us
    ppermute x6, starting transfers between devices, z_step(): return lax.ppermute(array, 'mp', pairs)  9.19 us
    pallas_call x1, Pallas kernels, on_device(): pl.pallas_call(load_in_kernel, out_shape=(pltpu.VMEM((WIDTH, HEAD), BF16)...  4.11 us
    pallas_call x1, Pallas kernels, on_device(): pl.pallas_call(load_out_kernel, out_shape=(pltpu.VMEM((NMP * GROUP * HEAD...  3.98 us
    ppermute x6, waiting for transfers between devices, z_step(): return lax.ppermute(array, 'mp', pairs)  2.62 us
  transfers between devices with their start and end apart: 14, of which 6 were waited for; matrix products, arithmetic and copies ran while one was open for 0% of the time, Pallas kernels for 10%

profile of v6, /device:TPU:1, one launch (start us, length us, event | category | flops | bytes accessed | tf_op | source)
XLA Modules:
  0.0 86.0 jit_solution(1369011522660685626)
XLA Ops:
  0.0 1.7 %pick.1 = (bf16[16,2,8,512]{3,2,1,0:T(8,128)(2,1)S(1)}, s32[3,16]{1,0:T(4,128)S(4)}, f32[8]{0:T(128)S(4)}) custom-call(s32[16,16]{1,0:T(8,128)} %tally_ref.1, s32[1,256]{1,0:T(1,128)} %select_ref.1, bf16[1024,512]{1,0:T(8,128)(2,1)} %rows_ref.1, f32[8]{0:T(128)} %sharp_hbm.1), custom_call_target="tpu_custom_call" | custom-call | tf_op jit(solution)/shard_map/pick/pallas_call | solution.py:369
  1.7 14.9 %all_to_all.15.in_ref = bf16[16,2,8,512]{3,2,1,0:T(8,128)(2,1)S(1)} all-to-all(bf16[16,2,8,512]{3,2,1,0:T(8,128)(2,1)S(1)} %get-tuple-element.20), channel_id=1, replica_groups=mesh['seq'=16,'mp'=8] {'seq'}, dimensions={0} | all-to-all | bytes 524288 | tf_op jit(solution)/shard_map/all_to_all | solution.py:393
  16.7 3.7 %collective-permute-start.3 = (bf16[128,512]{1,0:T(8,128)(2,1)S(1)}, bf16[128,512]{1,0:T(8,128)(2,1)S(1)}, u32[]{:S(2)}, u32[]{:S(2)}) collective-permute-start(bf16[128,512]{1,0:T(8,128)(2,1)S(1)} %compact.1.after_ref.refs_0_), channel_id=1, source_target_pairs={{0,4},{1,5},{2,6},{3,7},{4,0},{5,1},{6,2},{7,3},{8,12},{9,13},{10,... | collective-permute-start | bytes 393224 | tf_op jit(solution)/shard_map/ppermute | solution.py:322
  20.4 0.7 collective-permute-start.1
  21.1 1.9 %collective-permute-start.5 = (bf16[128,512]{1,0:T(8,128)(2,1)S(1)}, bf16[128,512]{1,0:T(8,128)(2,1)S(1)}, u32[]{:S(2)}, u32[]{:S(2)}) collective-permute-start(bf16[128,512]{1,0:T(8,128)(2,1)S(1)} %compact.1.after_ref.refs_0_), channel_id=1, source_target_pairs={{0,6},{1,7},{2,0},{3,1},{4,2},{5,3},{6,4},{7,5},{8,14},{9,15},{10,... | collective-permute-start | bytes 393224 | tf_op jit(solution)/shard_map/ppermute | solution.py:322
  23.0 2.9 %collective-permute-start = (bf16[128,512]{1,0:T(8,128)(2,1)S(1)}, bf16[128,512]{1,0:T(8,128)(2,1)S(1)}, u32[]{:S(2)}, u32[]{:S(2)}) collective-permute-start(bf16[128,512]{1,0:T(8,128)(2,1)S(1)} %compact.1.after_ref.refs_0_), channel_id=1, source_target_pairs={{0,1},{1,0},{2,3},{3,2},{4,5},{5,4},{6,7},{7,6},{8,9},{9,8},{10,11... | collective-permute-start | bytes 393224 | tf_op jit(solution)/shard_map/ppermute | solution.py:326
  26.0 4.1 %load_in.1 = (bf16[4096,128]{1,0:T(8,128)(2,1)S(1)}, bf16[4096,128]{1,0:T(8,128)(2,1)S(1)}, bf16[4096,1024]{1,0:T(8,128)(2,1)S(1)}, f32[8,128]{1,0:T(8,128)S(1)}) custom-call(bf16[4096,128]{1,0:T(8,128)(2,1)} %keys_hbm.1, bf16[4096,128]{1,0:T(8,128)(2,1)} %values_hbm.1, bf16[4096,1024]{1,0:T(8,128)(2,1)} %query_hbm.1, ...), custom_call_target="tpu_custom_call" | custom-call | tf_op jit(solution)/shard_map/load_in/pallas_call | solution.py:402
  30.1 0.0 copy-start.1
  30.1 0.0 copy-start.3
  30.1 0.0 copy-start.4
  30.1 0.0 collective-permute-done.3.refs_4_
  30.2 0.1 collective-permute-start.4
  30.2 0.0 collective-permute-done.1.refs_2_
  30.3 0.5 collective-permute-start.2
  30.7 0.0 collective-permute-done.5.in_ref.refs_6_
  30.8 0.2 collective-permute-start.6
  30.9 0.0 collective-permute-done.refs_1_
  30.9 0.6 collective-permute-done.4.refs_5_
  31.6 0.2 collective-permute-done.2.refs_3_
  31.8 0.4 collective-permute-done.6.refs_7_
  32.2 0.0 copy-done.2
  32.2 2.2 %project_in.1 = (bf16[128,1024]{1,0:T(8,128)(2,1)S(1)}, bf16[16,128,256]{2,1,0:T(8,128)(2,1)S(1)}) custom-call(bf16[32,128]{1,0:T(8,128)(2,1)S(1)} %bitcast.2, bf16[4096,1024]{1,0:T(8,128)(2,1)S(1)} %get-tuple-element.21.query_weight_ref, bf16[4096,128]{1,0:T(8,128)(2,1)S(1)} %get-tuple-element.22.keys_ref, ...), custom_call_target="tpu_custom_call" | custom-call | flops 1342177280 | bytes 4194304 | tf_op jit(solution)/shard_map/project_in/pallas_call | solution.py:420
  34.4 19.2 %all_to_all.16.pair_ref = bf16[16,128,256]{2,1,0:T(8,128)(2,1)S(1)} all-to-all(bf16[16,128,256]{2,1,0:T(8,128)(2,1)S(1)} %get-tuple-element.26), channel_id=1, replica_groups=mesh['seq'=16,'mp'=8] {'seq'}, dimensions={0} | all-to-all | bytes 2097152 | tf_op jit(solution)/shard_map/all_to_all | solution.py:439
  53.5 2.1 %attend.1.own_ref = bf16[128,1024]{1,0:T(8,128)(2,1)S(1)} custom-call(f32[8]{0:T(128)S(4)} %get-tuple-element.19.sharp_ref, bf16[128,1024]{1,0:T(8,128)(2,1)S(1)} %get-tuple-element.25.query_ref, bf16[16,128,256]{2,1,0:T(8,128)(2,1)S(1)} %all_to_all.16.pair_ref), custom_call_target="tpu_custom_call" | custom-call | tf_op jit(solution)/shard_map/attend/pallas_call | solution.py:441
  55.6 0.1 collective-permute-start.9
  55.7 1.2 %collective-permute-start.8 = (bf16[128,1024]{1,0:T(8,128)(2,1)S(1)}, bf16[128,1024]{1,0:T(8,128)(2,1)S(1)}, u32[]{:S(2)}, u32[]{:S(2)}) collective-permute-start(bf16[128,1024]{1,0:T(8,128)(2,1)S(1)} %attend.1.own_ref), channel_id=1, source_target_pairs={{0,2},{1,3},{2,4},{3,5},{4,6},{5,7},{6,0},{7,1},{8,10},{9,11},{10,... | collective-permute-start | bytes 786440 | tf_op jit(solution)/shard_map/ppermute | solution.py:322
  56.9 1.6 %collective-permute-start.11 = (bf16[128,1024]{1,0:T(8,128)(2,1)S(1)}, bf16[128,1024]{1,0:T(8,128)(2,1)S(1)}, u32[]{:S(2)}, u32[]{:S(2)}) collective-permute-start(bf16[128,1024]{1,0:T(8,128)(2,1)S(1)} %attend.1.own_ref), channel_id=1, source_target_pairs={{0,6},{1,7},{2,0},{3,1},{4,2},{5,3},{6,4},{7,5},{8,14},{9,15},{10,... | collective-permute-start | bytes 786440 | tf_op jit(solution)/shard_map/ppermute | solution.py:322
  58.5 2.1 %collective-permute-start.7 = (bf16[128,1024]{1,0:T(8,128)(2,1)S(1)}, bf16[128,1024]{1,0:T(8,128)(2,1)S(1)}, u32[]{:S(2)}, u32[]{:S(2)}) collective-permute-start(bf16[128,1024]{1,0:T(8,128)(2,1)S(1)} %attend.1.own_ref), channel_id=1, source_target_pairs={{0,1},{1,0},{2,3},{3,2},{4,5},{5,4},{6,7},{7,6},{8,9},{9,8},{10,11... | collective-permute-start | bytes 786440 | tf_op jit(solution)/shard_map/ppermute | solution.py:326
  60.6 0.0 copy-done.1
  60.6 0.0 copy-done.3
  60.6 0.0 copy-done.4
  60.6 4.0 %load_out.1 = (bf16[8192,512]{1,0:T(8,128)(2,1)S(1)}, f32[128,512]{1,0:T(8,128)S(1)}, f32[128,128]{1,0:T(8,128)S(1)}, bf16[1024,256]{1,0:T(8,128)(2,1)S(1)}) custom-call(bf16[8192,512]{1,0:T(8,128)(2,1)} %weight_hbm.1, s32[16,16]{1,0:T(8,128)S(1)} %copy-done.1, s32[1,256]{1,0:T(1,128)S(1)} %copy-done.4, bf16[32,128]{1,0:T(8,128)(2,1)S(1)} %bitcast.3, ...), custom_call_target="tpu_custom_call" | custom-call | tf_op jit(solution)/shard_map/load_out/pallas_call | solution.py:449
  64.6 0.0 collective-permute-done.9.refs_2_
  64.6 3.4 %collective-permute-start.10 = (bf16[128,1024]{1,0:T(8,128)(2,1)S(1)}, bf16[128,1024]{1,0:T(8,128)(2,1)S(1)}, u32[]{:S(2)}, u32[]{:S(2)}) collective-permute-start(bf16[128,1024]{1,0:T(8,128)(2,1)S(1)} %collective-permute-done.9.refs_2_), channel_id=1, source_target_pairs={{0,1},{1,0},{2,3},{3,2},{4,5},{5,4},{6,7},{7,6},{8,9},{9,8},{10,11... | collective-permute-start | bytes 786440 | tf_op jit(solution)/shard_map/ppermute | solution.py:326
  68.0 2.6 %collective-permute-done.8.refs_1_ = bf16[128,1024]{1,0:T(8,128)(2,1)S(1)} collective-permute-done((bf16[128,1024]{1,0:T(8,128)(2,1)S(1)}, bf16[128,1024]{1,0:T(8,128)(2,1)S(1)}, u32[]{:S(2)}, u32[]{:S(2)}) %collective-permute-start.8) | collective-permute-done | bytes 262176 | tf_op jit(solution)/shard_map/ppermute | solution.py:322
  70.6 0.7 collective-permute-start.12
  71.3 0.0 collective-permute-done.11.refs_4_.in_ref
  71.4 0.1 collective-permute-start.13
  71.5 0.0 collective-permute-done.7.refs_0_
  71.5 0.0 collective-permute-done.10.refs_3_
  71.5 0.0 copy-start
  71.5 0.9 %project_middle.1.total_ref = f32[128,512]{1,0:T(8,128)S(1)} custom-call(f32[128,512]{1,0:T(8,128)S(1)} %get-tuple-element.29.total_in.token_ref, bf16[8192,512]{1,0:T(8,128)(2,1)S(1)} %get-tuple-element.30.weight_ref, bf16[128,1024]{1,0:T(8,128)(2,1)S(1)} %collective-permute-done.7.refs_0_, bf16[128,1024]{1,0:T(8,128)(2,1)S(1)} %collective-permute-done.8.refs_1_, ...), custom_call_target="tpu_custom_call" | custom-call | tf_op jit(solution)/shard_map/project_middle/pallas_call | solution.py:473
  72.4 0.1 collective-permute-done.12.refs_0_
  72.5 0.5 collective-permute-done.13.refs_1_
  73.0 0.5 project_last.1
  73.5 11.3 %all_to_all.17.back_ref = bf16[16,2,8,512]{3,2,1,0:T(8,128)(2,1)S(1)} all-to-all(bf16[16,2,8,512]{3,2,1,0:T(8,128)(2,1)S(1)} %project_last.1), channel_id=1, replica_groups=mesh['seq'=16,'mp'=8] {'seq'}, dimensions={0} | all-to-all | bytes 524288 | tf_op jit(solution)/shard_map/all_to_all | solution.py:490
  84.8 0.0 copy-done
  84.8 1.3 %blend.1 = bf16[1024,512]{1,0:T(8,128)(2,1)} custom-call(s32[3,16]{1,0:T(4,128)S(4)} %get-tuple-element.18.table_ref, bf16[1024,256]{1,0:T(8,128)(2,1)S(1)} %get-tuple-element.27.hot_ref, bf16[1024,512]{1,0:T(8,128)(2,1)S(1)} %copy-done, bf16[16,2,8,512]{3,2,1,0:T(8,128)(2,1)S(1)} %all_to_all.17.back_ref), custom_call_target="tpu_custom_call" | custom-call | tf_op jit(solution)/shard_map/blend/pallas_call | solution.py:491
  (4 shorter events, 0.1 us)
Async XLA Ops:
  0.0 32.2 %copy-start.2 = (bf16[4096]{0:T(1024)(128)(2,1)S(1)}, bf16[4096]{0:T(1024)(128)(2,1)}, u32[]{:S(2)}) copy-start(bf16[4096]{0:T(1024)(128)(2,1)} %param.11) | copy-start | bytes 24580
  16.7 13.5 %collective-permute-start.3 = (bf16[128,512]{1,0:T(8,128)(2,1)S(1)}, bf16[128,512]{1,0:T(8,128)(2,1)S(1)}, u32[]{:S(2)}, u32[]{:S(2)}) collective-permute-start(bf16[128,512]{1,0:T(8,128)(2,1)S(1)} %compact.1.after_ref.refs_0_), channel_id=1, source_target_pairs={{0,4},{1,5},{2,6},{3,7},{4,0},{5,1},{6,2},{7,3},{8,12},{9,13},{10,... | collective-permute-start | bytes 393224 | tf_op jit(solution)/shard_map/ppermute | solution.py:322
  20.4 9.9 %collective-permute-start.1 = (bf16[128,512]{1,0:T(8,128)(2,1)S(1)}, bf16[128,512]{1,0:T(8,128)(2,1)S(1)}, u32[]{:S(2)}, u32[]{:S(2)}) collective-permute-start(bf16[128,512]{1,0:T(8,128)(2,1)S(1)} %compact.1.after_ref.refs_0_), channel_id=1, source_target_pairs={{0,2},{1,3},{2,4},{3,5},{4,6},{5,7},{6,0},{7,1},{8,10},{9,11},{10,... | collective-permute-start | bytes 393224 | tf_op jit(solution)/shard_map/ppermute | solution.py:322
  21.1 9.6 %collective-permute-start.5 = (bf16[128,512]{1,0:T(8,128)(2,1)S(1)}, bf16[128,512]{1,0:T(8,128)(2,1)S(1)}, u32[]{:S(2)}, u32[]{:S(2)}) collective-permute-start(bf16[128,512]{1,0:T(8,128)(2,1)S(1)} %compact.1.after_ref.refs_0_), channel_id=1, source_target_pairs={{0,6},{1,7},{2,0},{3,1},{4,2},{5,3},{6,4},{7,5},{8,14},{9,15},{10,... | collective-permute-start | bytes 393224 | tf_op jit(solution)/shard_map/ppermute | solution.py:322
  23.0 7.9 %collective-permute-start = (bf16[128,512]{1,0:T(8,128)(2,1)S(1)}, bf16[128,512]{1,0:T(8,128)(2,1)S(1)}, u32[]{:S(2)}, u32[]{:S(2)}) collective-permute-start(bf16[128,512]{1,0:T(8,128)(2,1)S(1)} %compact.1.after_ref.refs_0_), channel_id=1, source_target_pairs={{0,1},{1,0},{2,3},{3,2},{4,5},{5,4},{6,7},{7,6},{8,9},{9,8},{10,11... | collective-permute-start | bytes 393224 | tf_op jit(solution)/shard_map/ppermute | solution.py:326
  30.1 30.5 %copy-start.1 = (s32[16,16]{1,0:T(8,128)S(1)}, s32[16,16]{1,0:T(8,128)}, u32[]{:S(2)}) copy-start(s32[16,16]{1,0:T(8,128)} %tally_ref.1) | copy-start | bytes 3076
  30.1 30.5 %copy-start.3 = (bf16[4096]{0:T(1024)(128)(2,1)S(1)}, bf16[4096]{0:T(1024)(128)(2,1)}, u32[]{:S(2)}) copy-start(bf16[4096]{0:T(1024)(128)(2,1)} %param.12) | copy-start | bytes 24580
  30.1 30.5 %copy-start.4 = (s32[1,256]{1,0:T(1,128)S(1)}, s32[1,256]{1,0:T(1,128)}, u32[]{:S(2)}) copy-start(s32[1,256]{1,0:T(1,128)} %select_ref.1) | copy-start | bytes 3076
  30.2 1.4 %collective-permute-start.4 = (bf16[128,512]{1,0:T(8,128)(2,1)S(1)}, bf16[128,512]{1,0:T(8,128)(2,1)S(1)}, u32[]{:S(2)}, u32[]{:S(2)}) collective-permute-start(bf16[128,512]{1,0:T(8,128)(2,1)S(1)} %collective-permute-done.3.refs_4_), channel_id=1, source_target_pairs={{0,1},{1,0},{2,3},{3,2},{4,5},{5,4},{6,7},{7,6},{8,9},{9,8},{10,11... | collective-permute-start | bytes 393224 | tf_op jit(solution)/shard_map/ppermute | solution.py:326
  30.3 1.5 %collective-permute-start.2 = (bf16[128,512]{1,0:T(8,128)(2,1)S(1)}, bf16[128,512]{1,0:T(8,128)(2,1)S(1)}, u32[]{:S(2)}, u32[]{:S(2)}) collective-permute-start(bf16[128,512]{1,0:T(8,128)(2,1)S(1)} %collective-permute-done.1.refs_2_), channel_id=1, source_target_pairs={{0,1},{1,0},{2,3},{3,2},{4,5},{5,4},{6,7},{7,6},{8,9},{9,8},{10,11... | collective-permute-start | bytes 393224 | tf_op jit(solution)/shard_map/ppermute | solution.py:326
  30.8 1.4 %collective-permute-start.6 = (bf16[128,512]{1,0:T(8,128)(2,1)S(1)}, bf16[128,512]{1,0:T(8,128)(2,1)S(1)}, u32[]{:S(2)}, u32[]{:S(2)}) collective-permute-start(bf16[128,512]{1,0:T(8,128)(2,1)S(1)} %hand_on.2), channel_id=1, source_target_pairs={{0,1},{1,0},{2,3},{3,2},{4,5},{5,4},{6,7},{7,6},{8,9},{9,8},{10,11... | collective-permute-start | bytes 393224 | tf_op jit(solution)/shard_map/ppermute | solution.py:326
  55.6 9.0 %collective-permute-start.9 = (bf16[128,1024]{1,0:T(8,128)(2,1)S(1)}, bf16[128,1024]{1,0:T(8,128)(2,1)S(1)}, u32[]{:S(2)}, u32[]{:S(2)}) collective-permute-start(bf16[128,1024]{1,0:T(8,128)(2,1)S(1)} %attend.1.own_ref), channel_id=1, source_target_pairs={{0,4},{1,5},{2,6},{3,7},{4,0},{5,1},{6,2},{7,3},{8,12},{9,13},{10,... | collective-permute-start | bytes 786440 | tf_op jit(solution)/shard_map/ppermute | solution.py:322
  55.7 14.9 %collective-permute-start.8 = (bf16[128,1024]{1,0:T(8,128)(2,1)S(1)}, bf16[128,1024]{1,0:T(8,128)(2,1)S(1)}, u32[]{:S(2)}, u32[]{:S(2)}) collective-permute-start(bf16[128,1024]{1,0:T(8,128)(2,1)S(1)} %attend.1.own_ref), channel_id=1, source_target_pairs={{0,2},{1,3},{2,4},{3,5},{4,6},{5,7},{6,0},{7,1},{8,10},{9,11},{10,... | collective-permute-start | bytes 786440 | tf_op jit(solution)/shard_map/ppermute | solution.py:322
  56.9 14.5 %collective-permute-start.11 = (bf16[128,1024]{1,0:T(8,128)(2,1)S(1)}, bf16[128,1024]{1,0:T(8,128)(2,1)S(1)}, u32[]{:S(2)}, u32[]{:S(2)}) collective-permute-start(bf16[128,1024]{1,0:T(8,128)(2,1)S(1)} %attend.1.own_ref), channel_id=1, source_target_pairs={{0,6},{1,7},{2,0},{3,1},{4,2},{5,3},{6,4},{7,5},{8,14},{9,15},{10,... | collective-permute-start | bytes 786440 | tf_op jit(solution)/shard_map/ppermute | solution.py:322
  58.5 13.0 %collective-permute-start.7 = (bf16[128,1024]{1,0:T(8,128)(2,1)S(1)}, bf16[128,1024]{1,0:T(8,128)(2,1)S(1)}, u32[]{:S(2)}, u32[]{:S(2)}) collective-permute-start(bf16[128,1024]{1,0:T(8,128)(2,1)S(1)} %attend.1.own_ref), channel_id=1, source_target_pairs={{0,1},{1,0},{2,3},{3,2},{4,5},{5,4},{6,7},{7,6},{8,9},{9,8},{10,11... | collective-permute-start | bytes 786440 | tf_op jit(solution)/shard_map/ppermute | solution.py:326
  64.6 6.9 %collective-permute-start.10 = (bf16[128,1024]{1,0:T(8,128)(2,1)S(1)}, bf16[128,1024]{1,0:T(8,128)(2,1)S(1)}, u32[]{:S(2)}, u32[]{:S(2)}) collective-permute-start(bf16[128,1024]{1,0:T(8,128)(2,1)S(1)} %collective-permute-done.9.refs_2_), channel_id=1, source_target_pairs={{0,1},{1,0},{2,3},{3,2},{4,5},{5,4},{6,7},{7,6},{8,9},{9,8},{10,11... | collective-permute-start | bytes 786440 | tf_op jit(solution)/shard_map/ppermute | solution.py:326
  70.6 1.9 %collective-permute-start.12 = (bf16[128,1024]{1,0:T(8,128)(2,1)S(1)}, bf16[128,1024]{1,0:T(8,128)(2,1)S(1)}, u32[]{:S(2)}, u32[]{:S(2)}) collective-permute-start(bf16[128,1024]{1,0:T(8,128)(2,1)S(1)} %collective-permute-done.8.refs_1_), channel_id=1, source_target_pairs={{0,1},{1,0},{2,3},{3,2},{4,5},{5,4},{6,7},{7,6},{8,9},{9,8},{10,11... | collective-permute-start | bytes 786440 | tf_op jit(solution)/shard_map/ppermute | solution.py:326
  71.4 1.6 %collective-permute-start.13 = (bf16[128,1024]{1,0:T(8,128)(2,1)S(1)}, bf16[128,1024]{1,0:T(8,128)(2,1)S(1)}, u32[]{:S(2)}, u32[]{:S(2)}) collective-permute-start(bf16[128,1024]{1,0:T(8,128)(2,1)S(1)} %hand_on.3), channel_id=1, source_target_pairs={{0,1},{1,0},{2,3},{3,2},{4,5},{5,4},{6,7},{7,6},{8,9},{9,8},{10,11... | collective-permute-start | bytes 786440 | tf_op jit(solution)/shard_map/ppermute | solution.py:326
  71.5 13.3 %copy-start = (bf16[1024,512]{1,0:T(8,128)(2,1)S(1)}, bf16[1024,512]{1,0:T(8,128)(2,1)}, u32[]{:S(2)}) copy-start(bf16[1024,512]{1,0:T(8,128)(2,1)} %rows_ref.1) | copy-start | bytes 3145732

commit v7 on v6

--- a/solution.py
+++ b/solution.py
@@ -152,15 +152,24 @@
         spread_ref[r // parts, r % parts : r % parts + 1] = wide[r : r + 1]
 
 
-def project_in_kernel(gain_in, query_weight_ref, keys_ref, values_ref, *refs):
+def square_sum(blocks):
+    total = jnp.zeros((OWNED, 128), F32)
+    for block in blocks:
+        for c in range(FEAT // 128):
+            wide = block[:, 128 * c : 128 * (c + 1)].astype(F32)
+            total = total + wide * wide
+    return total
+
+
+def square_kernel(*refs):
+    refs[-1][...] = square_sum(refs[:-1])
+
+
+def project_in_kernel(squares_ref, gain_in, query_weight_ref, keys_ref, values_ref, *refs):
     blocks, (query_ref, pair_ref, gain_ref) = refs[:NMP], refs[NMP:]
     parts = FEAT // 128
     spread(gain_in, gain_ref)
-    squares = jnp.zeros((OWNED, 128), F32)
-    for k in range(NMP):
-        for c in range(parts):
-            wide = blocks[k][:, 128 * c : 128 * (c + 1)].astype(F32)
-            squares = squares + wide * wide
+    squares = squares_ref[...] + square_sum([blocks[k] for k in (1, 3, 5, 7)])
     inverse = lax.rsqrt(jnp.sum(squares, axis=1, keepdims=True) / WIDTH + 1e-05)
     query = jnp.zeros((OWNED, GROUP * HEAD), F32)
     keys = jnp.zeros((OWNED, HEAD), F32)
@@ -417,19 +426,28 @@
     blocks[1] = other_core(tokens)
     add_cores(blocks, loaded)
     blocks = [blocks[k] for k in range(NMP)]
+    squares = pl.pallas_call(
+        square_kernel,
+        out_shape=pltpu.VMEM((OWNED, 128), F32),
+        in_specs=[VMEM] * 4,
+        out_specs=VMEM,
+        compiler_params=params(4),
+        name="square",
+    )(*(blocks[k] for k in (0, 2, 4, 6)))
     query, pair = pl.pallas_call(
         project_in_kernel,
         out_shape=(
             pltpu.VMEM((OWNED, GROUP * HEAD), BF16),
             pltpu.VMEM((NSEQ, OWNED, 2 * HEAD), BF16),
         ),
-        in_specs=[VMEM] * (4 + NMP),
+        in_specs=[VMEM] * (5 + NMP),
         out_specs=[VMEM] * 2,
         scratch_shapes=[pltpu.VMEM((NMP, FEAT // 128, 128), F32)],
         compiler_params=params(16),
         cost_estimate=cost(2 * OWNED * WIDTH * 10 * HEAD, 4 * MIB),
         name="project_in",
     )(
+        squares,
         prelayer_gain_vector.reshape(WIDTH // 128, 128),
         asker,
         lookup,

time: 86.2 us -> 86.2 us (level)
  transfers between devices with their start and end apart: 14 -> 14, of which waited for: 6 -> 6; matrix products, arithmetic and copies ran while one was open for 0% -> 0% of each run, Pallas kernels for 10% -> 11%
where the time goes in v7:
time: 86.2 us; the launch traced here: 85.9 us
  blocking collectives  45.3 us (53%)
  starting transfers between devices  19.2 us (22%)
  Pallas kernels  16.8 us (19%)
  waiting for transfers between devices  4.37 us (5%)
    all_to_all x1, blocking collectives, on_device(): pairs = lax.all_to_all(pair, 'seq', split_axis=0, concat_axis=0, tiled=True)  19.2 us
    all_to_all x1, blocking collectives, on_device(): lax.all_to_all(outgoing, 'seq', split_axis=0, concat_axis=0, tiled=True)  14.9 us
    all_to_all x1, blocking collectives, on_device(): lax.all_to_all(outgoing_back, 'seq', split_axis=0, concat_axis=0, tiled=T...  11.2 us
    ppermute x8, starting transfers between devices, other_core(): return lax.ppermute(array, 'mp', [(m, m ^ 1) for m in range(NMP)])  10 us
    ppermute x6, starting transfers between devices, z_step(): return lax.ppermute(array, 'mp', pairs)  9.19 us
    pallas_call x1, Pallas kernels, on_device(): pl.pallas_call(load_in_kernel, out_shape=(pltpu.VMEM((WIDTH, HEAD), BF16)...  4.11 us
    pallas_call x1, Pallas kernels, on_device(): pl.pallas_call(load_out_kernel, out_shape=(pltpu.VMEM((NMP * GROUP * HEAD...  3.98 us
    ppermute x6, waiting for transfers between devices, z_step(): return lax.ppermute(array, 'mp', pairs)  2.63 us
  transfers between devices with their start and end apart: 14, of which 6 were waited for; matrix products, arithmetic and copies ran while one was open for 0% of the time, Pallas kernels for 11%

profile of v7, /device:TPU:1, one launch (start us, length us, event | category | flops | bytes accessed | tf_op | source)
XLA Modules:
  0.0 85.9 jit_solution(2941309570466945795)
XLA Ops:
  0.0 1.7 %pick.1 = (bf16[16,2,8,512]{3,2,1,0:T(8,128)(2,1)S(1)}, s32[3,16]{1,0:T(4,128)S(4)}, f32[8]{0:T(128)S(4)}) custom-call(s32[16,16]{1,0:T(8,128)} %tally_ref.1, s32[1,256]{1,0:T(1,128)} %select_ref.1, bf16[1024,512]{1,0:T(8,128)(2,1)} %rows_ref.1, f32[8]{0:T(128)} %sharp_hbm.1), custom_call_target="tpu_custom_call" | custom-call | tf_op jit(solution)/shard_map/pick/pallas_call | solution.py:378
  1.7 14.9 %all_to_all.15.in_ref = bf16[16,2,8,512]{3,2,1,0:T(8,128)(2,1)S(1)} all-to-all(bf16[16,2,8,512]{3,2,1,0:T(8,128)(2,1)S(1)} %get-tuple-element.20), channel_id=1, replica_groups=mesh['seq'=16,'mp'=8] {'seq'}, dimensions={0} | all-to-all | bytes 524288 | tf_op jit(solution)/shard_map/all_to_all | solution.py:402
  16.7 3.7 %collective-permute-start.1 = (bf16[128,512]{1,0:T(8,128)(2,1)S(1)}, bf16[128,512]{1,0:T(8,128)(2,1)S(1)}, u32[]{:S(2)}, u32[]{:S(2)}) collective-permute-start(bf16[128,512]{1,0:T(8,128)(2,1)S(1)} %compact.1.refs_0_.after_ref), channel_id=1, source_target_pairs={{0,4},{1,5},{2,6},{3,7},{4,0},{5,1},{6,2},{7,3},{8,12},{9,13},{10,... | collective-permute-start | bytes 393224 | tf_op jit(solution)/shard_map/ppermute | solution.py:331
  20.4 0.7 collective-permute-start
  21.1 1.9 %collective-permute-start.2 = (bf16[128,512]{1,0:T(8,128)(2,1)S(1)}, bf16[128,512]{1,0:T(8,128)(2,1)S(1)}, u32[]{:S(2)}, u32[]{:S(2)}) collective-permute-start(bf16[128,512]{1,0:T(8,128)(2,1)S(1)} %compact.1.refs_0_.after_ref), channel_id=1, source_target_pairs={{0,6},{1,7},{2,0},{3,1},{4,2},{5,3},{6,4},{7,5},{8,14},{9,15},{10,... | collective-permute-start | bytes 393224 | tf_op jit(solution)/shard_map/ppermute | solution.py:331
  23.0 2.9 %collective-permute-start.3 = (bf16[128,512]{1,0:T(8,128)(2,1)S(1)}, bf16[128,512]{1,0:T(8,128)(2,1)S(1)}, u32[]{:S(2)}, u32[]{:S(2)}) collective-permute-start(bf16[128,512]{1,0:T(8,128)(2,1)S(1)} %compact.1.refs_0_.after_ref), channel_id=1, source_target_pairs={{0,1},{1,0},{2,3},{3,2},{4,5},{5,4},{6,7},{7,6},{8,9},{9,8},{10,11... | collective-permute-start | bytes 393224 | tf_op jit(solution)/shard_map/ppermute | solution.py:335
  26.0 4.1 %load_in.1 = (bf16[4096,128]{1,0:T(8,128)(2,1)S(1)}, bf16[4096,128]{1,0:T(8,128)(2,1)S(1)}, bf16[4096,1024]{1,0:T(8,128)(2,1)S(1)}, f32[8,128]{1,0:T(8,128)S(1)}) custom-call(bf16[4096,128]{1,0:T(8,128)(2,1)} %keys_hbm.1, bf16[4096,128]{1,0:T(8,128)(2,1)} %values_hbm.1, bf16[4096,1024]{1,0:T(8,128)(2,1)} %query_hbm.1, ...), custom_call_target="tpu_custom_call" | custom-call | tf_op jit(solution)/shard_map/load_in/pallas_call | solution.py:411
  30.1 0.0 copy-start.1
  30.1 0.0 copy-start.3
  30.1 0.0 copy-start.4
  30.1 0.0 collective-permute-done.1.refs_2_.refs_4_
  30.2 0.1 collective-permute-start.5
  30.2 0.0 collective-permute-done.refs_1_.refs_2_
  30.3 0.5 collective-permute-start.4
  30.7 0.0 collective-permute-done.2.refs_3_.in_ref.refs_6_
  30.8 0.2 collective-permute-start.6
  30.9 0.1 square.1.squares_ref
  31.1 0.0 collective-permute-done.3.refs_1_
  31.1 0.5 collective-permute-done.5.refs_5_
  31.6 0.2 collective-permute-done.4.refs_3_
  31.8 0.4 collective-permute-done.6.refs_7_
  32.2 0.0 copy-done.2
  32.2 2.1 %project_in.1 = (bf16[128,1024]{1,0:T(8,128)(2,1)S(1)}, bf16[16,128,256]{2,1,0:T(8,128)(2,1)S(1)}) custom-call(f32[128,128]{1,0:T(8,128)S(1)} %square.1.squares_ref, bf16[32,128]{1,0:T(8,128)(2,1)S(1)} %bitcast.2, bf16[4096,1024]{1,0:T(8,128)(2,1)S(1)} %get-tuple-element.21.query_weight_ref, bf16[4096,128]{1,0:T(8,128)(2,1)S(1)} %get-tuple-element.22.keys_ref, ...), custom_call_target="tpu_custom_call" | custom-call | flops 1342177280 | bytes 4194304 | tf_op jit(solution)/shard_map/project_in/pallas_call | solution.py:437
  34.3 19.2 %all_to_all.16.pair_ref = bf16[16,128,256]{2,1,0:T(8,128)(2,1)S(1)} all-to-all(bf16[16,128,256]{2,1,0:T(8,128)(2,1)S(1)} %get-tuple-element.26), channel_id=1, replica_groups=mesh['seq'=16,'mp'=8] {'seq'}, dimensions={0} | all-to-all | bytes 2097152 | tf_op jit(solution)/shard_map/all_to_all | solution.py:457
  53.5 2.1 %attend.1.own_ref = bf16[128,1024]{1,0:T(8,128)(2,1)S(1)} custom-call(f32[8]{0:T(128)S(4)} %get-tuple-element.19.sharp_ref, bf16[128,1024]{1,0:T(8,128)(2,1)S(1)} %get-tuple-element.25.query_ref, bf16[16,128,256]{2,1,0:T(8,128)(2,1)S(1)} %all_to_all.16.pair_ref), custom_call_target="tpu_custom_call" | custom-call | tf_op jit(solution)/shard_map/attend/pallas_call | solution.py:459
  55.6 0.1 collective-permute-start.9
  55.7 1.1 %collective-permute-start.8 = (bf16[128,1024]{1,0:T(8,128)(2,1)S(1)}, bf16[128,1024]{1,0:T(8,128)(2,1)S(1)}, u32[]{:S(2)}, u32[]{:S(2)}) collective-permute-start(bf16[128,1024]{1,0:T(8,128)(2,1)S(1)} %attend.1.own_ref), channel_id=1, source_target_pairs={{0,2},{1,3},{2,4},{3,5},{4,6},{5,7},{6,0},{7,1},{8,10},{9,11},{10,... | collective-permute-start | bytes 786440 | tf_op jit(solution)/shard_map/ppermute | solution.py:331
  56.8 1.7 %collective-permute-start.11 = (bf16[128,1024]{1,0:T(8,128)(2,1)S(1)}, bf16[128,1024]{1,0:T(8,128)(2,1)S(1)}, u32[]{:S(2)}, u32[]{:S(2)}) collective-permute-start(bf16[128,1024]{1,0:T(8,128)(2,1)S(1)} %attend.1.own_ref), channel_id=1, source_target_pairs={{0,6},{1,7},{2,0},{3,1},{4,2},{5,3},{6,4},{7,5},{8,14},{9,15},{10,... | collective-permute-start | bytes 786440 | tf_op jit(solution)/shard_map/ppermute | solution.py:331
  58.5 2.1 %collective-permute-start.7 = (bf16[128,1024]{1,0:T(8,128)(2,1)S(1)}, bf16[128,1024]{1,0:T(8,128)(2,1)S(1)}, u32[]{:S(2)}, u32[]{:S(2)}) collective-permute-start(bf16[128,1024]{1,0:T(8,128)(2,1)S(1)} %attend.1.own_ref), channel_id=1, source_target_pairs={{0,1},{1,0},{2,3},{3,2},{4,5},{5,4},{6,7},{7,6},{8,9},{9,8},{10,11... | collective-permute-start | bytes 786440 | tf_op jit(solution)/shard_map/ppermute | solution.py:335
  60.6 0.0 copy-done.1
  60.6 0.0 copy-done.3
  60.6 0.0 copy-done.4
  60.6 4.0 %load_out.1 = (bf16[8192,512]{1,0:T(8,128)(2,1)S(1)}, f32[128,512]{1,0:T(8,128)S(1)}, f32[128,128]{1,0:T(8,128)S(1)}, bf16[1024,256]{1,0:T(8,128)(2,1)S(1)}) custom-call(bf16[8192,512]{1,0:T(8,128)(2,1)} %weight_hbm.1, s32[16,16]{1,0:T(8,128)S(1)} %copy-done.1, s32[1,256]{1,0:T(1,128)S(1)} %copy-done.4, bf16[32,128]{1,0:T(8,128)(2,1)S(1)} %bitcast.3, ...), custom_call_target="tpu_custom_call" | custom-call | tf_op jit(solution)/shard_map/load_out/pallas_call | solution.py:467
  64.6 0.0 collective-permute-done.9.refs_2_
  64.6 3.4 %collective-permute-start.10 = (bf16[128,1024]{1,0:T(8,128)(2,1)S(1)}, bf16[128,1024]{1,0:T(8,128)(2,1)S(1)}, u32[]{:S(2)}, u32[]{:S(2)}) collective-permute-start(bf16[128,1024]{1,0:T(8,128)(2,1)S(1)} %collective-permute-done.9.refs_2_), channel_id=1, source_target_pairs={{0,1},{1,0},{2,3},{3,2},{4,5},{5,4},{6,7},{7,6},{8,9},{9,8},{10,11... | collective-permute-start | bytes 786440 | tf_op jit(solution)/shard_map/ppermute | solution.py:335
  68.0 2.6 %collective-permute-done.8.refs_1_ = bf16[128,1024]{1,0:T(8,128)(2,1)S(1)} collective-permute-done((bf16[128,1024]{1,0:T(8,128)(2,1)S(1)}, bf16[128,1024]{1,0:T(8,128)(2,1)S(1)}, u32[]{:S(2)}, u32[]{:S(2)}) %collective-permute-start.8) | collective-permute-done | bytes 262176 | tf_op jit(solution)/shard_map/ppermute | solution.py:331
  70.6 0.7 collective-permute-start.12
  71.3 0.0 collective-permute-done.11.refs_4_.in_ref
  71.4 0.1 collective-permute-start.13
  71.4 0.0 collective-permute-done.7.refs_0_
  71.5 0.0 collective-permute-done.10.refs_3_
  71.5 0.0 copy-start
  71.5 0.9 %project_middle.1.total_ref = f32[128,512]{1,0:T(8,128)S(1)} custom-call(f32[128,512]{1,0:T(8,128)S(1)} %get-tuple-element.29.total_in.token_ref, bf16[8192,512]{1,0:T(8,128)(2,1)S(1)} %get-tuple-element.30.weight_ref, bf16[128,1024]{1,0:T(8,128)(2,1)S(1)} %collective-permute-done.7.refs_0_, bf16[128,1024]{1,0:T(8,128)(2,1)S(1)} %collective-permute-done.8.refs_1_, ...), custom_call_target="tpu_custom_call" | custom-call | tf_op jit(solution)/shard_map/project_middle/pallas_call | solution.py:491
  72.4 0.1 collective-permute-done.12.refs_0_
  72.5 0.5 collective-permute-done.13.refs_1_
  73.0 0.5 project_last.1
  73.5 11.2 %all_to_all.17.back_ref = bf16[16,2,8,512]{3,2,1,0:T(8,128)(2,1)S(1)} all-to-all(bf16[16,2,8,512]{3,2,1,0:T(8,128)(2,1)S(1)} %project_last.1), channel_id=1, replica_groups=mesh['seq'=16,'mp'=8] {'seq'}, dimensions={0} | all-to-all | bytes 524288 | tf_op jit(solution)/shard_map/all_to_all | solution.py:508
  84.7 1.3 %blend.1 = bf16[1024,512]{1,0:T(8,128)(2,1)} custom-call(s32[3,16]{1,0:T(4,128)S(4)} %get-tuple-element.18.table_ref, bf16[1024,256]{1,0:T(8,128)(2,1)S(1)} %get-tuple-element.27.hot_ref, bf16[1024,512]{1,0:T(8,128)(2,1)S(1)} %copy-done, bf16[16,2,8,512]{3,2,1,0:T(8,128)(2,1)S(1)} %all_to_all.17.back_ref), custom_call_target="tpu_custom_call" | custom-call | tf_op jit(solution)/shard_map/blend/pallas_call | solution.py:509
  (5 shorter events, 0.1 us)
Async XLA Ops:
  0.0 32.2 %copy-start.2 = (bf16[4096]{0:T(1024)(128)(2,1)S(1)}, bf16[4096]{0:T(1024)(128)(2,1)}, u32[]{:S(2)}) copy-start(bf16[4096]{0:T(1024)(128)(2,1)} %param.11) | copy-start | bytes 24580
  16.7 13.5 %collective-permute-start.1 = (bf16[128,512]{1,0:T(8,128)(2,1)S(1)}, bf16[128,512]{1,0:T(8,128)(2,1)S(1)}, u32[]{:S(2)}, u32[]{:S(2)}) collective-permute-start(bf16[128,512]{1,0:T(8,128)(2,1)S(1)} %compact.1.refs_0_.after_ref), channel_id=1, source_target_pairs={{0,4},{1,5},{2,6},{3,7},{4,0},{5,1},{6,2},{7,3},{8,12},{9,13},{10,... | collective-permute-start | bytes 393224 | tf_op jit(solution)/shard_map/ppermute | solution.py:331
  20.4 9.9 %collective-permute-start = (bf16[128,512]{1,0:T(8,128)(2,1)S(1)}, bf16[128,512]{1,0:T(8,128)(2,1)S(1)}, u32[]{:S(2)}, u32[]{:S(2)}) collective-permute-start(bf16[128,512]{1,0:T(8,128)(2,1)S(1)} %compact.1.refs_0_.after_ref), channel_id=1, source_target_pairs={{0,2},{1,3},{2,4},{3,5},{4,6},{5,7},{6,0},{7,1},{8,10},{9,11},{10,... | collective-permute-start | bytes 393224 | tf_op jit(solution)/shard_map/ppermute | solution.py:331
  21.1 9.6 %collective-permute-start.2 = (bf16[128,512]{1,0:T(8,128)(2,1)S(1)}, bf16[128,512]{1,0:T(8,128)(2,1)S(1)}, u32[]{:S(2)}, u32[]{:S(2)}) collective-permute-start(bf16[128,512]{1,0:T(8,128)(2,1)S(1)} %compact.1.refs_0_.after_ref), channel_id=1, source_target_pairs={{0,6},{1,7},{2,0},{3,1},{4,2},{5,3},{6,4},{7,5},{8,14},{9,15},{10,... | collective-permute-start | bytes 393224 | tf_op jit(solution)/shard_map/ppermute | solution.py:331
  23.0 8.0 %collective-permute-start.3 = (bf16[128,512]{1,0:T(8,128)(2,1)S(1)}, bf16[128,512]{1,0:T(8,128)(2,1)S(1)}, u32[]{:S(2)}, u32[]{:S(2)}) collective-permute-start(bf16[128,512]{1,0:T(8,128)(2,1)S(1)} %compact.1.refs_0_.after_ref), channel_id=1, source_target_pairs={{0,1},{1,0},{2,3},{3,2},{4,5},{5,4},{6,7},{7,6},{8,9},{9,8},{10,11... | collective-permute-start | bytes 393224 | tf_op jit(solution)/shard_map/ppermute | solution.py:335
  30.1 30.5 %copy-start.1 = (s32[16,16]{1,0:T(8,128)S(1)}, s32[16,16]{1,0:T(8,128)}, u32[]{:S(2)}) copy-start(s32[16,16]{1,0:T(8,128)} %tally_ref.1) | copy-start | bytes 3076
  30.1 30.5 %copy-start.3 = (bf16[4096]{0:T(1024)(128)(2,1)S(1)}, bf16[4096]{0:T(1024)(128)(2,1)}, u32[]{:S(2)}) copy-start(bf16[4096]{0:T(1024)(128)(2,1)} %param.12) | copy-start | bytes 24580
  30.1 30.5 %copy-start.4 = (s32[1,256]{1,0:T(1,128)S(1)}, s32[1,256]{1,0:T(1,128)}, u32[]{:S(2)}) copy-start(s32[1,256]{1,0:T(1,128)} %select_ref.1) | copy-start | bytes 3076
  30.2 1.4 %collective-permute-start.5 = (bf16[128,512]{1,0:T(8,128)(2,1)S(1)}, bf16[128,512]{1,0:T(8,128)(2,1)S(1)}, u32[]{:S(2)}, u32[]{:S(2)}) collective-permute-start(bf16[128,512]{1,0:T(8,128)(2,1)S(1)} %collective-permute-done.1.refs_2_.refs_4_), channel_id=1, source_target_pairs={{0,1},{1,0},{2,3},{3,2},{4,5},{5,4},{6,7},{7,6},{8,9},{9,8},{10,11... | collective-permute-start | bytes 393224 | tf_op jit(solution)/shard_map/ppermute | solution.py:335
  30.3 1.5 %collective-permute-start.4 = (bf16[128,512]{1,0:T(8,128)(2,1)S(1)}, bf16[128,512]{1,0:T(8,128)(2,1)S(1)}, u32[]{:S(2)}, u32[]{:S(2)}) collective-permute-start(bf16[128,512]{1,0:T(8,128)(2,1)S(1)} %collective-permute-done.refs_1_.refs_2_), channel_id=1, source_target_pairs={{0,1},{1,0},{2,3},{3,2},{4,5},{5,4},{6,7},{7,6},{8,9},{9,8},{10,11... | collective-permute-start | bytes 393224 | tf_op jit(solution)/shard_map/ppermute | solution.py:335
  30.8 1.4 %collective-permute-start.6 = (bf16[128,512]{1,0:T(8,128)(2,1)S(1)}, bf16[128,512]{1,0:T(8,128)(2,1)S(1)}, u32[]{:S(2)}, u32[]{:S(2)}) collective-permute-start(bf16[128,512]{1,0:T(8,128)(2,1)S(1)} %hand_on.2), channel_id=1, source_target_pairs={{0,1},{1,0},{2,3},{3,2},{4,5},{5,4},{6,7},{7,6},{8,9},{9,8},{10,11... | collective-permute-start | bytes 393224 | tf_op jit(solution)/shard_map/ppermute | solution.py:335
  55.6 9.0 %collective-permute-start.9 = (bf16[128,1024]{1,0:T(8,128)(2,1)S(1)}, bf16[128,1024]{1,0:T(8,128)(2,1)S(1)}, u32[]{:S(2)}, u32[]{:S(2)}) collective-permute-start(bf16[128,1024]{1,0:T(8,128)(2,1)S(1)} %attend.1.own_ref), channel_id=1, source_target_pairs={{0,4},{1,5},{2,6},{3,7},{4,0},{5,1},{6,2},{7,3},{8,12},{9,13},{10,... | collective-permute-start | bytes 786440 | tf_op jit(solution)/shard_map/ppermute | solution.py:331
  55.7 14.9 %collective-permute-start.8 = (bf16[128,1024]{1,0:T(8,128)(2,1)S(1)}, bf16[128,1024]{1,0:T(8,128)(2,1)S(1)}, u32[]{:S(2)}, u32[]{:S(2)}) collective-permute-start(bf16[128,1024]{1,0:T(8,128)(2,1)S(1)} %attend.1.own_ref), channel_id=1, source_target_pairs={{0,2},{1,3},{2,4},{3,5},{4,6},{5,7},{6,0},{7,1},{8,10},{9,11},{10,... | collective-permute-start | bytes 786440 | tf_op jit(solution)/shard_map/ppermute | solution.py:331
  56.8 14.5 %collective-permute-start.11 = (bf16[128,1024]{1,0:T(8,128)(2,1)S(1)}, bf16[128,1024]{1,0:T(8,128)(2,1)S(1)}, u32[]{:S(2)}, u32[]{:S(2)}) collective-permute-start(bf16[128,1024]{1,0:T(8,128)(2,1)S(1)} %attend.1.own_ref), channel_id=1, source_target_pairs={{0,6},{1,7},{2,0},{3,1},{4,2},{5,3},{6,4},{7,5},{8,14},{9,15},{10,... | collective-permute-start | bytes 786440 | tf_op jit(solution)/shard_map/ppermute | solution.py:331
  58.5 13.0 %collective-permute-start.7 = (bf16[128,1024]{1,0:T(8,128)(2,1)S(1)}, bf16[128,1024]{1,0:T(8,128)(2,1)S(1)}, u32[]{:S(2)}, u32[]{:S(2)}) collective-permute-start(bf16[128,1024]{1,0:T(8,128)(2,1)S(1)} %attend.1.own_ref), channel_id=1, source_target_pairs={{0,1},{1,0},{2,3},{3,2},{4,5},{5,4},{6,7},{7,6},{8,9},{9,8},{10,11... | collective-permute-start | bytes 786440 | tf_op jit(solution)/shard_map/ppermute | solution.py:335
  64.6 6.9 %collective-permute-start.10 = (bf16[128,1024]{1,0:T(8,128)(2,1)S(1)}, bf16[128,1024]{1,0:T(8,128)(2,1)S(1)}, u32[]{:S(2)}, u32[]{:S(2)}) collective-permute-start(bf16[128,1024]{1,0:T(8,128)(2,1)S(1)} %collective-permute-done.9.refs_2_), channel_id=1, source_target_pairs={{0,1},{1,0},{2,3},{3,2},{4,5},{5,4},{6,7},{7,6},{8,9},{9,8},{10,11... | collective-permute-start | bytes 786440 | tf_op jit(solution)/shard_map/ppermute | solution.py:335
  70.6 1.9 %collective-permute-start.12 = (bf16[128,1024]{1,0:T(8,128)(2,1)S(1)}, bf16[128,1024]{1,0:T(8,128)(2,1)S(1)}, u32[]{:S(2)}, u32[]{:S(2)}) collective-permute-start(bf16[128,1024]{1,0:T(8,128)(2,1)S(1)} %collective-permute-done.8.refs_1_), channel_id=1, source_target_pairs={{0,1},{1,0},{2,3},{3,2},{4,5},{5,4},{6,7},{7,6},{8,9},{9,8},{10,11... | collective-permute-start | bytes 786440 | tf_op jit(solution)/shard_map/ppermute | solution.py:335
  71.4 1.6 %collective-permute-start.13 = (bf16[128,1024]{1,0:T(8,128)(2,1)S(1)}, bf16[128,1024]{1,0:T(8,128)(2,1)S(1)}, u32[]{:S(2)}, u32[]{:S(2)}) collective-permute-start(bf16[128,1024]{1,0:T(8,128)(2,1)S(1)} %hand_on.3), channel_id=1, source_target_pairs={{0,1},{1,0},{2,3},{3,2},{4,5},{5,4},{6,7},{7,6},{8,9},{9,8},{10,11... | collective-permute-start | bytes 786440 | tf_op jit(solution)/shard_map/ppermute | solution.py:335
  71.5 13.2 %copy-start = (bf16[1024,512]{1,0:T(8,128)(2,1)S(1)}, bf16[1024,512]{1,0:T(8,128)(2,1)}, u32[]{:S(2)}) copy-start(bf16[1024,512]{1,0:T(8,128)(2,1)} %rows_ref.1) | copy-start | bytes 3145732

commit v8 on v7

--- a/solution.py
+++ b/solution.py
@@ -161,14 +161,14 @@
     return total
 
 
-def square_kernel(*refs):
-    refs[-1][...] = square_sum(refs[:-1])
-
-
-def project_in_kernel(squares_ref, gain_in, query_weight_ref, keys_ref, values_ref, *refs):
-    blocks, (query_ref, pair_ref, gain_ref) = refs[:NMP], refs[NMP:]
+def square_kernel(gain_in, *refs):
+    spread(gain_in, refs[-1])
+    refs[-2][...] = square_sum(refs[:-2])
+
+
+def project_in_kernel(squares_ref, gain_ref, query_weight_ref, keys_ref, values_ref, *refs):
+    blocks, (query_ref, pair_ref) = refs[:NMP], refs[NMP:]
     parts = FEAT // 128
-    spread(gain_in, gain_ref)
     squares = squares_ref[...] + square_sum([blocks[k] for k in (1, 3, 5, 7)])
     inverse = lax.rsqrt(jnp.sum(squares, axis=1, keepdims=True) / WIDTH + 1e-05)
     query = jnp.zeros((OWNED, GROUP * HEAD), F32)
@@ -426,14 +426,14 @@
     blocks[1] = other_core(tokens)
     add_cores(blocks, loaded)
     blocks = [blocks[k] for k in range(NMP)]
-    squares = pl.pallas_call(
+    squares, gain = pl.pallas_call(
         square_kernel,
-        out_shape=pltpu.VMEM((OWNED, 128), F32),
-        in_specs=[VMEM] * 4,
-        out_specs=VMEM,
+        out_shape=(pltpu.VMEM((OWNED, 128), F32), pltpu.VMEM((NMP, FEAT // 128, 128), F32)),
+        in_specs=[VMEM] * 5,
+        out_specs=(VMEM, VMEM),
         compiler_params=params(4),
         name="square",
-    )(*(blocks[k] for k in (0, 2, 4, 6)))
+    )(prelayer_gain_vector.reshape(WIDTH // 128, 128), *(blocks[k] for k in (0, 2, 4, 6)))
     query, pair = pl.pallas_call(
         project_in_kernel,
         out_shape=(
@@ -442,13 +442,12 @@
         ),
         in_specs=[VMEM] * (5 + NMP),
         out_specs=[VMEM] * 2,
-        scratch_shapes=[pltpu.VMEM((NMP, FEAT // 128, 128), F32)],
         compiler_params=params(16),
         cost_estimate=cost(2 * OWNED * WIDTH * 10 * HEAD, 4 * MIB),
         name="project_in",
     )(
         squares,
-        prelayer_gain_vector.reshape(WIDTH // 128, 128),
+        gain,
         asker,
         lookup,
         content,

time: 86.2 us -> 86.1 us (level)
  no operation moved by 1% of the time
where the time goes in v8:
time: 86.1 us; the launch traced here: 85.9 us
  blocking collectives  45.4 us (53%)
  starting transfers between devices  19.2 us (22%)
  Pallas kernels  16.7 us (19%)
  waiting for transfers between devices  4.35 us (5%)
    all_to_all x1, blocking collectives, on_device(): pairs = lax.all_to_all(pair, 'seq', split_axis=0, concat_axis=0, tiled=True)  19.2 us
    all_to_all x1, blocking collectives, on_device(): lax.all_to_all(outgoing, 'seq', split_axis=0, concat_axis=0, tiled=True)  14.9 us
    all_to_all x1, blocking collectives, on_device(): lax.all_to_all(outgoing_back, 'seq', split_axis=0, concat_axis=0, tiled=T...  11.2 us
    ppermute x8, starting transfers between devices, other_core(): return lax.ppermute(array, 'mp', [(m, m ^ 1) for m in range(NMP)])  10 us
    ppermute x6, starting transfers between devices, z_step(): return lax.ppermute(array, 'mp', pairs)  9.19 us
    pallas_call x1, Pallas kernels, on_device(): pl.pallas_call(load_in_kernel, out_shape=(pltpu.VMEM((WIDTH, HEAD), BF16)...  4.11 us
    pallas_call x1, Pallas kernels, on_device(): pl.pallas_call(load_out_kernel, out_shape=(pltpu.VMEM((NMP * GROUP * HEAD...  3.98 us
    ppermute x6, waiting for transfers between devices, z_step(): return lax.ppermute(array, 'mp', pairs)  2.61 us
  transfers between devices with their start and end apart: 14, of which 6 were waited for; matrix products, arithmetic and copies ran while one was open for 0% of the time, Pallas kernels for 11%

profile of v8, /device:TPU:1, one launch (start us, length us, event | category | flops | bytes accessed | tf_op | source)
XLA Modules:
  0.0 85.9 jit_solution(955411493224938133)
XLA Ops:
  0.0 1.7 %pick.1 = (bf16[16,2,8,512]{3,2,1,0:T(8,128)(2,1)S(1)}, s32[3,16]{1,0:T(4,128)S(4)}, f32[8]{0:T(128)S(4)}) custom-call(s32[16,16]{1,0:T(8,128)} %tally_ref.1, s32[1,256]{1,0:T(1,128)} %select_ref.1, bf16[1024,512]{1,0:T(8,128)(2,1)} %rows_ref.1, f32[8]{0:T(128)} %sharp_hbm.1), custom_call_target="tpu_custom_call" | custom-call | tf_op jit(solution)/shard_map/pick/pallas_call | solution.py:378
  1.7 14.9 %all_to_all.15.in_ref = bf16[16,2,8,512]{3,2,1,0:T(8,128)(2,1)S(1)} all-to-all(bf16[16,2,8,512]{3,2,1,0:T(8,128)(2,1)S(1)} %get-tuple-element.22), channel_id=1, replica_groups=mesh['seq'=16,'mp'=8] {'seq'}, dimensions={0} | all-to-all | bytes 524288 | tf_op jit(solution)/shard_map/all_to_all | solution.py:402
  16.7 3.7 %collective-permute-start.1 = (bf16[128,512]{1,0:T(8,128)(2,1)S(1)}, bf16[128,512]{1,0:T(8,128)(2,1)S(1)}, u32[]{:S(2)}, u32[]{:S(2)}) collective-permute-start(bf16[128,512]{1,0:T(8,128)(2,1)S(1)} %compact.1.refs_0_.after_ref), channel_id=1, source_target_pairs={{0,4},{1,5},{2,6},{3,7},{4,0},{5,1},{6,2},{7,3},{8,12},{9,13},{10,... | collective-permute-start | bytes 393224 | tf_op jit(solution)/shard_map/ppermute | solution.py:331
  20.4 0.7 collective-permute-start
  21.1 1.9 %collective-permute-start.2 = (bf16[128,512]{1,0:T(8,128)(2,1)S(1)}, bf16[128,512]{1,0:T(8,128)(2,1)S(1)}, u32[]{:S(2)}, u32[]{:S(2)}) collective-permute-start(bf16[128,512]{1,0:T(8,128)(2,1)S(1)} %compact.1.refs_0_.after_ref), channel_id=1, source_target_pairs={{0,6},{1,7},{2,0},{3,1},{4,2},{5,3},{6,4},{7,5},{8,14},{9,15},{10,... | collective-permute-start | bytes 393224 | tf_op jit(solution)/shard_map/ppermute | solution.py:331
  23.0 2.9 %collective-permute-start.3 = (bf16[128,512]{1,0:T(8,128)(2,1)S(1)}, bf16[128,512]{1,0:T(8,128)(2,1)S(1)}, u32[]{:S(2)}, u32[]{:S(2)}) collective-permute-start(bf16[128,512]{1,0:T(8,128)(2,1)S(1)} %compact.1.refs_0_.after_ref), channel_id=1, source_target_pairs={{0,1},{1,0},{2,3},{3,2},{4,5},{5,4},{6,7},{7,6},{8,9},{9,8},{10,11... | collective-permute-start | bytes 393224 | tf_op jit(solution)/shard_map/ppermute | solution.py:335
  26.0 4.1 %load_in.1 = (bf16[4096,128]{1,0:T(8,128)(2,1)S(1)}, bf16[4096,128]{1,0:T(8,128)(2,1)S(1)}, bf16[4096,1024]{1,0:T(8,128)(2,1)S(1)}, f32[8,128]{1,0:T(8,128)S(1)}) custom-call(bf16[4096,128]{1,0:T(8,128)(2,1)} %keys_hbm.1, bf16[4096,128]{1,0:T(8,128)(2,1)} %values_hbm.1, bf16[4096,1024]{1,0:T(8,128)(2,1)} %query_hbm.1, ...), custom_call_target="tpu_custom_call" | custom-call | tf_op jit(solution)/shard_map/load_in/pallas_call | solution.py:411
  30.1 0.0 copy-start.1
  30.1 0.0 copy-start.3
  30.1 0.0 copy-start.4
  30.1 0.0 collective-permute-done.1.refs_2_.refs_4_
  30.2 0.1 collective-permute-start.5
  30.2 0.0 collective-permute-done.refs_1_.refs_2_
  30.3 0.5 collective-permute-start.4
  30.7 0.0 collective-permute-done.2.refs_3_.in_ref.refs_6_
  30.8 0.2 collective-permute-start.6
  30.9 0.0 copy-done.2
  30.9 0.1 square.1
  31.1 0.0 collective-permute-done.3.refs_1_
  31.1 0.5 collective-permute-done.5.refs_5_
  31.6 0.2 collective-permute-done.4.refs_3_
  31.8 0.4 collective-permute-done.6.refs_7_
  32.2 2.0 %project_in.1 = (bf16[128,1024]{1,0:T(8,128)(2,1)S(1)}, bf16[16,128,256]{2,1,0:T(8,128)(2,1)S(1)}) custom-call(f32[128,128]{1,0:T(8,128)S(1)} %get-tuple-element.23.squares_ref, f32[8,4,128]{2,1,0:T(4,128)S(1)} %get-tuple-element.24.gain_ref, bf16[4096,1024]{1,0:T(8,128)(2,1)S(1)} %get-tuple-element.25.query_weight_ref, ...), custom_call_target="tpu_custom_call" | custom-call | flops 1342177280 | bytes 4194304 | tf_op jit(solution)/shard_map/project_in/pallas_call | solution.py:437
  34.2 19.2 %all_to_all.16.pair_ref = bf16[16,128,256]{2,1,0:T(8,128)(2,1)S(1)} all-to-all(bf16[16,128,256]{2,1,0:T(8,128)(2,1)S(1)} %get-tuple-element.30), channel_id=1, replica_groups=mesh['seq'=16,'mp'=8] {'seq'}, dimensions={0} | all-to-all | bytes 2097152 | tf_op jit(solution)/shard_map/all_to_all | solution.py:456
  53.4 2.1 %attend.1.own_ref = bf16[128,1024]{1,0:T(8,128)(2,1)S(1)} custom-call(f32[8]{0:T(128)S(4)} %get-tuple-element.21.sharp_ref, bf16[128,1024]{1,0:T(8,128)(2,1)S(1)} %get-tuple-element.29.query_ref, bf16[16,128,256]{2,1,0:T(8,128)(2,1)S(1)} %all_to_all.16.pair_ref), custom_call_target="tpu_custom_call" | custom-call | tf_op jit(solution)/shard_map/attend/pallas_call | solution.py:458
  55.5 0.1 collective-permute-start.9
  55.6 1.2 %collective-permute-start.8 = (bf16[128,1024]{1,0:T(8,128)(2,1)S(1)}, bf16[128,1024]{1,0:T(8,128)(2,1)S(1)}, u32[]{:S(2)}, u32[]{:S(2)}) collective-permute-start(bf16[128,1024]{1,0:T(8,128)(2,1)S(1)} %attend.1.own_ref), channel_id=1, source_target_pairs={{0,2},{1,3},{2,4},{3,5},{4,6},{5,7},{6,0},{7,1},{8,10},{9,11},{10,... | collective-permute-start | bytes 786440 | tf_op jit(solution)/shard_map/ppermute | solution.py:331
  56.8 1.6 %collective-permute-start.11 = (bf16[128,1024]{1,0:T(8,128)(2,1)S(1)}, bf16[128,1024]{1,0:T(8,128)(2,1)S(1)}, u32[]{:S(2)}, u32[]{:S(2)}) collective-permute-start(bf16[128,1024]{1,0:T(8,128)(2,1)S(1)} %attend.1.own_ref), channel_id=1, source_target_pairs={{0,6},{1,7},{2,0},{3,1},{4,2},{5,3},{6,4},{7,5},{8,14},{9,15},{10,... | collective-permute-start | bytes 786440 | tf_op jit(solution)/shard_map/ppermute | solution.py:331
  58.4 2.1 %collective-permute-start.7 = (bf16[128,1024]{1,0:T(8,128)(2,1)S(1)}, bf16[128,1024]{1,0:T(8,128)(2,1)S(1)}, u32[]{:S(2)}, u32[]{:S(2)}) collective-permute-start(bf16[128,1024]{1,0:T(8,128)(2,1)S(1)} %attend.1.own_ref), channel_id=1, source_target_pairs={{0,1},{1,0},{2,3},{3,2},{4,5},{5,4},{6,7},{7,6},{8,9},{9,8},{10,11... | collective-permute-start | bytes 786440 | tf_op jit(solution)/shard_map/ppermute | solution.py:335
  60.5 0.0 copy-done.1
  60.5 0.0 copy-done.3
  60.5 4.0 %load_out.1 = (bf16[8192,512]{1,0:T(8,128)(2,1)S(1)}, f32[128,512]{1,0:T(8,128)S(1)}, f32[128,128]{1,0:T(8,128)S(1)}, bf16[1024,256]{1,0:T(8,128)(2,1)S(1)}) custom-call(bf16[8192,512]{1,0:T(8,128)(2,1)} %weight_hbm.1, s32[16,16]{1,0:T(8,128)S(1)} %copy-done.1, s32[1,256]{1,0:T(1,128)S(1)} %copy-done.4, bf16[32,128]{1,0:T(8,128)(2,1)S(1)} %bitcast.3, ...), custom_call_target="tpu_custom_call" | custom-call | tf_op jit(solution)/shard_map/load_out/pallas_call | solution.py:466
  64.5 0.0 collective-permute-done.9.refs_2_
  64.5 3.4 %collective-permute-start.10 = (bf16[128,1024]{1,0:T(8,128)(2,1)S(1)}, bf16[128,1024]{1,0:T(8,128)(2,1)S(1)}, u32[]{:S(2)}, u32[]{:S(2)}) collective-permute-start(bf16[128,1024]{1,0:T(8,128)(2,1)S(1)} %collective-permute-done.9.refs_2_), channel_id=1, source_target_pairs={{0,1},{1,0},{2,3},{3,2},{4,5},{5,4},{6,7},{7,6},{8,9},{9,8},{10,11... | collective-permute-start | bytes 786440 | tf_op jit(solution)/shard_map/ppermute | solution.py:335
  67.9 2.6 %collective-permute-done.8.refs_1_ = bf16[128,1024]{1,0:T(8,128)(2,1)S(1)} collective-permute-done((bf16[128,1024]{1,0:T(8,128)(2,1)S(1)}, bf16[128,1024]{1,0:T(8,128)(2,1)S(1)}, u32[]{:S(2)}, u32[]{:S(2)}) %collective-permute-start.8) | collective-permute-done | bytes 262176 | tf_op jit(solution)/shard_map/ppermute | solution.py:331
  70.5 0.7 collective-permute-start.12
  71.2 0.0 collective-permute-done.11.refs_4_.in_ref
  71.3 0.1 collective-permute-start.13
  71.4 0.0 collective-permute-done.7.refs_0_
  71.4 0.0 collective-permute-done.10.refs_3_
  71.4 0.0 copy-start
  71.4 0.9 %project_middle.1.total_ref = f32[128,512]{1,0:T(8,128)S(1)} custom-call(f32[128,512]{1,0:T(8,128)S(1)} %get-tuple-element.33.total_in.token_ref, bf16[8192,512]{1,0:T(8,128)(2,1)S(1)} %get-tuple-element.34.weight_ref, bf16[128,1024]{1,0:T(8,128)(2,1)S(1)} %collective-permute-done.7.refs_0_, bf16[128,1024]{1,0:T(8,128)(2,1)S(1)} %collective-permute-done.8.refs_1_, ...), custom_call_target="tpu_custom_call" | custom-call | tf_op jit(solution)/shard_map/project_middle/pallas_call | solution.py:490
  72.3 0.1 collective-permute-done.12.refs_0_
  72.4 0.5 collective-permute-done.13.refs_1_
  72.9 0.5 project_last.1
  73.4 11.2 %all_to_all.17.back_ref = bf16[16,2,8,512]{3,2,1,0:T(8,128)(2,1)S(1)} all-to-all(bf16[16,2,8,512]{3,2,1,0:T(8,128)(2,1)S(1)} %project_last.1), channel_id=1, replica_groups=mesh['seq'=16,'mp'=8] {'seq'}, dimensions={0} | all-to-all | bytes 524288 | tf_op jit(solution)/shard_map/all_to_all | solution.py:507
  84.6 0.0 copy-done
  84.6 1.3 %blend.1 = bf16[1024,512]{1,0:T(8,128)(2,1)} custom-call(s32[3,16]{1,0:T(4,128)S(4)} %get-tuple-element.20.table_ref, bf16[1024,256]{1,0:T(8,128)(2,1)S(1)} %get-tuple-element.31.hot_ref, bf16[1024,512]{1,0:T(8,128)(2,1)S(1)} %copy-done, bf16[16,2,8,512]{3,2,1,0:T(8,128)(2,1)S(1)} %all_to_all.17.back_ref), custom_call_target="tpu_custom_call" | custom-call | tf_op jit(solution)/shard_map/blend/pallas_call | solution.py:508
  (5 shorter events, 0.1 us)
Async XLA Ops:
  0.0 30.9 %copy-start.2 = (bf16[4096]{0:T(1024)(128)(2,1)S(1)}, bf16[4096]{0:T(1024)(128)(2,1)}, u32[]{:S(2)}) copy-start(bf16[4096]{0:T(1024)(128)(2,1)} %param.11) | copy-start | bytes 24580
  16.7 13.5 %collective-permute-start.1 = (bf16[128,512]{1,0:T(8,128)(2,1)S(1)}, bf16[128,512]{1,0:T(8,128)(2,1)S(1)}, u32[]{:S(2)}, u32[]{:S(2)}) collective-permute-start(bf16[128,512]{1,0:T(8,128)(2,1)S(1)} %compact.1.refs_0_.after_ref), channel_id=1, source_target_pairs={{0,4},{1,5},{2,6},{3,7},{4,0},{5,1},{6,2},{7,3},{8,12},{9,13},{10,... | collective-permute-start | bytes 393224 | tf_op jit(solution)/shard_map/ppermute | solution.py:331
  20.4 9.9 %collective-permute-start = (bf16[128,512]{1,0:T(8,128)(2,1)S(1)}, bf16[128,512]{1,0:T(8,128)(2,1)S(1)}, u32[]{:S(2)}, u32[]{:S(2)}) collective-permute-start(bf16[128,512]{1,0:T(8,128)(2,1)S(1)} %compact.1.refs_0_.after_ref), channel_id=1, source_target_pairs={{0,2},{1,3},{2,4},{3,5},{4,6},{5,7},{6,0},{7,1},{8,10},{9,11},{10,... | collective-permute-start | bytes 393224 | tf_op jit(solution)/shard_map/ppermute | solution.py:331
  21.1 9.6 %collective-permute-start.2 = (bf16[128,512]{1,0:T(8,128)(2,1)S(1)}, bf16[128,512]{1,0:T(8,128)(2,1)S(1)}, u32[]{:S(2)}, u32[]{:S(2)}) collective-permute-start(bf16[128,512]{1,0:T(8,128)(2,1)S(1)} %compact.1.refs_0_.after_ref), channel_id=1, source_target_pairs={{0,6},{1,7},{2,0},{3,1},{4,2},{5,3},{6,4},{7,5},{8,14},{9,15},{10,... | collective-permute-start | bytes 393224 | tf_op jit(solution)/shard_map/ppermute | solution.py:331
  23.0 8.0 %collective-permute-start.3 = (bf16[128,512]{1,0:T(8,128)(2,1)S(1)}, bf16[128,512]{1,0:T(8,128)(2,1)S(1)}, u32[]{:S(2)}, u32[]{:S(2)}) collective-permute-start(bf16[128,512]{1,0:T(8,128)(2,1)S(1)} %compact.1.refs_0_.after_ref), channel_id=1, source_target_pairs={{0,1},{1,0},{2,3},{3,2},{4,5},{5,4},{6,7},{7,6},{8,9},{9,8},{10,11... | collective-permute-start | bytes 393224 | tf_op jit(solution)/shard_map/ppermute | solution.py:335
  30.1 30.4 %copy-start.1 = (s32[16,16]{1,0:T(8,128)S(1)}, s32[16,16]{1,0:T(8,128)}, u32[]{:S(2)}) copy-start(s32[16,16]{1,0:T(8,128)} %tally_ref.1) | copy-start | bytes 3076
  30.1 30.4 %copy-start.3 = (bf16[4096]{0:T(1024)(128)(2,1)S(1)}, bf16[4096]{0:T(1024)(128)(2,1)}, u32[]{:S(2)}) copy-start(bf16[4096]{0:T(1024)(128)(2,1)} %param.12) | copy-start | bytes 24580
  30.1 30.4 %copy-start.4 = (s32[1,256]{1,0:T(1,128)S(1)}, s32[1,256]{1,0:T(1,128)}, u32[]{:S(2)}) copy-start(s32[1,256]{1,0:T(1,128)} %select_ref.1) | copy-start | bytes 3076
  30.2 1.4 %collective-permute-start.5 = (bf16[128,512]{1,0:T(8,128)(2,1)S(1)}, bf16[128,512]{1,0:T(8,128)(2,1)S(1)}, u32[]{:S(2)}, u32[]{:S(2)}) collective-permute-start(bf16[128,512]{1,0:T(8,128)(2,1)S(1)} %collective-permute-done.1.refs_2_.refs_4_), channel_id=1, source_target_pairs={{0,1},{1,0},{2,3},{3,2},{4,5},{5,4},{6,7},{7,6},{8,9},{9,8},{10,11... | collective-permute-start | bytes 393224 | tf_op jit(solution)/shard_map/ppermute | solution.py:335
  30.3 1.5 %collective-permute-start.4 = (bf16[128,512]{1,0:T(8,128)(2,1)S(1)}, bf16[128,512]{1,0:T(8,128)(2,1)S(1)}, u32[]{:S(2)}, u32[]{:S(2)}) collective-permute-start(bf16[128,512]{1,0:T(8,128)(2,1)S(1)} %collective-permute-done.refs_1_.refs_2_), channel_id=1, source_target_pairs={{0,1},{1,0},{2,3},{3,2},{4,5},{5,4},{6,7},{7,6},{8,9},{9,8},{10,11... | collective-permute-start | bytes 393224 | tf_op jit(solution)/shard_map/ppermute | solution.py:335
  30.8 1.4 %collective-permute-start.6 = (bf16[128,512]{1,0:T(8,128)(2,1)S(1)}, bf16[128,512]{1,0:T(8,128)(2,1)S(1)}, u32[]{:S(2)}, u32[]{:S(2)}) collective-permute-start(bf16[128,512]{1,0:T(8,128)(2,1)S(1)} %hand_on.2), channel_id=1, source_target_pairs={{0,1},{1,0},{2,3},{3,2},{4,5},{5,4},{6,7},{7,6},{8,9},{9,8},{10,11... | collective-permute-start | bytes 393224 | tf_op jit(solution)/shard_map/ppermute | solution.py:335
  55.5 9.0 %collective-permute-start.9 = (bf16[128,1024]{1,0:T(8,128)(2,1)S(1)}, bf16[128,1024]{1,0:T(8,128)(2,1)S(1)}, u32[]{:S(2)}, u32[]{:S(2)}) collective-permute-start(bf16[128,1024]{1,0:T(8,128)(2,1)S(1)} %attend.1.own_ref), channel_id=1, source_target_pairs={{0,4},{1,5},{2,6},{3,7},{4,0},{5,1},{6,2},{7,3},{8,12},{9,13},{10,... | collective-permute-start | bytes 786440 | tf_op jit(solution)/shard_map/ppermute | solution.py:331
  55.6 14.9 %collective-permute-start.8 = (bf16[128,1024]{1,0:T(8,128)(2,1)S(1)}, bf16[128,1024]{1,0:T(8,128)(2,1)S(1)}, u32[]{:S(2)}, u32[]{:S(2)}) collective-permute-start(bf16[128,1024]{1,0:T(8,128)(2,1)S(1)} %attend.1.own_ref), channel_id=1, source_target_pairs={{0,2},{1,3},{2,4},{3,5},{4,6},{5,7},{6,0},{7,1},{8,10},{9,11},{10,... | collective-permute-start | bytes 786440 | tf_op jit(solution)/shard_map/ppermute | solution.py:331
  56.8 14.5 %collective-permute-start.11 = (bf16[128,1024]{1,0:T(8,128)(2,1)S(1)}, bf16[128,1024]{1,0:T(8,128)(2,1)S(1)}, u32[]{:S(2)}, u32[]{:S(2)}) collective-permute-start(bf16[128,1024]{1,0:T(8,128)(2,1)S(1)} %attend.1.own_ref), channel_id=1, source_target_pairs={{0,6},{1,7},{2,0},{3,1},{4,2},{5,3},{6,4},{7,5},{8,14},{9,15},{10,... | collective-permute-start | bytes 786440 | tf_op jit(solution)/shard_map/ppermute | solution.py:331
  58.4 13.0 %collective-permute-start.7 = (bf16[128,1024]{1,0:T(8,128)(2,1)S(1)}, bf16[128,1024]{1,0:T(8,128)(2,1)S(1)}, u32[]{:S(2)}, u32[]{:S(2)}) collective-permute-start(bf16[128,1024]{1,0:T(8,128)(2,1)S(1)} %attend.1.own_ref), channel_id=1, source_target_pairs={{0,1},{1,0},{2,3},{3,2},{4,5},{5,4},{6,7},{7,6},{8,9},{9,8},{10,11... | collective-permute-start | bytes 786440 | tf_op jit(solution)/shard_map/ppermute | solution.py:335
  64.5 6.9 %collective-permute-start.10 = (bf16[128,1024]{1,0:T(8,128)(2,1)S(1)}, bf16[128,1024]{1,0:T(8,128)(2,1)S(1)}, u32[]{:S(2)}, u32[]{:S(2)}) collective-permute-start(bf16[128,1024]{1,0:T(8,128)(2,1)S(1)} %collective-permute-done.9.refs_2_), channel_id=1, source_target_pairs={{0,1},{1,0},{2,3},{3,2},{4,5},{5,4},{6,7},{7,6},{8,9},{9,8},{10,11... | collective-permute-start | bytes 786440 | tf_op jit(solution)/shard_map/ppermute | solution.py:335
  70.5 1.9 %collective-permute-start.12 = (bf16[128,1024]{1,0:T(8,128)(2,1)S(1)}, bf16[128,1024]{1,0:T(8,128)(2,1)S(1)}, u32[]{:S(2)}, u32[]{:S(2)}) collective-permute-start(bf16[128,1024]{1,0:T(8,128)(2,1)S(1)} %collective-permute-done.8.refs_1_), channel_id=1, source_target_pairs={{0,1},{1,0},{2,3},{3,2},{4,5},{5,4},{6,7},{7,6},{8,9},{9,8},{10,11... | collective-permute-start | bytes 786440 | tf_op jit(solution)/shard_map/ppermute | solution.py:335
  71.3 1.6 %collective-permute-start.13 = (bf16[128,1024]{1,0:T(8,128)(2,1)S(1)}, bf16[128,1024]{1,0:T(8,128)(2,1)S(1)}, u32[]{:S(2)}, u32[]{:S(2)}) collective-permute-start(bf16[128,1024]{1,0:T(8,128)(2,1)S(1)} %hand_on.3), channel_id=1, source_target_pairs={{0,1},{1,0},{2,3},{3,2},{4,5},{5,4},{6,7},{7,6},{8,9},{9,8},{10,11... | collective-permute-start | bytes 786440 | tf_op jit(solution)/shard_map/ppermute | solution.py:335
  71.4 13.2 %copy-start = (bf16[1024,512]{1,0:T(8,128)(2,1)S(1)}, bf16[1024,512]{1,0:T(8,128)(2,1)}, u32[]{:S(2)}) copy-start(bf16[1024,512]{1,0:T(8,128)(2,1)} %rows_ref.1) | copy-start | bytes 3145732
